TPU v7x, 32 devices: a whole 2x2x4 slice. The times are simulated.
32 devices in a mesh: dp: 4 (over z), seq: 8 (over y, x, core).
Axes of the slice: x: 2, y: 2, z: 4, core: 2. Of those that a mesh axis runs over, the one named last changes fastest.
Arguments:
- tokens: bfloat16 [64, 4, 2560], P('dp'), may hold values from -6 to 6
- attn_gain: float32 [2560], replicated, may hold values from 0.1 to 1.9
- qkv_weight: bfloat16 [3072, 2560], P(('seq', 'dp'))
- out_weight: bfloat16 [2560, 2560], P(('seq', 'dp')), may hold values from -0.125 to 0.125
- mlp_gain: float32 [2560], replicated, may hold values from 0.1 to 1.9
- gate_up: bfloat16 [2, 7680, 2560], P(None, 'seq'), may hold values from -0.125 to 0.125
- down_weight: bfloat16 [7680, 2560], P('seq'), may hold values from -0.0625 to 0.0625
- kv_pool: bfloat16 [2048, 128, 512], P(('dp', 'seq')), may hold values from -6 to 6
- cache_len: int32 [64], P('dp'), may hold values from 1 to 16384, as said below
- page_table: int32 [64, 16], P('dp'), may hold values from 0 to 511, as said below
Outputs:
- layer_out: bfloat16 [64, 4, 2560], P('dp')
- written_pool: bfloat16 [2048, 128, 512], P(('dp', 'seq'))
Inputs may be any that keep to these rules, and one draw needn't show every extreme that they name: `cache_len`: some request of the whole batch has exactly 16384 cached tokens; lengths under 2048 occur. `page_table`: within the 16 requests of one dp index all entries differ. Slot s lies on seq index s // 64; in every dp index some seq index holds exactly 64 of its pages.
All inputs are finite; a program needn't handle non-finite values.
Results may differ from a plain program's by a relative error of at most 0.018.
Values may be sent and summed in bfloat16 or wider, within the bound.
No kernel may reach another device: no remote copies, remote signals or barrier semaphores. Data moves between devices by JAX's collectives and lax.ppermute only.
A program may use at most 128 MiB of HBM per device.

v0:
```python
import jax
import jax.numpy as jnp
from jax import lax
from jax.sharding import PartitionSpec as P

low_fill = -1e30


def rms_norm(values, gains):
    floats = values.astype(jnp.float32)
    return floats * lax.rsqrt(jnp.mean(floats * floats, axis=-1, keepdims=True) + 1e-06) * gains


def rotate(values, positions):
    quarter = values.shape[-1] // 4
    freq_index = jnp.arange(quarter).astype(jnp.float32)
    inverse = 10000.0 ** (-freq_index / quarter)
    angles = positions[..., None] * inverse
    first = values[..., :quarter]
    second = values[..., quarter : 2 * quarter]
    others = values[..., 2 * quarter :]
    cosine = jnp.cos(angles)
    sine = jnp.sin(angles)
    return jnp.concatenate(
        [first * cosine - second * sine, second * cosine + first * sine, others], axis=-1
    )


def body(
    tokens,
    attn_gain,
    qkv_weight,
    out_weight,
    mlp_gain,
    gate_up,
    down_weight,
    kv_pool,
    cache_len,
    page_table,
):
    seq_index = lax.axis_index("seq")
    requests, new_count, model_width = tokens.shape
    slot_count, page_len, pair_width = kv_pool.shape
    head_dim = pair_width // 2
    head_count = out_weight.shape[1] // head_dim
    page_count = page_table.shape[1]
    window = page_count * page_len
    row_count = requests * new_count
    query_rows = new_count * head_count
    split_q = head_count * head_dim
    scale = head_dim ** (-0.5)
    contract = (((1,), (1,)), ((), ()))
    qkv_local, out_local = (
        lax.all_gather(qkv_weight, "dp", axis=0, tiled=True),
        lax.all_gather(out_weight, "dp", axis=0, tiled=True),
    )
    normed = rms_norm(tokens, attn_gain).astype(jnp.bfloat16).reshape(row_count, model_width)
    local_part = lax.dot_general(
        normed, qkv_local, contract, preferred_element_type=jnp.float32
    ).astype(jnp.bfloat16)
    projected = lax.all_gather(local_part, "seq", axis=1, tiled=True).reshape(
        requests, new_count, -1
    )
    positions_int = cache_len[:, None] + jnp.arange(new_count, dtype=jnp.int32)[None, :]
    positions = positions_int.astype(jnp.float32)
    queries = rotate(
        projected[:, :, :split_q]
        .astype(jnp.float32)
        .reshape(requests, new_count, head_count, head_dim),
        positions[:, :, None],
    ).astype(jnp.bfloat16)
    keys_new = rotate(
        projected[:, :, split_q : split_q + head_dim].astype(jnp.float32), positions
    ).astype(jnp.bfloat16)
    values_new = projected[:, :, split_q + head_dim :]
    slot_ids = seq_index * slot_count + jnp.arange(slot_count, dtype=jnp.int32)
    matches = page_table[None, :, :] == slot_ids[:, None, None]
    owners = jnp.any(matches, axis=2)
    in_use = jnp.any(owners, axis=1)
    page_of = jnp.sum(
        jnp.where(matches, jnp.arange(page_count, dtype=jnp.int32)[None, None, :], 0), axis=(1, 2)
    )
    slot_length = jnp.sum(jnp.where(owners, cache_len[None, :], 0), axis=1)
    query_flat = queries.reshape(requests, query_rows * head_dim)
    slot_queries = jnp.dot(
        owners.astype(jnp.bfloat16), query_flat, preferred_element_type=jnp.float32
    )
    slot_queries = slot_queries.astype(jnp.bfloat16).reshape(slot_count, query_rows, head_dim)
    scores = (
        jnp.einsum(
            "pqd,pkd->pqk",
            slot_queries,
            kv_pool[:, :, :head_dim],
            preferred_element_type=jnp.float32,
        )
        * scale
    )
    cycle = page_of[:, None] * page_len + jnp.arange(page_len, dtype=jnp.int32)[None, :]
    key_pos = slot_length[:, None] - 1 - jnp.mod(slot_length[:, None] - 1 - cycle, window)
    query_pos = (
        slot_length[:, None] + (jnp.arange(query_rows, dtype=jnp.int32) // head_count)[None, :]
    )
    visible = (
        in_use[:, None, None]
        & (key_pos >= 0)[:, None, :]
        & (key_pos[:, None, :] > query_pos[:, :, None] - window)
    )
    slot_peak = jnp.max(jnp.where(visible, scores, low_fill), axis=2)
    weights = jnp.where(visible, jnp.exp(scores - slot_peak[:, :, None]), 0.0)
    slot_sum = jnp.sum(weights, axis=2)
    slot_out = jnp.einsum(
        "pqk,pkd->pqd",
        weights.astype(jnp.bfloat16),
        kv_pool[:, :, head_dim:],
        preferred_element_type=jnp.float32,
    )
    request_peak = jnp.max(jnp.where(owners[:, :, None], slot_peak[:, None, :], low_fill), axis=0)
    owner_peak = jnp.max(jnp.where(owners[:, :, None], request_peak[None, :, :], low_fill), axis=1)
    factor = jnp.exp(slot_peak - owner_peak)
    request_sum = jnp.sum(
        jnp.where(owners[:, :, None], (slot_sum * factor)[:, None, :], 0.0), axis=0
    )
    request_out = jnp.einsum(
        "pr,pqd->rqd",
        owners.astype(jnp.float32),
        slot_out * factor[:, :, None],
        precision=lax.Precision.HIGHEST,
    )
    query_block = queries.reshape(requests, query_rows, head_dim)
    new_scores = (
        jnp.einsum("rqd,rud->rqu", query_block, keys_new, preferred_element_type=jnp.float32)
        * scale
    )
    causal = jnp.arange(new_count)[None, :] <= (jnp.arange(query_rows) // head_count)[:, None]
    new_peak = jnp.max(jnp.where(causal[None], new_scores, low_fill), axis=2)
    global_peak = lax.pmax(request_peak, "seq")
    rescale = jnp.exp(request_peak - global_peak)
    old_denominator, weighted = (
        lax.psum((request_sum * rescale).astype(jnp.bfloat16), "seq").astype(jnp.float32),
        lax.psum((request_out * rescale[:, :, None]).astype(jnp.bfloat16), "seq").astype(
            jnp.float32
        ),
    )
    top_peak = jnp.maximum(global_peak, new_peak)
    new_weights = jnp.where(causal[None], jnp.exp(new_scores - top_peak[:, :, None]), 0.0)
    carried = jnp.exp(global_peak - top_peak)
    fresh_sum = jnp.sum(new_weights, axis=2)
    fresh_out = jnp.einsum(
        "rqu,rud->rqd",
        new_weights.astype(jnp.bfloat16),
        values_new,
        preferred_element_type=jnp.float32,
    )
    carried, fresh_sum, fresh_out = (carried, fresh_sum, fresh_out)
    denominator = old_denominator * carried + fresh_sum
    numerator = weighted * carried[:, :, None] + fresh_out
    attended = (
        (numerator / denominator[:, :, None]).astype(jnp.bfloat16).reshape(row_count, split_q)
    )
    heads_part = lax.dot_general(
        attended, out_local, contract, preferred_element_type=jnp.float32
    ).astype(jnp.bfloat16)
    heads_out = lax.all_gather(heads_part, "seq", axis=1, tiled=True)
    residual = (
        tokens.reshape(row_count, model_width).astype(jnp.float32) + heads_out.astype(jnp.float32)
    ).astype(jnp.bfloat16)
    hidden_in = rms_norm(residual, mlp_gain).astype(jnp.bfloat16)
    gate_and_up = jnp.einsum("rd,gfd->grf", hidden_in, gate_up, preferred_element_type=jnp.float32)
    hidden = (jax.nn.gelu(gate_and_up[0], approximate=True) * gate_and_up[1]).astype(jnp.bfloat16)
    partial_sum = jnp.dot(hidden, down_weight, preferred_element_type=jnp.float32)
    full_sum = lax.psum(partial_sum.astype(jnp.bfloat16), "seq").astype(jnp.float32)
    layer_out = (residual.astype(jnp.float32) + full_sum).astype(jnp.bfloat16)
    layer_out = layer_out.reshape(requests, new_count, model_width)
    page_index = jnp.mod(positions_int // page_len, page_count)
    slot_taken = jnp.take_along_axis(page_table, page_index, axis=1)
    local_slot = slot_taken - seq_index * slot_count
    local_slot = jnp.where((local_slot >= 0) & (local_slot < slot_count), local_slot, slot_count)
    offset = jnp.mod(positions_int, page_len)
    new_rows = jnp.concatenate([keys_new, values_new], axis=-1)
    written_pool = kv_pool.at[local_slot, offset].set(new_rows, mode="drop")
    return (layer_out, written_pool)


def solution(mesh):
    in_specs = (
        P("dp", None, None),
        P(),
        P(("seq", "dp"), None),
        P(("seq", "dp"), None),
        P(),
        P(None, "seq", None),
        P("seq", None),
        P(("dp", "seq"), None, None),
        P("dp"),
        P("dp", None),
    )
    out_specs = (P("dp", None, None), P(("dp", "seq"), None, None))
    return jax.shard_map(body, mesh=mesh, in_specs=in_specs, out_specs=out_specs, check_vma=False)
```

profile of v0, /device:TPU:0, one launch (start us, length us, event | category | flops | bytes accessed | tf_op | source)
XLA Modules:
  0.0 274.5 jit_solution(16844363583284267730)
XLA Ops:
  7.2 7.8 %copy.153 = bf16[64,128,512]{2,1,0:T(8,128)(2,1)} copy(bf16[64,128,512]{2,1,0:T(8,128)(2,1)} %param.17) | data formatting | bytes 16777216
  16.4 45.0 %all-gather.4.cloned.1.call-done = bf16[384,2560]{1,0:T(8,128)(2,1)} async-done(((bf16[96,2560]{1,0:T(8,128)(2,1)}), bf16[384,2560]{1,0:T(8,128)(2,1)}) %all-gather.4.cloned.1.call-update) | async-done | bytes 1966096 | tf_op jit(solution)/shard_map/all_gather | solution.py:54
  61.5 2.3 convolution_convert_fusion.3
  63.8 9.8 %all_gather.13 = bf16[64,3072]{1,0:T(8,128)(2,1)S(1)} all-gather(bf16[64,384]{1,0:T(8,128)(2,1)S(1)} %convolution_convert_fusion.3), channel_id=1, replica_groups=mesh['dp'=4,'seq'=8] {'seq'}, dimensions={1}, use_global_device_ids=true | all-gather | bytes 442368 | tf_op jit(solution)/shard_map/all_gather | solution.py:61
  75.2 0.5 convolution_convert_fusion
  76.0 3.5 %select_reduce_fusion = (f32[64,40]{1,0:T(8,128)S(1)}, f32[64,40,128]{2,1,0:T(8,128)S(1)}) fusion(s32[64,40]{1,0:T(8,128)S(1)} %add_add_fusion, s32[64,128]{1,0:T(8,128)S(1)} %fusion.59, pred[64,128]{1,0:T(8,128)(4,1)S(1)} %compare_and_fusion.1, bf16[64,40,256]{2,1,0:T(8,128)(2,1)S(1)} %bitcast.52, bf16[64,128,512]{2,1,0:T(8,128)(2,1)} %copy.153), kind=kOutput, calls=%fused_computation.13 | convolution fusion | flops 169408000 | bytes 6877184 | tf_op jit(solution)/shard_map/pqd,pkd->pqk/dot_general | solution.py:90
  79.9 13.5 %pmax.7 = f32[16,40]{1,0:T(8,128)S(1)} all-reduce(f32[16,40]{1,0:T(8,128)S(1)} %select_reduce_fusion.3), channel_id=1, replica_groups=mesh['dp'=4,'seq'=8] {'seq'}, use_global_device_ids=true, to_apply=%region_8.9 | all-reduce | flops 640 | bytes 5120 | tf_op jit(solution)/shard_map/pmax | solution.py:136
  93.6 1.3 fusion.19
  95.3 3.3 %fusion.6 = f32[64,40,256]{2,1,0:T(8,128)S(1)} fusion(bf16[64,128,512]{2,1,0:T(8,128)(2,1)} %copy.153, f32[64,40]{1,0:T(8,128)S(1)} %get-tuple-element.11, f32[64,40,128]{2,1,0:T(8,128)} %copy-done.1, f32[64,40]{1,0:T(8,128)S(1)} %get-tuple-element.19, s32[64,40]{1,0:T(8,128)S(1)} %add_add_fusion, s32[64,128]{1,0:T(8,128)S(1)} %fusion.59, ...), kind=kOutput, calls=%fused_computation.10 | convolution fusion | flops 170065920 | bytes 8198144 | tf_op jit(solution)/shard_map/pqk,pkd->pqd/dot_general | solution.py:111
  99.1 2.4 fusion.15
  101.5 0.7 all-gather.6.cloned.1.call-update
  102.5 0.8 gather_fusion
  103.4 11.9 %psum.22 = bf16[16,40]{1,0:T(8,128)(2,1)S(1)} all-reduce(bf16[16,40]{1,0:T(8,128)(2,1)S(1)} %get-tuple-element.8), channel_id=1, replica_groups=mesh['dp'=4,'seq'=8] {'seq'}, use_global_device_ids=true, to_apply=%region_13.14 | all-reduce | flops 640 | bytes 2560 | tf_op jit(solution)/shard_map/psum | solution.py:139
  115.8 37.7 %all-reduce.3.cloned.1.call-done = bf16[16,40,256]{2,0,1:T(8,128)(2,1)} async-done(((bf16[16,40,256]{2,0,1:T(8,128)(2,1)}), bf16[16,40,256]{2,0,1:T(8,128)(2,1)}) %all-reduce.3.cloned.1.call-update) | async-done | bytes 327696 | tf_op jit(solution)/shard_map/psum | solution.py:140
  153.5 1.3 fusion.28
  155.3 37.4 %all-gather.6.cloned.1.call-done = bf16[320,2560]{1,0:T(8,128)(2,1)} async-done(((bf16[80,2560]{1,0:T(8,128)(2,1)}), bf16[320,2560]{1,0:T(8,128)(2,1)}) %all-gather.6.cloned.1.call-update) | async-done | bytes 1638416 | tf_op jit(solution)/shard_map/all_gather | solution.py:55
  192.7 2.0 fusion.18
  194.7 9.7 %all-gather = bf16[8,320,64]{1,2,0:T(8,128)(2,1)S(1)} all-gather(bf16[1,320,64]{1,2,0:T(8,128)(2,1)S(1)} %fusion.18), channel_id=1, replica_groups=mesh['dp'=4,'seq'=8] {'seq'}, dimensions={0}, use_global_device_ids=true | all-gather | bytes 368640 | tf_op jit(solution)/shard_map/all_gather | solution.py:163
  205.4 7.0 %convolution_bitcast_fusion = f32[2,64,960]{2,1,0:T(8,128)S(1)} fusion(bf16[2,960,2560]{2,1,0:T(8,128)(2,1)} %param.15, bf16[64,2560]{1,0:T(8,128)(2,1)S(1)} %get-tuple-element.5, f32[2560]{0:T(1024)S(1)} %copy-done.5, f32[64]{0:T(128)S(1)} %add_rsqrt_fusion.1), kind=kOutput, calls=%fused_computation.16 | convolution fusion | flops 629800960 | bytes 10660096 | tf_op jit(solution)/shard_map/rd,gfd->grf/dot_general | solution.py:168
  212.4 1.7 convolution_convert_fusion.1
  214.4 9.1 %scatter_fusion = bf16[64,128,512]{2,1,0:T(8,128)(2,1)} fusion(bf16[64,128,512]{2,1,0:T(8,128)(2,1)} %copy.153, s32[64]{0:T(128)S(1)} %reshape.596, bf16[64,512]{1,0:T(8,128)(2,1)S(1)} %reshape.598), kind=kCustom, calls=%fused_computation.1 | custom fusion | bytes 197120 | tf_op jit(solution)/shard_map/scatter | solution.py:180
  223.5 42.6 %all-reduce.5.cloned.1.call-done = bf16[64,2560]{1,0:T(8,128)(2,1)} async-done(((bf16[64,2560]{1,0:T(8,128)(2,1)}), bf16[64,2560]{1,0:T(8,128)(2,1)}) %all-reduce.5.cloned.1.call-update) | async-done | bytes 327696 | tf_op jit(solution)/shard_map/psum | solution.py:171
  266.1 1.1 fusion.25
  267.2 0.8 reshape.586
  (98 shorter events, 7.2 us)
Async XLA Ops:
  7.2 8.0 %copy-start.2 = (bf16[16,4,2560]{2,1,0:T(4,128)(2,1)S(1)}, bf16[16,4,2560]{2,1,0:T(4,128)(2,1)}, u32[]{:S(2)}) copy-start(bf16[16,4,2560]{2,1,0:T(4,128)(2,1)} %param.10) | copy-start | bytes 983044
  7.2 8.2 %copy-start.6 = (f32[2560]{0:T(1024)S(1)}, f32[2560]{0:T(1024)}, u32[]{:S(2)}) copy-start(f32[2560]{0:T(1024)} %param.11) | copy-start | bytes 30724
  7.2 54.3 %all-gather.4.cloned.1.call-start = ((), (), s32[]{:S(2)}) async-start(), calls=%async_computation | async-start | bytes 2457600 | tf_op jit(solution)/shard_map/all_gather | solution.py:54
  15.0 0.7 copy-start
  15.0 0.9 copy-start.7
  15.1 138.4 %all-reduce.3.cloned.1.call-start = ((), (), s32[]{:S(2)}) async-start(), calls=%async_computation.1 | async-start | bytes 655360 | tf_op jit(solution)/shard_map/psum | solution.py:140
  73.7 19.8 %copy-start.3 = (bf16[16,4,3072]{2,1,0:T(4,128)(2,1)}, bf16[16,4,3072]{2,1,0:T(4,128)(2,1)S(1)}, u32[]{:S(2)}) copy-start(bf16[16,4,3072]{2,1,0:T(4,128)(2,1)S(1)} %reshape.581) | copy-start | bytes 1179652
  79.5 15.7 %copy-start.1 = (f32[64,40,128]{2,1,0:T(8,128)}, f32[64,40,128]{2,1,0:T(8,128)S(1)}, u32[]{:S(2)}) copy-start(f32[64,40,128]{2,1,0:T(8,128)S(1)} %get-tuple-element.20) | copy-start | bytes 3932164
  95.3 3.3 %slice-start.2 = ((bf16[16,4,3072]{2,1,0:T(4,128)(2,1)}), bf16[16,4,128]{2,1,0:T(4,128)(2,1)S(1)}, s32[]{:S(2)}) async-start(bf16[16,4,3072]{2,1,0:T(4,128)(2,1)} %copy-done.3), calls=%async_computation.6 | async-start | bytes 32768 | tf_op jit(solution)/shard_map/slice | solution.py:21
  101.5 91.2 %all-gather.6.cloned.1.call-start = ((), (), s32[]{:S(2)}) async-start(), calls=%async_computation.2 | async-start | bytes 2048000 | tf_op jit(solution)/shard_map/all_gather | solution.py:55
  102.2 163.9 %all-reduce.5.cloned.1.call-start = ((), (), s32[]{:S(2)}) async-start(), calls=%async_computation.3 | async-start | bytes 655360 | tf_op jit(solution)/shard_map/psum | solution.py:171
  102.5 13.0 %copy-start.4 = (bf16[16,4,3072]{2,1,0:T(4,128)(2,1)S(1)}, bf16[16,4,3072]{2,1,0:T(4,128)(2,1)}, u32[]{:S(2)}) copy-start(bf16[16,4,3072]{2,1,0:T(4,128)(2,1)} %copy-done.3) | copy-start | bytes 1179652
  204.7 0.7 copy-start.5
  204.9 7.5 %slice-start = ((s8[4915200]{0:T(1024)(128)(4,1)}), s8[4194304]{0:T(1024)(128)(4,1)S(1)}, s32[]{:S(2)}) async-start(s8[4915200]{0:T(1024)(128)(4,1)} %bitcast.50), calls=%async_computation.4 | async-start | bytes 8388608
  205.4 7.0 %slice-start.1 = ((s8[4915200]{0:T(1024)(128)(4,1)}), s8[720896]{0:T(1024)(128)(4,1)S(1)}, s32[]{:S(2)}) async-start(s8[4915200]{0:T(1024)(128)(4,1)} %bitcast.50), calls=%async_computation.5 | async-start | bytes 1441792
  212.3 1.9 slice-start.3
Sparse Core Ops, SparseCore 0:
  15.2 46.2 all-gather.3
  101.6 51.8 all-reduce.2
  155.1 37.5 all-gather.5
  214.2 51.8 all-reduce.4
where the time goes:
time: 275 us; the launch traced here: 274 us
  waiting for transfers between devices  163 us (59%)
  blocking collectives  44.9 us (16%)
  matrix products  23.2 us (8%)
  local copies, waits for them, and re-layouts  21.9 us (8%)
  between operations  14.3 us (5%)
  other arithmetic  6.55 us (2%)
    all_gather x1, waiting for transfers between devices, body(): lax.all_gather(qkv_weight, 'dp', axis=0, tiled=True)  45 us
    psum x1, waiting for transfers between devices, body(): lax.psum(partial_sum.astype(jnp.bfloat16), 'seq').astype(jnp.float32)  42.6 us
    psum x1, waiting for transfers between devices, body(): lax.psum((request_out * rescale[:, :, None]).astype(jnp.bfloat16), 'seq')  37.7 us
    all_gather x1, waiting for transfers between devices, body(): lax.all_gather(out_weight, 'dp', axis=0, tiled=True)  37.4 us
    pmax x1, blocking collectives, body(): global_peak = lax.pmax(request_peak, 'seq')  13.5 us
    psum x1, blocking collectives, body(): lax.psum((request_sum * rescale).astype(jnp.bfloat16), 'seq')  11.9 us
    all_gather x1, blocking collectives, body(): lax.all_gather(local_part, 'seq', axis=1, tiled=True)  9.82 us
    all_gather x1, blocking collectives, body(): heads_out = lax.all_gather(heads_part, 'seq', axis=1, tiled=True)  9.73 us
  transfers between devices with their start and end apart: 4, of which 4 were waited for; matrix products, arithmetic and copies ran while one was open for 5% of the time, Pallas kernels for 0%

commit v1 on v0

v1 whole, which is shorter than its diff:
```python
import functools

import jax
import jax.numpy as jnp
from jax import lax
from jax.experimental import pallas as pl
from jax.experimental.pallas import tpu as pltpu
from jax.sharding import PartitionSpec as P

f32 = jnp.float32
bf16 = jnp.bfloat16
low_fill = -1e30
floor_peak = -1e29
contract = (((1,), (1,)), ((), ()))


def rms_norm(values, gains):
    floats = values.astype(f32)
    return floats * lax.rsqrt(jnp.mean(floats * floats, axis=-1, keepdims=True) + 1e-06) * gains


def swap(values, axis, size, mask):
    return lax.ppermute(values, axis, [(i, i ^ mask) for i in range(size)])


def tree_sum(terms):
    while len(terms) > 1:
        terms = [terms[i] + terms[i + 1] for i in range(0, len(terms), 2)]
    return terms[0]


def copy_kernel(parts, source, target, sems):
    count = source.shape[0] // parts
    copies = [
        pltpu.make_async_copy(
            source.at[pl.ds(i * count, count)], target.at[pl.ds(i * count, count)], sems.at[i]
        )
        for i in range(parts)
    ]
    for copy in copies:
        copy.start()
    for copy in copies:
        copy.wait()


def copy_pool(kv_pool):
    parts = min(16, kv_pool.shape[0])
    return pl.pallas_call(
        functools.partial(copy_kernel, parts),
        out_shape=jax.ShapeDtypeStruct(kv_pool.shape, kv_pool.dtype),
        in_specs=[pl.BlockSpec(memory_space=pl.ANY)],
        out_specs=pl.BlockSpec(memory_space=pl.ANY),
        scratch_shapes=[pltpu.SemaphoreType.DMA((parts,))],
        cost_estimate=pl.CostEstimate(
            flops=0, bytes_accessed=2 * kv_pool.size * 2, transcendentals=0
        ),
        name="copy_pool",
    )(kv_pool)


def split_three(values):
    high = values.astype(bf16).astype(f32)
    middle = (values - high).astype(bf16).astype(f32)
    low = (values - high - middle).astype(bf16).astype(f32)
    return high, middle, low


def diagonal(rows):
    return lax.broadcasted_iota(jnp.int32, (rows, 128), 0) == lax.broadcasted_iota(
        jnp.int32, (rows, 128), 1
    )


def pack_logs(columns, rows):
    eye = diagonal(rows)
    lines = [
        jnp.sum(jnp.where(eye, jnp.broadcast_to(c, (rows, 128)), 0.0), axis=0, keepdims=True)
        for c in columns
    ]
    lines += [jnp.zeros((1, 128), f32)] * (8 - len(lines))
    high, middle, low = split_three(jnp.concatenate(lines, axis=0))
    return jnp.concatenate(
        [
            jnp.concatenate([high, middle], axis=1),
            jnp.concatenate([low, jnp.zeros((8, 128), f32)], axis=1),
        ],
        axis=0,
    )


def unpack_logs(block):
    return block[0:8, 0:128] + block[0:8, 128:256] + block[8:16, 0:128]


def merge_parts(packs, requests, rows):
    total = requests * rows
    bodies = [ref[...].astype(f32) for ref in packs]
    logs = [unpack_logs(body[total : total + 16]) for body in bodies]
    eye = diagonal(rows)
    results, columns = [], []
    for r in range(requests):
        cols = [
            jnp.sum(
                jnp.where(eye, jnp.broadcast_to(log[r : r + 1, :], (rows, 128)), 0.0),
                axis=1,
                keepdims=True,
            )
            for log in logs
        ]
        top = functools.reduce(jnp.maximum, cols)
        scales = [jnp.exp(c - top) for c in cols]
        norm = functools.reduce(jnp.add, scales)
        parts = [
            body[r * rows : (r + 1) * rows] * scale for body, scale in zip(bodies, scales)
        ]
        results.append(functools.reduce(jnp.add, parts) / norm)
        columns.append(top + jnp.log(norm))
    return results, columns


def pair_kernel(requests, rows, mine, other, out):
    results, columns = merge_parts([mine, other], requests, rows)
    body = jnp.concatenate(results + [pack_logs(columns, rows)], axis=0)
    out[...] = body.astype(bf16)


def merge_pair(mine, other, requests, rows):
    return pl.pallas_call(
        functools.partial(pair_kernel, requests, rows),
        out_shape=jax.ShapeDtypeStruct(mine.shape, bf16),
        name="merge_pair",
    )(mine, other)


def final_kernel(count, requests, rows, heads, *refs):
    packs, out, scratch_low, scratch_high = refs[:count], refs[count], refs[-2], refs[-1]
    results, unused = merge_parts(packs, requests, rows)
    body = jnp.concatenate(results, axis=0)
    scratch_low[...] = body[:, 0:128]
    scratch_high[...] = body[:, 128:256]
    lines = requests * rows // heads
    for h in range(heads):
        low = scratch_low[pl.ds(h, lines, stride=heads), :]
        high = scratch_high[pl.ds(h, lines, stride=heads), :]
        out[:, h * 256 : (h + 1) * 256] = jnp.concatenate([low, high], axis=1).astype(bf16)


def merge_final(packs, requests, rows, heads):
    lines = requests * rows // heads
    return pl.pallas_call(
        functools.partial(final_kernel, len(packs), requests, rows, heads),
        out_shape=jax.ShapeDtypeStruct((lines, heads * 256), bf16),
        scratch_shapes=[pltpu.VMEM((requests * rows, 128), f32)] * 2,
        name="merge_final",
    )(*packs)


def attention_kernel(
    dims,
    slots,
    patches,
    lengths,
    place,
    cosine,
    sine,
    projected,
    pool,
    pool_copy,
    packed,
    pool_out,
    buffer,
    query_low,
    query_high,
    fresh,
    peak,
    norm,
    total,
    patch_buffer,
    in_sems,
    patch_sems,
):
    requests, new_count, heads, pages, page_len, window, chunk, n_seq = dims
    rows = new_count * heads
    lines = requests * new_count
    chunks = pages // chunk
    loads = [
        pltpu.make_async_copy(
            pool.at[pl.ds(i * chunk, chunk)], buffer.at[pl.ds(i * chunk, chunk)], in_sems.at[i]
        )
        for i in range(chunks)
    ]
    for load in loads:
        load.start()

    cos = cosine[...]
    sin = sine[...]

    def turned(block):
        x = projected[:, block * 128 : (block + 1) * 128].astype(f32)
        return (x * cos + pltpu.roll(x, 64, 1) * sin).astype(bf16).astype(f32)

    for h in range(heads):
        query_low[pl.ds(h, lines, stride=heads), :] = turned(2 * h)
        query_high[pl.ds(h, lines, stride=heads), :] = projected[
            :, h * 256 + 128 : h * 256 + 256
        ].astype(f32)
    fresh[:, 0:128] = turned(2 * heads).astype(bf16)
    fresh[:, 128:512] = projected[:, heads * 256 + 128 : heads * 256 + 512]

    peak[...] = jnp.full(peak.shape, floor_peak, f32)
    norm[...] = jnp.zeros(norm.shape, f32)
    total[...] = jnp.zeros(total.shape, f32)

    token_of = lax.broadcasted_iota(jnp.int32, (rows, 1), 0) // heads
    lane = lax.broadcasted_iota(jnp.int32, (1, page_len), 1)
    scale = 256.0 ** (-0.5)

    def query_of(r):
        span = pl.ds(pl.multiple_of(r * rows, 8), rows)
        return jnp.concatenate([query_low[span, :], query_high[span, :]], axis=1).astype(bf16)

    def part(query, keys, values, visible):
        scores = lax.dot_general(query, keys, contract, preferred_element_type=f32) * scale
        scores = jnp.where(visible, scores, low_fill)
        top = jnp.maximum(jnp.max(scores, axis=1, keepdims=True), floor_peak)
        weights = jnp.exp(scores - top)
        amount = jnp.sum(weights, axis=1, keepdims=True)
        mixed = jnp.dot(weights.astype(bf16), values, preferred_element_type=f32)
        return top, amount, mixed

    def add(r, top, amount, mixed):
        span = pl.ds(pl.multiple_of(r * rows, 8), rows)
        old = peak[span, :]
        high = jnp.maximum(old, top)
        keep = jnp.exp(old - high)
        take = jnp.exp(top - high)
        peak[span, :] = high
        norm[span, :] = norm[span, :] * keep + amount * take
        total[span, :] = total[span, :] * jnp.concatenate(
            [keep, keep], axis=1
        ) + mixed * jnp.concatenate([take, take], axis=1)

    me = place[0]
    fresh_lane = lax.broadcasted_iota(jnp.int32, (1, lines), 1)
    for step in range(-(-requests // n_seq)):
        r = me + step * n_seq

        @pl.when(r < requests)
        def _():
            index = fresh_lane - r * new_count
            seen = (index >= 0) & (index <= token_of)
            add(r, *part(query_of(r), fresh[:, 0:256], fresh[:, 256:512], seen))

    def one_chunk(c, carry):
        pltpu.make_async_copy(
            pool.at[pl.ds(c * chunk, chunk)], buffer.at[pl.ds(c * chunk, chunk)], in_sems.at[c]
        ).wait()
        parts = []
        for k in range(chunk):
            page = c * chunk + k
            r = slots[0, page]
            length = slots[1, page]
            start = slots[2, page] * page_len
            age = jnp.bitwise_and(length - 1 - start - lane, window - 1)
            limit = jnp.minimum(length - 1, window - 2 - token_of)
            parts.append(
                (
                    r,
                    part(
                        query_of(r),
                        buffer[page, :, 0:256],
                        buffer[page, :, 256:512],
                        age <= limit,
                    ),
                )
            )
        for r, values in parts:
            add(r, *values)
        return carry

    lax.fori_loop(0, chunks, one_chunk, 0)

    def patch_copy(i):
        row = pl.multiple_of(patches[1, i] * 16, 16)
        return pltpu.make_async_copy(
            patch_buffer.at[i],
            pool_out.at[jnp.maximum(patches[0, i], 0), pl.ds(row, 16)],
            patch_sems.at[i],
        )

    def write_patch(i, carry):
        slot = patches[0, i]

        @pl.when(slot >= 0)
        def _():
            r = i // 2
            row = pl.multiple_of(patches[1, i] * 16, 16)
            old = buffer[slot, pl.ds(row, 16), :]
            cycle = patches[2, i] * page_len + row
            line = lax.broadcasted_iota(jnp.int32, (16, lines), 0)
            token = jnp.bitwise_and(cycle + line - lengths[r], window - 1)
            column = lax.broadcasted_iota(jnp.int32, (16, lines), 1)
            pick = (token < new_count) & (column == r * new_count + token)
            new = jnp.dot(pick.astype(f32).astype(bf16), fresh[...], preferred_element_type=f32)
            row_token = jnp.bitwise_and(
                cycle + lax.broadcasted_iota(jnp.int32, (16, 1), 0) - lengths[r], window - 1
            )
            patch_buffer[i] = jnp.where(row_token < new_count, new, old.astype(f32)).astype(bf16)
            patch_copy(i).start()

        return carry

    lax.fori_loop(0, 2 * requests, write_patch, 0)

    half = requests // 2
    for side in range(2):
        logs = []
        for k in range(half):
            r = side * half + k
            span = slice(r * rows, (r + 1) * rows)
            amount = norm[span, :]
            some = amount > 0.0
            safe = jnp.where(some, amount, 1.0)
            logs.append(jnp.where(some, peak[span, :] + jnp.log(safe), low_fill))
            inverse = jnp.where(some, 1.0 / safe, 0.0)
            total[span, :] = total[span, :] * jnp.concatenate([inverse, inverse], axis=1)
        packed[side, 0 : half * rows, :] = total[
            side * half * rows : (side + 1) * half * rows, :
        ].astype(bf16)
        packed[side, half * rows : half * rows + 16, :] = pack_logs(logs, rows).astype(bf16)

    def wait_patch(i, carry):
        @pl.when(patches[0, i] >= 0)
        def _():
            patch_copy(i).wait()

        return carry

    lax.fori_loop(0, 2 * requests, wait_patch, 0)


def attention(dims, slots, patches, lengths, place, cosine, sine, projected, pool, pool_copy):
    requests, new_count, heads, pages, page_len, window, chunk, n_seq = dims
    rows = new_count * heads
    lines = requests * new_count
    smem = pl.BlockSpec(memory_space=pltpu.SMEM)
    vmem = pl.BlockSpec(memory_space=pltpu.VMEM)
    hbm = pl.BlockSpec(memory_space=pl.ANY)
    return pl.pallas_call(
        functools.partial(attention_kernel, dims),
        out_shape=(
            jax.ShapeDtypeStruct((2, requests // 2 * rows + 16, 256), bf16),
            jax.ShapeDtypeStruct(pool.shape, pool.dtype),
        ),
        in_specs=[smem, smem, smem, smem, vmem, vmem, vmem, hbm, hbm],
        out_specs=(vmem, hbm),
        scratch_shapes=[
            pltpu.VMEM(pool.shape, bf16),
            pltpu.VMEM((requests * rows, 128), f32),
            pltpu.VMEM((requests * rows, 128), f32),
            pltpu.VMEM((lines, 512), bf16),
            pltpu.VMEM((requests * rows, 128), f32),
            pltpu.VMEM((requests * rows, 128), f32),
            pltpu.VMEM((requests * rows, 256), f32),
            pltpu.VMEM((2 * requests, 16, 512), bf16),
            pltpu.SemaphoreType.DMA((pages // chunk,)),
            pltpu.SemaphoreType.DMA((2 * requests,)),
        ],
        input_output_aliases={8: 1},
        compiler_params=pltpu.CompilerParams(vmem_limit_bytes=24 * 1024 * 1024),
        cost_estimate=pl.CostEstimate(
            flops=4 * pages * rows * page_len * 256,
            bytes_accessed=pool.size * 2,
            transcendentals=pages * rows * page_len,
        ),
        name="page_attention",
    )(slots, patches, lengths, place, cosine, sine, projected, pool, pool_copy)


def body(
    n_dp,
    n_seq,
    tokens,
    attn_gain,
    qkv_weight,
    out_weight,
    mlp_gain,
    gate_up,
    down_weight,
    kv_pool,
    cache_len,
    page_table,
):
    seq_index = lax.axis_index("seq")
    dp_index = lax.axis_index("dp")
    core = seq_index % 2
    chips = n_seq // 2
    requests, new_count, width = tokens.shape
    pages, page_len, pair_width = kv_pool.shape
    head_dim = pair_width // 2
    heads = out_weight.shape[1] // head_dim
    page_count = page_table.shape[1]
    window = page_count * page_len
    lines = requests * new_count
    half = lines // 2
    rows = new_count * heads

    def ordered(mine, other, axis=0):
        return jnp.where(
            core == 0,
            jnp.concatenate([mine, other], axis=axis),
            jnp.concatenate([other, mine], axis=axis),
        )

    out_local = lax.all_gather(out_weight, "dp", axis=0, tiled=True)

    stream = tokens.reshape(lines, width)
    my_half = jnp.where(core == 0, stream[:half], stream[half:])
    far = list(range(2, n_dp, 2))
    far_halves = [swap(my_half, "dp", n_dp, k) for k in far]
    partner_weight = swap(qkv_weight, "dp", n_dp, 1)
    pool_copy = copy_pool(kv_pool)
    far_half = jnp.concatenate(far_halves, axis=0)
    far_other = swap(far_half, "seq", n_seq, 1)
    groups = [stream]
    for i in range(len(far)):
        groups += [far_half[i * half : (i + 1) * half], far_other[i * half : (i + 1) * half]]
    normed = rms_norm(jnp.concatenate(groups, axis=0), attn_gain).astype(bf16)
    by_mine = lax.dot_general(normed, qkv_weight, contract, preferred_element_type=f32)
    by_partner = lax.dot_general(normed, partner_weight, contract, preferred_element_type=f32)
    products = jnp.where(
        dp_index % 2 == 0,
        jnp.concatenate([by_mine, by_partner], axis=1),
        jnp.concatenate([by_partner, by_mine], axis=1),
    ).astype(bf16)
    blocks = [products[:lines]]
    for i, k in enumerate(far):
        back = swap(products[(i + 1) * lines : (i + 2) * lines], "dp", n_dp, k)
        blocks.append(ordered(back[:half], back[half:]))
    pair = dp_index // 2
    columns = []
    for j in range(n_dp // 2):
        block = blocks[0]
        for k in range(1, n_dp // 2):
            block = jnp.where((pair ^ k) == j, blocks[k], block)
        columns.append(block)
    projected = lax.all_gather(
        jnp.concatenate(columns, axis=1), "seq", axis=1, tiled=True
    )

    positions_int = cache_len[:, None] + jnp.arange(new_count, dtype=jnp.int32)[None, :]
    quarter = head_dim // 4
    inverse = 10000.0 ** (-jnp.arange(quarter).astype(f32) / quarter)
    angles = positions_int.reshape(lines, 1).astype(f32) * inverse
    cosine = jnp.cos(angles)
    sine = jnp.sin(angles)
    cosine = jnp.concatenate([cosine, cosine], axis=1)
    sine = jnp.concatenate([-sine, sine], axis=1)
    slot_ids = seq_index * pages + jnp.arange(pages, dtype=jnp.int32)
    matches = page_table[None, :, :] == slot_ids[:, None, None]
    number = jnp.arange(page_count, dtype=jnp.int32)[None, None, :]
    owner = jnp.arange(requests, dtype=jnp.int32)[None, :, None]
    slots = jnp.stack(
        [
            jnp.sum(jnp.where(matches, owner, 0), axis=(1, 2)),
            jnp.sum(jnp.where(matches, cache_len[None, :, None], 0), axis=(1, 2)),
            jnp.sum(jnp.where(matches, number, 0), axis=(1, 2)),
        ]
    )
    ends = jnp.stack([cache_len, cache_len + (new_count - 1)], axis=1)
    end_page = (ends // page_len) % page_count
    end_block = (ends % page_len) // 16
    hit = end_page[:, :, None] == jnp.arange(page_count, dtype=jnp.int32)[None, None, :]
    end_slot = jnp.sum(jnp.where(hit, page_table[:, None, :], 0), axis=2) - seq_index * pages
    good = (end_slot >= 0) & (end_slot < pages)
    same = (end_page[:, 0] == end_page[:, 1]) & (end_block[:, 0] == end_block[:, 1])
    good = good & jnp.stack([jnp.ones_like(same), ~same], axis=1)
    patches = jnp.stack(
        [
            jnp.where(good, end_slot, -1).reshape(-1),
            end_block.reshape(-1),
            end_page.reshape(-1),
        ]
    )

    dims = (requests, new_count, heads, pages, page_len, window, min(8, pages), n_seq)
    packed, written_pool = attention(
        dims,
        slots,
        patches,
        cache_len,
        seq_index.reshape(1),
        cosine,
        sine,
        projected,
        kv_pool,
        pool_copy,
    )

    side = requests // 2
    mine = jnp.where(core == 0, packed[0], packed[1])
    theirs = jnp.where(core == 0, packed[1], packed[0])
    merged = merge_pair(mine, swap(theirs, "seq", n_seq, 1), side, rows)
    packs = [merged] + [swap(merged, "seq", n_seq, 2 * c) for c in range(1, chips)]
    attended_half = merge_final(packs, side, rows, heads)
    attended = ordered(attended_half, swap(attended_half, "seq", n_seq, 1))

    heads_part = lax.dot_general(
        attended, out_local, contract, preferred_element_type=f32
    ).astype(bf16)
    heads_out = lax.all_gather(heads_part, "seq", axis=1, tiled=True)
    residual = (stream.astype(f32) + heads_out.astype(f32)).astype(bf16)
    hidden_in = rms_norm(residual, mlp_gain).astype(bf16)
    gate_and_up = jnp.einsum("rd,gfd->grf", hidden_in, gate_up, preferred_element_type=f32)
    hidden = (jax.nn.gelu(gate_and_up[0], approximate=True) * gate_and_up[1]).astype(bf16)
    partial_sum = jnp.dot(hidden, down_weight, preferred_element_type=f32)

    keep = jnp.where(core == 0, partial_sum[:half], partial_sum[half:])
    give = jnp.where(core == 0, partial_sum[half:], partial_sum[:half]).astype(bf16)
    chip_sum = (keep + swap(give, "seq", n_seq, 1).astype(f32)).astype(bf16)
    terms = [chip_sum] + [swap(chip_sum, "seq", n_seq, 2 * c) for c in range(1, chips)]
    full_half = tree_sum([term.astype(f32) for term in terms])
    my_residual = jnp.where(core == 0, residual[:half], residual[half:])
    out_half = (my_residual.astype(f32) + full_half).astype(bf16)
    layer_out = ordered(out_half, swap(out_half, "seq", n_seq, 1))
    return layer_out.reshape(requests, new_count, width), written_pool


def solution(mesh):
    in_specs = (
        P("dp", None, None),
        P(),
        P(("seq", "dp"), None),
        P(("seq", "dp"), None),
        P(),
        P(None, "seq", None),
        P("seq", None),
        P(("dp", "seq"), None, None),
        P("dp"),
        P("dp", None),
    )
    out_specs = (P("dp", None, None), P(("dp", "seq"), None, None))
    return jax.shard_map(
        functools.partial(body, mesh.shape["dp"], mesh.shape["seq"]),
        mesh=mesh,
        in_specs=in_specs,
        out_specs=out_specs,
        check_vma=False,
    )
```

time: 275 us -> 398 us (1.45)
  Pallas kernels: 0 us -> 279 us
  waiting for transfers between devices: 163 us -> 45.3 us
  blocking collectives: 44.9 us -> 19.9 us
  local copies, waits for them, and re-layouts: 21.9 us -> 6.8 us
  starting transfers between devices: 0.16 us -> 14.2 us
  matrix products: 23.2 us -> 10.8 us
    pallas_call x0 -> x4, Pallas kernels: none -> 279 us  [the longest x1 255 us: copy_pool(): pl.pallas_call(functools.partial(copy_kernel, parts), out_shape=jax.Shape...]
    all_gather x2 -> x1, waiting for transfers between devices: 82.4 us -> 0.01 us  [body(): out_local = lax.all_gather(out_weight, 'dp', axis=0, tiled=True)]
    psum x2 -> x0, waiting for transfers between devices: 80.3 us -> none  [the longest x1 42.6 us: body(): lax.psum(partial_sum.astype(jnp.bfloat16), 'seq').astype(jnp.float32)]
    ppermute x0 -> x14, waiting for transfers between devices: none -> 45.3 us  [swap(): return lax.ppermute(values, axis, [(i, i ^ mask) for i in range(size)])]
    ppermute x0 -> x14, starting transfers between devices: none -> 14.2 us  [swap(): return lax.ppermute(values, axis, [(i, i ^ mask) for i in range(size)])]
    pmax x1 -> x0, blocking collectives: 13.5 us -> none  [body(): global_peak = lax.pmax(request_peak, 'seq')]
    dot_general x10 -> x5, matrix products: 23.2 us -> 10.8 us  [the longest x1 6.96 us: body(): jnp.einsum('rd,gfd->grf', hidden_in, gate_up, preferred_element_type=f32)]
    psum x1 -> x0, blocking collectives: 11.9 us -> none  [body(): lax.psum((request_sum * rescale).astype(jnp.bfloat16), 'seq')]
  transfers between devices with their start and end apart: 4 -> 15, of which waited for: 4 -> 12; matrix products, arithmetic and copies ran while one was open for 5% -> 2% of each run, Pallas kernels for 0% -> 70%
where the time goes in v1:
time: 398 us; the launch traced here: 397 us
  Pallas kernels  279 us (70%)
  waiting for transfers between devices  45.3 us (11%)
  blocking collectives  19.9 us (5%)
  between operations  14.4 us (4%)
  starting transfers between devices  14.2 us (4%)
  matrix products  10.8 us (3%)
  local copies, waits for them, and re-layouts  6.8 us (2%)
  other arithmetic  6.4 us (2%)
    pallas_call x1, Pallas kernels, copy_pool(): pl.pallas_call(functools.partial(copy_kernel, parts), out_shape=jax.Shape...  255 us
    ppermute x14, waiting for transfers between devices, swap(): return lax.ppermute(values, axis, [(i, i ^ mask) for i in range(size)])  45.3 us
    pallas_call x1, Pallas kernels, attention(): pl.pallas_call(functools.partial(attention_kernel, dims), out_shape=(jax....  19.7 us
    ppermute x14, starting transfers between devices, swap(): return lax.ppermute(values, axis, [(i, i ^ mask) for i in range(size)])  14.2 us
    all_gather x1, blocking collectives, body(): lax.all_gather(jnp.concatenate(columns, axis=1), 'seq', axis=1, tiled=True)  10.3 us
    all_gather x1, blocking collectives, body(): heads_out = lax.all_gather(heads_part, 'seq', axis=1, tiled=True)  9.57 us
  transfers between devices with their start and end apart: 15, of which 12 were waited for; matrix products, arithmetic and copies ran while one was open for 2% of the time, Pallas kernels for 70%

profile of v1, /device:TPU:0, one launch (start us, length us, event | category | flops | bytes accessed | tf_op | source)
XLA Modules:
  0.0 397.0 jit_solution(5843930148107473750)
XLA Ops:
  8.4 4.1 %collective-permute-start = (bf16[32,2560]{1,0:T(8,128)(2,1)S(1)}, bf16[32,2560]{1,0:T(8,128)(2,1)S(1)}, u32[]{:S(2)}, u32[]{:S(2)}) collective-permute-start(bf16[32,2560]{1,0:T(8,128)(2,1)S(1)} %select_n.208), channel_id=1, source_target_pairs={{0,16},{8,24},{16,0},{24,8},{1,17},{9,25},{17,1},{25,9},{2,18},{10... | collective-permute-start | bytes 491528 | tf_op jit(solution)/shard_map/ppermute | solution.py:23
  12.5 1.6 collective-permute-start.2
  17.8 2.5 collective-permute-done
  22.5 20.7 %collective-permute-done.2 = bf16[96,2560]{1,0:T(8,128)(2,1)S(1)} collective-permute-done((bf16[96,2560]{1,0:T(8,128)(2,1)}, bf16[96,2560]{1,0:T(8,128)(2,1)S(1)}, u32[]{:S(2)}, u32[]{:S(2)}) %collective-permute-start.2) | collective-permute-done | bytes 491552 | tf_op jit(solution)/shard_map/ppermute | solution.py:23
  44.6 255.4 %copy_pool.1.pool_copy = bf16[64,128,512]{2,1,0:T(8,128)(2,1)} custom-call(bf16[64,128,512]{2,1,0:T(8,128)(2,1)} %pool.1), custom_call_target="tpu_custom_call" | custom-call | bytes 16777216 | tf_op jit(solution)/shard_map/copy_pool/pallas_call | solution.py:48
  300.1 10.3 %all_gather.9.projected = bf16[64,3072]{1,0:T(8,128)(2,1)S(1)} all-gather(bf16[64,384]{1,0:T(8,128)(2,1)S(1)} %pad_maximum_fusion.1), channel_id=1, replica_groups=mesh['dp'=4,'seq'=8] {'seq'}, dimensions={1}, use_global_device_ids=true | all-gather | bytes 442368 | tf_op jit(solution)/shard_map/all_gather | solution.py:447
  310.4 3.4 copy-done
  313.8 19.7 %page_attention.1 = (bf16[2,336,256]{2,1,0:T(8,128)(2,1)S(1)}, bf16[64,128,512]{2,1,0:T(8,128)(2,1)}) custom-call(s32[3,64]{1,0:T(4,128)S(1)} %pad_add_fusion.slots, s32[3,32]{1,0:T(4,128)S(1)} %pad_add_fusion.1.patches, s32[16]{0:T(128)S(1)} %copy-done.1, s32[1]{0:T(128)} %bitcast.5.place, ...), custom_call_target="tpu_custom_call", output_to_operand_aliasing={{1}: (8, {})} | custom-call | flops 335544320 | bytes 8388608 | tf_op jit(solution)/shard_map/page_attention/pallas_call | solution.py:349
  334.2 1.3 collective-permute-done.4.other
  336.2 1.9 merge_pair.1.refs_0_
  340.4 1.2 collective-permute-start.7
  341.7 3.9 collective-permute-done.5.refs_1_
  345.6 2.6 collective-permute-done.6.refs_2_
  348.2 1.5 collective-permute-done.7.refs_3_
  350.4 2.2 merge_final.1
  352.6 1.6 collective-permute-done.8
  354.2 2.2 fusion.3
  356.4 9.6 %all-gather = bf16[8,320,64]{1,2,0:T(8,128)(2,1)S(1)} all-gather(bf16[1,320,64]{1,2,0:T(8,128)(2,1)S(1)} %fusion.3), channel_id=1, replica_groups=mesh['dp'=4,'seq'=8] {'seq'}, dimensions={0}, use_global_device_ids=true | all-gather | bytes 368640 | tf_op jit(solution)/shard_map/all_gather | solution.py:511
  366.9 7.0 %convolution_bitcast_fusion = f32[2,64,960]{2,1,0:T(8,128)S(1)} fusion(bf16[2,960,2560]{2,1,0:T(8,128)(2,1)} %param.15, bf16[64,2560]{1,0:T(8,128)(2,1)S(1)} %get-tuple-element.10, f32[2560]{0:T(1024)S(1)} %copy-done.10, f32[64]{0:T(128)S(1)} %add_rsqrt_fusion), kind=kOutput, calls=%fused_computation.5 | convolution fusion | flops 629800960 | bytes 10660096 | tf_op jit(solution)/shard_map/rd,gfd->grf/dot_general | solution.py:514
  376.5 1.5 collective-permute-start.10
  378.6 1.5 collective-permute-start.12
  380.0 3.5 collective-permute-done.10
  383.6 4.1 %collective-permute-done.11 = bf16[32,2560]{1,0:T(8,128)(2,1)S(1)} collective-permute-done((bf16[32,2560]{1,0:T(8,128)(2,1)S(1)}, bf16[32,2560]{1,0:T(8,128)(2,1)S(1)}, u32[]{:S(2)}, u32[]{:S(2)}) %collective-permute-start.11) | collective-permute-done | bytes 163872 | tf_op jit(solution)/shard_map/ppermute | solution.py:23
  387.9 1.4 collective-permute-done.13
  (85 shorter events, 17.8 us)
Async XLA Ops:
  7.2 13.2 %copy-start.2 = (bf16[16,4,2560]{2,1,0:T(4,128)(2,1)S(1)}, bf16[16,4,2560]{2,1,0:T(4,128)(2,1)}, u32[]{:S(2)}) copy-start(bf16[16,4,2560]{2,1,0:T(4,128)(2,1)} %param.10) | copy-start | bytes 983044
  7.2 10.4 %copy-start.1 = (s32[16]{0:T(128)S(1)}, s32[16]{0:T(128)}, u32[]{:S(2)}) copy-start(s32[16]{0:T(128)} %lengths.1) | copy-start | bytes 196
  7.2 10.4 %copy-start.8 = (s32[16,16]{1,0:T(8,128)S(1)}, s32[16,16]{1,0:T(8,128)}, u32[]{:S(2)}) copy-start(s32[16,16]{1,0:T(8,128)} %param.19) | copy-start | bytes 3076
  7.2 347.0 %all-gather.3.cloned.1.call-start = ((), (), s32[]{:S(2)}) async-start(), calls=%async_computation | async-start | bytes 2048000 | tf_op jit(solution)/shard_map/all_gather | solution.py:415
  8.3 13.6 %copy-start.9 = (f32[2560]{0:T(1024)S(1)}, f32[2560]{0:T(1024)}, u32[]{:S(2)}) copy-start(f32[2560]{0:T(1024)} %param.11) | copy-start | bytes 30724
  8.4 11.9 %collective-permute-start = (bf16[32,2560]{1,0:T(8,128)(2,1)S(1)}, bf16[32,2560]{1,0:T(8,128)(2,1)S(1)}, u32[]{:S(2)}, u32[]{:S(2)}) collective-permute-start(bf16[32,2560]{1,0:T(8,128)(2,1)S(1)} %select_n.208), channel_id=1, source_target_pairs={{0,16},{8,24},{16,0},{24,8},{1,17},{9,25},{17,1},{25,9},{2,18},{10... | collective-permute-start | bytes 491528 | tf_op jit(solution)/shard_map/ppermute | solution.py:23
  12.5 30.7 %collective-permute-start.2 = (bf16[96,2560]{1,0:T(8,128)(2,1)}, bf16[96,2560]{1,0:T(8,128)(2,1)S(1)}, u32[]{:S(2)}, u32[]{:S(2)}) collective-permute-start(bf16[96,2560]{1,0:T(8,128)(2,1)} %param.12), channel_id=1, source_target_pairs={{0,8},{8,0},{16,24},{24,16},{1,9},{9,1},{17,25},{25,17},{2,10},{10... | collective-permute-start | bytes 1474568 | tf_op jit(solution)/shard_map/ppermute | solution.py:23
  20.3 1.4 collective-permute-start.1
  20.3 1.8 copy-start.3
  43.6 256.3 %collective-permute-start.3 = (bf16[64,192]{1,0:T(8,128)(2,1)S(1)}, bf16[64,192]{1,0:T(8,128)(2,1)S(1)}, u32[]{:S(2)}, u32[]{:S(2)}) collective-permute-start(bf16[64,192]{1,0:T(8,128)(2,1)S(1)} %slice.79), channel_id=1, source_target_pairs={{0,16},{8,24},{16,0},{24,8},{1,17},{9,25},{17,1},{25,9},{2,18},{10... | collective-permute-start | bytes 73736 | tf_op jit(solution)/shard_map/ppermute | solution.py:23
  310.4 3.4 copy-start
  334.2 1.4 collective-permute-start.4
  338.2 7.4 %collective-permute-start.5 = (bf16[336,256]{1,0:T(8,128)(2,1)}, bf16[336,256]{1,0:T(8,128)(2,1)S(1)}, u32[]{:S(2)}, u32[]{:S(2)}) collective-permute-start(bf16[336,256]{1,0:T(8,128)(2,1)} %merge_pair.1.refs_0_), channel_id=1, source_target_pairs={{0,2},{1,3},{2,0},{3,1},{4,6},{5,7},{6,4},{7,5},{8,10},{9,11},{10,... | collective-permute-start | bytes 516104 | tf_op jit(solution)/shard_map/ppermute | solution.py:23
  339.4 8.8 %collective-permute-start.6 = (bf16[336,256]{1,0:T(8,128)(2,1)}, bf16[336,256]{1,0:T(8,128)(2,1)S(1)}, u32[]{:S(2)}, u32[]{:S(2)}) collective-permute-start(bf16[336,256]{1,0:T(8,128)(2,1)} %merge_pair.1.refs_0_), channel_id=1, source_target_pairs={{0,4},{1,5},{2,6},{3,7},{4,0},{5,1},{6,2},{7,3},{8,12},{9,13},{10,... | collective-permute-start | bytes 516104 | tf_op jit(solution)/shard_map/ppermute | solution.py:23
  340.4 9.3 %collective-permute-start.7 = (bf16[336,256]{1,0:T(8,128)(2,1)}, bf16[336,256]{1,0:T(8,128)(2,1)S(1)}, u32[]{:S(2)}, u32[]{:S(2)}) collective-permute-start(bf16[336,256]{1,0:T(8,128)(2,1)} %merge_pair.1.refs_0_), channel_id=1, source_target_pairs={{0,6},{1,7},{2,4},{3,5},{4,2},{5,3},{6,0},{7,1},{8,14},{9,15},{10,... | collective-permute-start | bytes 516104 | tf_op jit(solution)/shard_map/ppermute | solution.py:23
  345.6 4.1 %copy-start.4 = (bf16[336,256]{1,0:T(8,128)(2,1)}, bf16[336,256]{1,0:T(8,128)(2,1)S(1)}, u32[]{:S(2)}) copy-start(bf16[336,256]{1,0:T(8,128)(2,1)S(1)} %collective-permute-done.5.refs_1_) | copy-start | bytes 516100
  352.6 1.6 collective-permute-start.8
  366.4 7.5 %slice-start = ((s8[4915200]{0:T(1024)(128)(4,1)}), s8[4194304]{0:T(1024)(128)(4,1)S(1)}, s32[]{:S(2)}) async-start(s8[4915200]{0:T(1024)(128)(4,1)} %bitcast.45), calls=%async_computation.1 | async-start | bytes 8388608
  366.9 7.0 %slice-start.1 = ((s8[4915200]{0:T(1024)(128)(4,1)}), s8[720896]{0:T(1024)(128)(4,1)S(1)}, s32[]{:S(2)}) async-start(s8[4915200]{0:T(1024)(128)(4,1)} %bitcast.45), calls=%async_computation.2 | async-start | bytes 1441792
  375.0 1.5 collective-permute-start.9
  376.5 7.1 %collective-permute-start.10 = (bf16[32,2560]{1,0:T(8,128)(2,1)S(1)}, bf16[32,2560]{1,0:T(8,128)(2,1)S(1)}, u32[]{:S(2)}, u32[]{:S(2)}) collective-permute-start(bf16[32,2560]{1,0:T(8,128)(2,1)S(1)} %add_convert_fusion.1), channel_id=1, source_target_pairs={{0,2},{1,3},{2,0},{3,1},{4,6},{5,7},{6,4},{7,5},{8,10},{9,11},{10,... | collective-permute-start | bytes 491528 | tf_op jit(solution)/shard_map/ppermute | solution.py:23
  378.0 9.7 %collective-permute-start.11 = (bf16[32,2560]{1,0:T(8,128)(2,1)S(1)}, bf16[32,2560]{1,0:T(8,128)(2,1)S(1)}, u32[]{:S(2)}, u32[]{:S(2)}) collective-permute-start(bf16[32,2560]{1,0:T(8,128)(2,1)S(1)} %add_convert_fusion.1), channel_id=1, source_target_pairs={{0,4},{1,5},{2,6},{3,7},{4,0},{5,1},{6,2},{7,3},{8,12},{9,13},{10,... | collective-permute-start | bytes 491528 | tf_op jit(solution)/shard_map/ppermute | solution.py:23
  378.6 9.1 %collective-permute-start.12 = (bf16[32,2560]{1,0:T(8,128)(2,1)S(1)}, bf16[32,2560]{1,0:T(8,128)(2,1)S(1)}, u32[]{:S(2)}, u32[]{:S(2)}) collective-permute-start(bf16[32,2560]{1,0:T(8,128)(2,1)S(1)} %add_convert_fusion.1), channel_id=1, source_target_pairs={{0,6},{1,7},{2,4},{3,5},{4,2},{5,3},{6,0},{7,1},{8,14},{9,15},{10,... | collective-permute-start | bytes 491528 | tf_op jit(solution)/shard_map/ppermute | solution.py:23
  387.8 1.5 collective-permute-start.13
  (4 other events, 3.5 us)
Sparse Core Ops, SparseCore 0:
  14.2 40.9 all-gather.2

commit v2 on v1

--- a/solution.py
+++ b/solution.py
@@ -29,28 +29,40 @@
     return terms[0]
 
 
-def copy_kernel(parts, source, target, sems):
+def copy_kernel(parts, source, target, buffer, in_sems, out_sems):
     count = source.shape[0] // parts
-    copies = [
-        pltpu.make_async_copy(
-            source.at[pl.ds(i * count, count)], target.at[pl.ds(i * count, count)], sems.at[i]
-        )
-        for i in range(parts)
+    spans = [pl.ds(i * count, count) for i in range(parts)]
+    loads = [
+        pltpu.make_async_copy(source.at[span], buffer.at[span], in_sems.at[i])
+        for i, span in enumerate(spans)
     ]
-    for copy in copies:
-        copy.start()
-    for copy in copies:
-        copy.wait()
+    stores = [
+        pltpu.make_async_copy(buffer.at[span], target.at[span], out_sems.at[i])
+        for i, span in enumerate(spans)
+    ]
+    for load in loads:
+        load.start()
+    for load, store in zip(loads, stores):
+        load.wait()
+        store.start()
+    for store in stores:
+        store.wait()
 
 
 def copy_pool(kv_pool):
     parts = min(16, kv_pool.shape[0])
+    hbm = pl.BlockSpec(memory_space=pltpu.HBM)
     return pl.pallas_call(
         functools.partial(copy_kernel, parts),
-        out_shape=jax.ShapeDtypeStruct(kv_pool.shape, kv_pool.dtype),
-        in_specs=[pl.BlockSpec(memory_space=pl.ANY)],
-        out_specs=pl.BlockSpec(memory_space=pl.ANY),
-        scratch_shapes=[pltpu.SemaphoreType.DMA((parts,))],
+        out_shape=pltpu.HBM(kv_pool.shape, kv_pool.dtype),
+        in_specs=[hbm],
+        out_specs=hbm,
+        scratch_shapes=[
+            pltpu.VMEM(kv_pool.shape, kv_pool.dtype),
+            pltpu.SemaphoreType.DMA((parts,)),
+            pltpu.SemaphoreType.DMA((parts,)),
+        ],
+        compiler_params=pltpu.CompilerParams(vmem_limit_bytes=24 * 1024 * 1024),
         cost_estimate=pl.CostEstimate(
             flops=0, bytes_accessed=2 * kv_pool.size * 2, transcendentals=0
         ),
@@ -128,6 +140,8 @@
     return pl.pallas_call(
         functools.partial(pair_kernel, requests, rows),
         out_shape=jax.ShapeDtypeStruct(mine.shape, bf16),
+        in_specs=[pl.BlockSpec(memory_space=pltpu.VMEM)] * 2,
+        out_specs=pl.BlockSpec(memory_space=pltpu.VMEM),
         name="merge_pair",
     )(mine, other)
 
@@ -150,6 +164,8 @@
     return pl.pallas_call(
         functools.partial(final_kernel, len(packs), requests, rows, heads),
         out_shape=jax.ShapeDtypeStruct((lines, heads * 256), bf16),
+        in_specs=[pl.BlockSpec(memory_space=pltpu.VMEM)] * len(packs),
+        out_specs=pl.BlockSpec(memory_space=pltpu.VMEM),
         scratch_shapes=[pltpu.VMEM((requests * rows, 128), f32)] * 2,
         name="merge_final",
     )(*packs)
@@ -166,11 +182,13 @@
     projected,
     pool,
     pool_copy,
-    packed,
+    mine,
+    theirs,
     pool_out,
     buffer,
     query_low,
     query_high,
+    queries,
     fresh,
     peak,
     norm,
@@ -182,15 +200,13 @@
     requests, new_count, heads, pages, page_len, window, chunk, n_seq = dims
     rows = new_count * heads
     lines = requests * new_count
-    chunks = pages // chunk
-    loads = [
-        pltpu.make_async_copy(
-            pool.at[pl.ds(i * chunk, chunk)], buffer.at[pl.ds(i * chunk, chunk)], in_sems.at[i]
-        )
-        for i in range(chunks)
-    ]
-    for load in loads:
-        load.start()
+
+    def load(c):
+        span = pl.ds(c * chunk, chunk)
+        return pltpu.make_async_copy(pool.at[span], buffer.at[span], in_sems.at[c])
+
+    for c in range(pages // chunk):
+        load(c).start()
 
     cos = cosine[...]
     sin = sine[...]
@@ -215,18 +231,23 @@
     lane = lax.broadcasted_iota(jnp.int32, (1, page_len), 1)
     scale = 256.0 ** (-0.5)
 
-    def query_of(r):
-        span = pl.ds(pl.multiple_of(r * rows, 8), rows)
-        return jnp.concatenate([query_low[span, :], query_high[span, :]], axis=1).astype(bf16)
-
-    def part(query, keys, values, visible):
-        scores = lax.dot_general(query, keys, contract, preferred_element_type=f32) * scale
-        scores = jnp.where(visible, scores, low_fill)
+    for r in range(requests):
+        span = slice(r * rows, (r + 1) * rows)
+        queries[r, 0:rows, :] = jnp.concatenate(
+            [query_low[span, :], query_high[span, :]], axis=1
+        ).astype(bf16)
+
+    def score(r, keys):
+        return lax.dot_general(queries[r, 0:rows, :], keys, contract, preferred_element_type=f32)
+
+    def weigh(scores, visible):
+        scores = jnp.where(visible, scores * scale, low_fill)
         top = jnp.maximum(jnp.max(scores, axis=1, keepdims=True), floor_peak)
         weights = jnp.exp(scores - top)
-        amount = jnp.sum(weights, axis=1, keepdims=True)
-        mixed = jnp.dot(weights.astype(bf16), values, preferred_element_type=f32)
-        return top, amount, mixed
+        return top, jnp.sum(weights, axis=1, keepdims=True), weights.astype(bf16)
+
+    def mix(weights, values):
+        return jnp.dot(weights, values, preferred_element_type=f32)
 
     def add(r, top, amount, mixed):
         span = pl.ds(pl.multiple_of(r * rows, 8), rows)
@@ -249,36 +270,30 @@
         def _():
             index = fresh_lane - r * new_count
             seen = (index >= 0) & (index <= token_of)
-            add(r, *part(query_of(r), fresh[:, 0:256], fresh[:, 256:512], seen))
+            top, amount, weights = weigh(score(r, fresh[:, 0:256]), seen)
+            add(r, top, amount, mix(weights, fresh[:, 256:512]))
 
     def one_chunk(c, carry):
-        pltpu.make_async_copy(
-            pool.at[pl.ds(c * chunk, chunk)], buffer.at[pl.ds(c * chunk, chunk)], in_sems.at[c]
-        ).wait()
-        parts = []
-        for k in range(chunk):
-            page = c * chunk + k
-            r = slots[0, page]
+        load(c).wait()
+        numbers = [c * chunk + k for k in range(chunk)]
+        owners = [slots[0, page] for page in numbers]
+        scores = [score(r, buffer[page, :, 0:256]) for r, page in zip(owners, numbers)]
+        weighed = []
+        for page, values in zip(numbers, scores):
             length = slots[1, page]
             start = slots[2, page] * page_len
             age = jnp.bitwise_and(length - 1 - start - lane, window - 1)
             limit = jnp.minimum(length - 1, window - 2 - token_of)
-            parts.append(
-                (
-                    r,
-                    part(
-                        query_of(r),
-                        buffer[page, :, 0:256],
-                        buffer[page, :, 256:512],
-                        age <= limit,
-                    ),
-                )
-            )
-        for r, values in parts:
-            add(r, *values)
+            weighed.append(weigh(values, age <= limit))
+        mixed = [
+            mix(weights, buffer[page, :, 256:512])
+            for page, (top, amount, weights) in zip(numbers, weighed)
+        ]
+        for r, (top, amount, weights), values in zip(owners, weighed, mixed):
+            add(r, top, amount, values)
         return carry
 
-    lax.fori_loop(0, chunks, one_chunk, 0)
+    lax.fori_loop(0, pages // chunk, one_chunk, 0)
 
     def patch_copy(i):
         row = pl.multiple_of(patches[1, i] * 16, 16)
@@ -313,21 +328,20 @@
     lax.fori_loop(0, 2 * requests, write_patch, 0)
 
     half = requests // 2
-    for side in range(2):
+    core = place[1]
+    for side, out in ((core, mine), (1 - core, theirs)):
         logs = []
         for k in range(half):
-            r = side * half + k
-            span = slice(r * rows, (r + 1) * rows)
+            span = pl.ds(pl.multiple_of((side * half + k) * rows, 8), rows)
             amount = norm[span, :]
             some = amount > 0.0
             safe = jnp.where(some, amount, 1.0)
             logs.append(jnp.where(some, peak[span, :] + jnp.log(safe), low_fill))
             inverse = jnp.where(some, 1.0 / safe, 0.0)
             total[span, :] = total[span, :] * jnp.concatenate([inverse, inverse], axis=1)
-        packed[side, 0 : half * rows, :] = total[
-            side * half * rows : (side + 1) * half * rows, :
-        ].astype(bf16)
-        packed[side, half * rows : half * rows + 16, :] = pack_logs(logs, rows).astype(bf16)
+        span = pl.ds(pl.multiple_of(side * half * rows, 8), half * rows)
+        out[0 : half * rows, :] = total[span, :].astype(bf16)
+        out[half * rows : half * rows + 16, :] = pack_logs(logs, rows).astype(bf16)
 
     def wait_patch(i, carry):
         @pl.when(patches[0, i] >= 0)
@@ -345,19 +359,21 @@
     lines = requests * new_count
     smem = pl.BlockSpec(memory_space=pltpu.SMEM)
     vmem = pl.BlockSpec(memory_space=pltpu.VMEM)
-    hbm = pl.BlockSpec(memory_space=pl.ANY)
+    hbm = pl.BlockSpec(memory_space=pltpu.HBM)
     return pl.pallas_call(
         functools.partial(attention_kernel, dims),
         out_shape=(
-            jax.ShapeDtypeStruct((2, requests // 2 * rows + 16, 256), bf16),
-            jax.ShapeDtypeStruct(pool.shape, pool.dtype),
+            jax.ShapeDtypeStruct((requests // 2 * rows + 16, 256), bf16),
+            jax.ShapeDtypeStruct((requests // 2 * rows + 16, 256), bf16),
+            pltpu.HBM(pool.shape, pool.dtype),
         ),
         in_specs=[smem, smem, smem, smem, vmem, vmem, vmem, hbm, hbm],
-        out_specs=(vmem, hbm),
+        out_specs=(vmem, vmem, hbm),
         scratch_shapes=[
             pltpu.VMEM(pool.shape, bf16),
             pltpu.VMEM((requests * rows, 128), f32),
             pltpu.VMEM((requests * rows, 128), f32),
+            pltpu.VMEM((requests, -(-rows // 16) * 16, 256), bf16),
             pltpu.VMEM((lines, 512), bf16),
             pltpu.VMEM((requests * rows, 128), f32),
             pltpu.VMEM((requests * rows, 128), f32),
@@ -366,7 +382,7 @@
             pltpu.SemaphoreType.DMA((pages // chunk,)),
             pltpu.SemaphoreType.DMA((2 * requests,)),
         ],
-        input_output_aliases={8: 1},
+        input_output_aliases={8: 2},
         compiler_params=pltpu.CompilerParams(vmem_limit_bytes=24 * 1024 * 1024),
         cost_estimate=pl.CostEstimate(
             flops=4 * pages * rows * page_len * 256,
@@ -412,20 +428,21 @@
             jnp.concatenate([other, mine], axis=axis),
         )
 
-    out_local = lax.all_gather(out_weight, "dp", axis=0, tiled=True)
-
     stream = tokens.reshape(lines, width)
-    my_half = jnp.where(core == 0, stream[:half], stream[half:])
+    partner_weight = swap(qkv_weight, "dp", n_dp, 1)
+    own_normed = rms_norm(stream, attn_gain).astype(bf16)
+    my_half = jnp.where(core == 0, own_normed[:half], own_normed[half:])
     far = list(range(2, n_dp, 2))
     far_halves = [swap(my_half, "dp", n_dp, k) for k in far]
-    partner_weight = swap(qkv_weight, "dp", n_dp, 1)
-    pool_copy = copy_pool(kv_pool)
+    held_pool = pltpu.with_memory_space_constraint(kv_pool, pltpu.HBM)
+    pool_copy = copy_pool(held_pool)
     far_half = jnp.concatenate(far_halves, axis=0)
     far_other = swap(far_half, "seq", n_seq, 1)
-    groups = [stream]
+    groups = [own_normed]
     for i in range(len(far)):
         groups += [far_half[i * half : (i + 1) * half], far_other[i * half : (i + 1) * half]]
-    normed = rms_norm(jnp.concatenate(groups, axis=0), attn_gain).astype(bf16)
+    partner_weight, pool_copy = lax.optimization_barrier((partner_weight, pool_copy))
+    normed = jnp.concatenate(groups, axis=0)
     by_mine = lax.dot_general(normed, qkv_weight, contract, preferred_element_type=f32)
     by_partner = lax.dot_general(normed, partner_weight, contract, preferred_element_type=f32)
     products = jnp.where(
@@ -433,6 +450,10 @@
         jnp.concatenate([by_mine, by_partner], axis=1),
         jnp.concatenate([by_partner, by_mine], axis=1),
     ).astype(bf16)
+    out_mine, far_half = lax.optimization_barrier((out_weight, far_half))
+    out_blocks = {0: out_mine, 1: swap(out_mine, "dp", n_dp, 1)}
+    for k in far:
+        out_blocks[k] = swap(out_mine, "dp", n_dp, k)
     blocks = [products[:lines]]
     for i, k in enumerate(far):
         back = swap(products[(i + 1) * lines : (i + 2) * lines], "dp", n_dp, k)
@@ -483,34 +504,49 @@
         ]
     )
 
-    dims = (requests, new_count, heads, pages, page_len, window, min(8, pages), n_seq)
-    packed, written_pool = attention(
+    dims = (requests, new_count, heads, pages, page_len, window, min(16, pages), n_seq)
+    mine, theirs, written_pool = attention(
         dims,
         slots,
         patches,
         cache_len,
-        seq_index.reshape(1),
+        jnp.stack([seq_index, core]),
         cosine,
         sine,
         projected,
-        kv_pool,
+        held_pool,
         pool_copy,
     )
 
     side = requests // 2
-    mine = jnp.where(core == 0, packed[0], packed[1])
-    theirs = jnp.where(core == 0, packed[1], packed[0])
     merged = merge_pair(mine, swap(theirs, "seq", n_seq, 1), side, rows)
+    merged, *early = lax.optimization_barrier((merged, *[out_blocks[k] for k in [1, *far]]))
+    for k, block in zip([1, *far], early):
+        out_blocks[k] = block
+    for k in far:
+        out_blocks[k ^ 1] = swap(out_blocks[k], "dp", n_dp, 1)
     packs = [merged] + [swap(merged, "seq", n_seq, 2 * c) for c in range(1, chips)]
+    packs, late = lax.optimization_barrier((packs, [out_blocks[k ^ 1] for k in far]))
+    for k, block in zip(far, late):
+        out_blocks[k ^ 1] = block
     attended_half = merge_final(packs, side, rows, heads)
     attended = ordered(attended_half, swap(attended_half, "seq", n_seq, 1))
 
-    heads_part = lax.dot_general(
-        attended, out_local, contract, preferred_element_type=f32
-    ).astype(bf16)
+    by_block = [
+        lax.dot_general(attended, out_blocks[k], contract, preferred_element_type=f32).astype(bf16)
+        for k in range(n_dp)
+    ]
+    heads_part = []
+    for j in range(n_dp):
+        block = by_block[0]
+        for k in range(1, n_dp):
+            block = jnp.where((dp_index ^ k) == j, by_block[k], block)
+        heads_part.append(block)
+    heads_part = jnp.concatenate(heads_part, axis=1)
     heads_out = lax.all_gather(heads_part, "seq", axis=1, tiled=True)
     residual = (stream.astype(f32) + heads_out.astype(f32)).astype(bf16)
     hidden_in = rms_norm(residual, mlp_gain).astype(bf16)
+    hidden_in = lax.optimization_barrier(hidden_in)
     gate_and_up = jnp.einsum("rd,gfd->grf", hidden_in, gate_up, preferred_element_type=f32)
     hidden = (jax.nn.gelu(gate_and_up[0], approximate=True) * gate_and_up[1]).astype(bf16)
     partial_sum = jnp.dot(hidden, down_weight, preferred_element_type=f32)

time: 398 us -> 105 us (0.26)
  Pallas kernels: 279 us -> 17.4 us
  waiting for transfers between devices: 45.3 us -> 24.3 us
  between operations: 14.4 us -> 1.01 us
  starting transfers between devices: 14.2 us -> 19.1 us
    pallas_call x1, Pallas kernels: 255 us -> 6.64 us  [copy_pool(): pl.pallas_call(functools.partial(copy_kernel, parts), out_shape=pltpu.HBM...]
    ppermute x14 -> x17, waiting for transfers between devices: 45.3 us -> 24.3 us  [swap(): return lax.ppermute(values, axis, [(i, i ^ mask) for i in range(size)])]
    pallas_call x1, Pallas kernels: 19.7 us -> 6.63 us  [attention(): pl.pallas_call(functools.partial(attention_kernel, dims), out_shape=(jax....]
    ppermute x14 -> x17, starting transfers between devices: 14.2 us -> 19.1 us  [swap(): return lax.ppermute(values, axis, [(i, i ^ mask) for i in range(size)])]
  transfers between devices with their start and end apart: 15 -> 17, of which waited for: 12 -> 11; matrix products, arithmetic and copies ran while one was open for 2% -> 5% of each run, Pallas kernels for 70% -> 15%
where the time goes in v2:
time: 105 us
  waiting for transfers between devices  24.3 us (23%)
  starting transfers between devices  19.1 us (18%)
  blocking collectives  18.3 us (17%)
  Pallas kernels  17.4 us (17%)
  matrix products  12.5 us (12%)
  other arithmetic  7.23 us (7%)
  local copies, waits for them, and re-layouts  4.85 us (5%)
    ppermute x17, waiting for transfers between devices, swap(): return lax.ppermute(values, axis, [(i, i ^ mask) for i in range(size)])  24.3 us
    ppermute x17, starting transfers between devices, swap(): return lax.ppermute(values, axis, [(i, i ^ mask) for i in range(size)])  19.1 us
    all_gather x1, blocking collectives, body(): lax.all_gather(jnp.concatenate(columns, axis=1), 'seq', axis=1, tiled=True)  9.89 us
    all_gather x1, blocking collectives, body(): heads_out = lax.all_gather(heads_part, 'seq', axis=1, tiled=True)  8.39 us
    dot_general x1, matrix products, body(): jnp.einsum('rd,gfd->grf', hidden_in, gate_up, preferred_element_type=f32)  6.88 us
    pallas_call x1, Pallas kernels, copy_pool(): pl.pallas_call(functools.partial(copy_kernel, parts), out_shape=pltpu.HBM...  6.64 us
    pallas_call x1, Pallas kernels, attention(): pl.pallas_call(functools.partial(attention_kernel, dims), out_shape=(jax....  6.63 us
    dot_general x4, matrix products, body(): lax.dot_general(attended, out_blocks[k], contract, preferred_element_type...  4.05 us
  transfers between devices with their start and end apart: 17, of which 11 were waited for; matrix products, arithmetic and copies ran while one was open for 5% of the time, Pallas kernels for 15%

profile of v2, /device:TPU:0, one launch (start us, length us, event | category | flops | bytes accessed | tf_op | source)
XLA Modules:
  0.0 104.6 jit_solution(10089081194553811945)
XLA Ops:
  3.9 4.1 %collective-permute-start = (bf16[32,2560]{1,0:T(8,128)(2,1)S(1)}, bf16[32,2560]{1,0:T(8,128)(2,1)S(1)}, u32[]{:S(2)}, u32[]{:S(2)}) collective-permute-start(bf16[32,2560]{1,0:T(8,128)(2,1)S(1)} %slice_select_fusion.1), channel_id=1, source_target_pairs={{0,16},{8,24},{16,0},{24,8},{1,17},{9,25},{17,1},{25,9},{2,18},{10... | collective-permute-start | bytes 491528 | tf_op jit(solution)/shard_map/ppermute | solution.py:23
  8.0 1.6 %collective-permute-start.2 = (bf16[96,2560]{1,0:T(8,128)(2,1)}, bf16[96,2560]{1,0:T(8,128)(2,1)S(1)}, u32[]{:S(2)}, u32[]{:S(2)}) collective-permute-start(bf16[96,2560]{1,0:T(8,128)(2,1)} %param.12), channel_id=1, source_target_pairs={{0,8},{8,0},{16,24},{24,16},{1,9},{9,1},{17,25},{25,17},{2,10},{10... | collective-permute-start | bytes 1474568 | tf_op jit(solution)/shard_map/ppermute | solution.py:23
  14.1 1.7 %collective-permute-done = bf16[32,2560]{1,0:T(8,128)(2,1)S(1)} collective-permute-done((bf16[32,2560]{1,0:T(8,128)(2,1)S(1)}, bf16[32,2560]{1,0:T(8,128)(2,1)S(1)}, u32[]{:S(2)}, u32[]{:S(2)}) %collective-permute-start) | collective-permute-done | bytes 163872 | tf_op jit(solution)/shard_map/ppermute | solution.py:23
  15.8 6.6 %copy_pool.1.pool_copy = bf16[64,128,512]{2,1,0:T(8,128)(2,1)} custom-call(bf16[64,128,512]{2,1,0:T(8,128)(2,1)} %pool.1), custom_call_target="tpu_custom_call" | custom-call | bytes 16777216 | tf_op jit(solution)/shard_map/copy_pool/pallas_call | solution.py:55
  25.0 2.7 %collective-permute-start.5 = (bf16[80,2560]{1,0:T(8,128)(2,1)S(1)}, bf16[80,2560]{1,0:T(8,128)(2,1)S(1)}, u32[]{:S(2)}, u32[]{:S(2)}) collective-permute-start(bf16[80,2560]{1,0:T(8,128)(2,1)S(1)} %copy-done.9), channel_id=1, source_target_pairs={{0,8},{8,0},{16,24},{24,16},{1,9},{9,1},{17,25},{25,17},{2,10},{10... | collective-permute-start | bytes 1228808 | tf_op jit(solution)/shard_map/ppermute | solution.py:23
  29.1 9.9 %all_gather.6.projected = bf16[64,3072]{1,0:T(8,128)(2,1)S(1)} all-gather(bf16[64,384]{1,0:T(8,128)(2,1)S(1)} %pad_maximum_fusion.3), channel_id=1, replica_groups=mesh['dp'=4,'seq'=8] {'seq'}, dimensions={1}, use_global_device_ids=true | all-gather | bytes 442368 | tf_op jit(solution)/shard_map/all_gather | solution.py:468
  39.0 6.6 %page_attention.1 = (bf16[336,256]{1,0:T(8,128)(2,1)S(1)}, bf16[336,256]{1,0:T(8,128)(2,1)S(1)}, bf16[64,128,512]{2,1,0:T(8,128)(2,1)}) custom-call(s32[3,64]{1,0:T(4,128)S(1)} %pad_add_fusion.slots, s32[3,32]{1,0:T(4,128)S(1)} %pad_add_fusion.1.patches, s32[16]{0:T(128)S(1)} %copy-done.1, ...), custom_call_target="tpu_custom_call", output_to_operand_aliasing={{2}: (8, {})} | custom-call | flops 335544320 | bytes 8388608 | tf_op jit(solution)/shard_map/page_attention/pallas_call | solution.py:363
  48.7 1.9 %merge_pair.1.refs_0_ = bf16[336,256]{1,0:T(8,128)(2,1)} custom-call(bf16[336,256]{1,0:T(8,128)(2,1)} %copy-done, bf16[336,256]{1,0:T(8,128)(2,1)} %copy-done.5), custom_call_target="tpu_custom_call" | custom-call | tf_op jit(solution)/shard_map/merge_pair/pallas_call | solution.py:140
  51.4 1.9 %collective-permute-start.7 = (bf16[336,256]{1,0:T(8,128)(2,1)}, bf16[336,256]{1,0:T(8,128)(2,1)S(1)}, u32[]{:S(2)}, u32[]{:S(2)}) collective-permute-start(bf16[336,256]{1,0:T(8,128)(2,1)} %merge_pair.1.refs_0_), channel_id=1, source_target_pairs={{0,2},{1,3},{2,0},{3,1},{4,6},{5,7},{6,4},{7,5},{8,10},{9,11},{10,... | collective-permute-start | bytes 516104 | tf_op jit(solution)/shard_map/ppermute | solution.py:23
  53.5 1.5 %collective-permute-start.9 = (bf16[336,256]{1,0:T(8,128)(2,1)}, bf16[336,256]{1,0:T(8,128)(2,1)S(1)}, u32[]{:S(2)}, u32[]{:S(2)}) collective-permute-start(bf16[336,256]{1,0:T(8,128)(2,1)} %merge_pair.1.refs_0_), channel_id=1, source_target_pairs={{0,6},{1,7},{2,4},{3,5},{4,2},{5,3},{6,0},{7,1},{8,14},{9,15},{10,... | collective-permute-start | bytes 516104 | tf_op jit(solution)/shard_map/ppermute | solution.py:23
  55.0 3.9 %collective-permute-done.7.refs_1_ = bf16[336,256]{1,0:T(8,128)(2,1)S(1)} collective-permute-done((bf16[336,256]{1,0:T(8,128)(2,1)}, bf16[336,256]{1,0:T(8,128)(2,1)S(1)}, u32[]{:S(2)}, u32[]{:S(2)}) %collective-permute-start.7) | collective-permute-done | bytes 172064 | tf_op jit(solution)/shard_map/ppermute | solution.py:23
  58.8 4.5 %collective-permute-done.8.refs_2_ = bf16[336,256]{1,0:T(8,128)(2,1)S(1)} collective-permute-done((bf16[336,256]{1,0:T(8,128)(2,1)}, bf16[336,256]{1,0:T(8,128)(2,1)S(1)}, u32[]{:S(2)}, u32[]{:S(2)}) %collective-permute-start.8) | collective-permute-done | bytes 172064 | tf_op jit(solution)/shard_map/ppermute | solution.py:23
  64.0 2.2 %merge_final.1 = bf16[32,2560]{1,0:T(8,128)(2,1)} custom-call(bf16[336,256]{1,0:T(8,128)(2,1)} %merge_pair.1.refs_0_, bf16[336,256]{1,0:T(8,128)(2,1)} %copy-done.2, bf16[336,256]{1,0:T(8,128)(2,1)} %copy-done.3, bf16[336,256]{1,0:T(8,128)(2,1)} %copy-done.4), custom_call_target="tpu_custom_call" | custom-call | tf_op jit(solution)/shard_map/merge_final/pallas_call | solution.py:164
  66.3 1.6 %collective-permute-done.11 = bf16[32,2560]{1,0:T(8,128)(2,1)S(1)} collective-permute-done((bf16[32,2560]{1,0:T(8,128)(2,1)}, bf16[32,2560]{1,0:T(8,128)(2,1)S(1)}, u32[]{:S(2)}, u32[]{:S(2)}) %collective-permute-start.11) | collective-permute-done | bytes 163872 | tf_op jit(solution)/shard_map/ppermute | solution.py:23
  67.9 1.3 %convolution_convert_fusion = bf16[64,80]{1,0:T(8,128)(2,1)S(1)} fusion(bf16[80,2560]{1,0:T(8,128)(2,1)S(1)} %copy-done.9, bf16[32,2560]{1,0:T(8,128)(2,1)S(1)} %collective-permute-done.11, bf16[32,2560]{1,0:T(8,128)(2,1)} %merge_final.1, pred[]{:T(512)S(6)} %eq.94), kind=kOutput, calls=%fused_computation.1 | convolution fusion | flops 27694080 | bytes 747521 | tf_op jit(solution)/shard_map/dot_general | solution.py:536
  69.2 1.3 %convolution_convert_fusion.2 = bf16[64,80]{1,0:T(8,128)(2,1)S(1)} fusion(bf16[80,2560]{1,0:T(8,128)(2,1)S(1)} %collective-permute-done.6, bf16[32,2560]{1,0:T(8,128)(2,1)S(1)} %collective-permute-done.11, bf16[32,2560]{1,0:T(8,128)(2,1)} %merge_final.1, pred[]{:T(512)S(6)} %eq.94), kind=kOutput, calls=%fused_computation.3 | convolution fusion | flops 27694080 | bytes 747521 | tf_op jit(solution)/shard_map/dot_general | solution.py:536
  70.4 1.3 %convolution_convert_fusion.1 = bf16[64,80]{1,0:T(8,128)(2,1)S(1)} fusion(bf16[80,2560]{1,0:T(8,128)(2,1)S(1)} %collective-permute-done.5, bf16[32,2560]{1,0:T(8,128)(2,1)S(1)} %collective-permute-done.11, bf16[32,2560]{1,0:T(8,128)(2,1)} %merge_final.1, pred[]{:T(512)S(6)} %eq.94), kind=kOutput, calls=%fused_computation.2 | convolution fusion | flops 27694080 | bytes 747521 | tf_op jit(solution)/shard_map/dot_general | solution.py:536
  72.1 8.4 %all-gather = bf16[8,320,64]{1,2,0:T(8,128)(2,1)S(1)} all-gather(bf16[1,320,64]{1,2,0:T(8,128)(2,1)S(1)} %maximum_bitcast_fusion), channel_id=1, replica_groups=mesh['dp'=4,'seq'=8] {'seq'}, dimensions={0}, use_global_device_ids=true | all-gather | bytes 368640 | tf_op jit(solution)/shard_map/all_gather | solution.py:546
  81.3 6.9 %convolution_bitcast_fusion = f32[2,64,960]{2,1,0:T(8,128)S(1)} fusion(bf16[2,960,2560]{2,1,0:T(8,128)(2,1)} %param.15, bf16[64,2560]{1,0:T(8,128)(2,1)S(1)} %fusion.2), kind=kOutput, calls=%fused_computation | convolution fusion | flops 629145600 | bytes 10649600 | tf_op jit(solution)/shard_map/rd,gfd->grf/dot_general | solution.py:550
  90.7 1.8 %collective-permute-start.13 = (bf16[32,2560]{1,0:T(8,128)(2,1)S(1)}, bf16[32,2560]{1,0:T(8,128)(2,1)S(1)}, u32[]{:S(2)}, u32[]{:S(2)}) collective-permute-start(bf16[32,2560]{1,0:T(8,128)(2,1)S(1)} %add_convert_fusion.1), channel_id=1, source_target_pairs={{0,2},{1,3},{2,0},{3,1},{4,6},{5,7},{6,4},{7,5},{8,10},{9,11},{10,... | collective-permute-start | bytes 491528 | tf_op jit(solution)/shard_map/ppermute | solution.py:23
  92.8 1.5 %collective-permute-start.15 = (bf16[32,2560]{1,0:T(8,128)(2,1)S(1)}, bf16[32,2560]{1,0:T(8,128)(2,1)S(1)}, u32[]{:S(2)}, u32[]{:S(2)}) collective-permute-start(bf16[32,2560]{1,0:T(8,128)(2,1)S(1)} %add_convert_fusion.1), channel_id=1, source_target_pairs={{0,6},{1,7},{2,4},{3,5},{4,2},{5,3},{6,0},{7,1},{8,14},{9,15},{10,... | collective-permute-start | bytes 491528 | tf_op jit(solution)/shard_map/ppermute | solution.py:23
  94.3 3.5 %collective-permute-done.13 = bf16[32,2560]{1,0:T(8,128)(2,1)S(1)} collective-permute-done((bf16[32,2560]{1,0:T(8,128)(2,1)S(1)}, bf16[32,2560]{1,0:T(8,128)(2,1)S(1)}, u32[]{:S(2)}, u32[]{:S(2)}) %collective-permute-start.13) | collective-permute-done | bytes 163872 | tf_op jit(solution)/shard_map/ppermute | solution.py:23
  97.8 4.4 %collective-permute-done.14 = bf16[32,2560]{1,0:T(8,128)(2,1)S(1)} collective-permute-done((bf16[32,2560]{1,0:T(8,128)(2,1)S(1)}, bf16[32,2560]{1,0:T(8,128)(2,1)S(1)}, u32[]{:S(2)}, u32[]{:S(2)}) %collective-permute-start.14) | collective-permute-done | bytes 163872 | tf_op jit(solution)/shard_map/ppermute | solution.py:23
  102.4 1.4 %collective-permute-done.16 = bf16[32,2560]{1,0:T(8,128)(2,1)S(1)} collective-permute-done((bf16[32,2560]{1,0:T(8,128)(2,1)S(1)}, bf16[32,2560]{1,0:T(8,128)(2,1)S(1)}, u32[]{:S(2)}, u32[]{:S(2)}) %collective-permute-start.16) | collective-permute-done | bytes 163872 | tf_op jit(solution)/shard_map/ppermute | solution.py:23
  (91 shorter events, 21.4 us)
Async XLA Ops:
  3.9 11.9 %collective-permute-start = (bf16[32,2560]{1,0:T(8,128)(2,1)S(1)}, bf16[32,2560]{1,0:T(8,128)(2,1)S(1)}, u32[]{:S(2)}, u32[]{:S(2)}) collective-permute-start(bf16[32,2560]{1,0:T(8,128)(2,1)S(1)} %slice_select_fusion.1), channel_id=1, source_target_pairs={{0,16},{8,24},{16,0},{24,8},{1,17},{9,25},{17,1},{25,9},{2,18},{10... | collective-permute-start | bytes 491528 | tf_op jit(solution)/shard_map/ppermute | solution.py:23
  8.0 15.2 %collective-permute-start.2 = (bf16[96,2560]{1,0:T(8,128)(2,1)}, bf16[96,2560]{1,0:T(8,128)(2,1)S(1)}, u32[]{:S(2)}, u32[]{:S(2)}) collective-permute-start(bf16[96,2560]{1,0:T(8,128)(2,1)} %param.12), channel_id=1, source_target_pairs={{0,8},{8,0},{16,24},{24,16},{1,9},{9,1},{17,25},{25,17},{2,10},{10... | collective-permute-start | bytes 1474568 | tf_op jit(solution)/shard_map/ppermute | solution.py:23
  15.8 6.8 %collective-permute-start.1 = (bf16[32,2560]{1,0:T(8,128)(2,1)S(1)}, bf16[32,2560]{1,0:T(8,128)(2,1)S(1)}, u32[]{:S(2)}, u32[]{:S(2)}) collective-permute-start(bf16[32,2560]{1,0:T(8,128)(2,1)S(1)} %collective-permute-done), channel_id=1, source_target_pairs={{0,1},{1,0},{2,3},{3,2},{4,5},{5,4},{6,7},{7,6},{8,9},{9,8},{10,11... | collective-permute-start | bytes 491528 | tf_op jit(solution)/shard_map/ppermute | solution.py:23
  15.8 6.8 %copy-start.8 = (bf16[96,2560]{1,0:T(8,128)(2,1)S(1)}, bf16[96,2560]{1,0:T(8,128)(2,1)}, u32[]{:S(2)}) copy-start(bf16[96,2560]{1,0:T(8,128)(2,1)} %param.12) | copy-start | bytes 1474564
  15.8 9.1 %copy-start.9 = (bf16[80,2560]{1,0:T(8,128)(2,1)S(1)}, bf16[80,2560]{1,0:T(8,128)(2,1)}, u32[]{:S(2)}) copy-start(bf16[80,2560]{1,0:T(8,128)(2,1)} %param.13) | copy-start | bytes 1228804
  22.5 16.5 %copy-start.1 = (s32[16]{0:T(128)S(1)}, s32[16]{0:T(128)}, u32[]{:S(2)}) copy-start(s32[16]{0:T(128)} %lengths.1) | copy-start | bytes 196
  23.6 5.3 %collective-permute-start.3 = (bf16[64,192]{1,0:T(8,128)(2,1)S(1)}, bf16[64,192]{1,0:T(8,128)(2,1)S(1)}, u32[]{:S(2)}, u32[]{:S(2)}) collective-permute-start(bf16[64,192]{1,0:T(8,128)(2,1)S(1)} %slice.69), channel_id=1, source_target_pairs={{0,16},{8,24},{16,0},{24,8},{1,17},{9,25},{17,1},{25,9},{2,18},{10... | collective-permute-start | bytes 73736 | tf_op jit(solution)/shard_map/ppermute | solution.py:23
  25.0 25.7 %collective-permute-start.5 = (bf16[80,2560]{1,0:T(8,128)(2,1)S(1)}, bf16[80,2560]{1,0:T(8,128)(2,1)S(1)}, u32[]{:S(2)}, u32[]{:S(2)}) collective-permute-start(bf16[80,2560]{1,0:T(8,128)(2,1)S(1)} %copy-done.9), channel_id=1, source_target_pairs={{0,8},{8,0},{16,24},{24,16},{1,9},{9,1},{17,25},{25,17},{2,10},{10... | collective-permute-start | bytes 1228808 | tf_op jit(solution)/shard_map/ppermute | solution.py:23
  27.6 23.0 %collective-permute-start.6 = (bf16[80,2560]{1,0:T(8,128)(2,1)S(1)}, bf16[80,2560]{1,0:T(8,128)(2,1)S(1)}, u32[]{:S(2)}, u32[]{:S(2)}) collective-permute-start(bf16[80,2560]{1,0:T(8,128)(2,1)S(1)} %copy-done.9), channel_id=1, source_target_pairs={{0,16},{8,24},{16,0},{24,8},{1,17},{9,25},{17,1},{25,9},{2,18},{10... | collective-permute-start | bytes 1228808 | tf_op jit(solution)/shard_map/ppermute | solution.py:23
  46.3 1.7 %collective-permute-start.4 = (bf16[336,256]{1,0:T(8,128)(2,1)S(1)}, bf16[336,256]{1,0:T(8,128)(2,1)S(1)}, u32[]{:S(2)}, u32[]{:S(2)}) collective-permute-start(bf16[336,256]{1,0:T(8,128)(2,1)S(1)} %get-tuple-element.19), channel_id=1, source_target_pairs={{0,1},{1,0},{2,3},{3,2},{4,5},{5,4},{6,7},{7,6},{8,9},{9,8},{10,11... | collective-permute-start | bytes 516104 | tf_op jit(solution)/shard_map/ppermute | solution.py:23
  50.6 12.7 %collective-permute-start.10 = (bf16[80,2560]{1,0:T(8,128)(2,1)S(1)}, bf16[80,2560]{1,0:T(8,128)(2,1)S(1)}, u32[]{:S(2)}, u32[]{:S(2)}) collective-permute-start(bf16[80,2560]{1,0:T(8,128)(2,1)S(1)} %collective-permute-done.6), channel_id=1, source_target_pairs={{0,8},{8,0},{16,24},{24,16},{1,9},{9,1},{17,25},{25,17},{2,10},{10... | collective-permute-start | bytes 1228808 | tf_op jit(solution)/shard_map/ppermute | solution.py:23
  51.4 7.4 %collective-permute-start.7 = (bf16[336,256]{1,0:T(8,128)(2,1)}, bf16[336,256]{1,0:T(8,128)(2,1)S(1)}, u32[]{:S(2)}, u32[]{:S(2)}) collective-permute-start(bf16[336,256]{1,0:T(8,128)(2,1)} %merge_pair.1.refs_0_), channel_id=1, source_target_pairs={{0,2},{1,3},{2,0},{3,1},{4,6},{5,7},{6,4},{7,5},{8,10},{9,11},{10,... | collective-permute-start | bytes 516104 | tf_op jit(solution)/shard_map/ppermute | solution.py:23
  53.3 10.0 %collective-permute-start.8 = (bf16[336,256]{1,0:T(8,128)(2,1)}, bf16[336,256]{1,0:T(8,128)(2,1)S(1)}, u32[]{:S(2)}, u32[]{:S(2)}) collective-permute-start(bf16[336,256]{1,0:T(8,128)(2,1)} %merge_pair.1.refs_0_), channel_id=1, source_target_pairs={{0,4},{1,5},{2,6},{3,7},{4,0},{5,1},{6,2},{7,3},{8,12},{9,13},{10,... | collective-permute-start | bytes 516104 | tf_op jit(solution)/shard_map/ppermute | solution.py:23
  53.5 9.8 %collective-permute-start.9 = (bf16[336,256]{1,0:T(8,128)(2,1)}, bf16[336,256]{1,0:T(8,128)(2,1)S(1)}, u32[]{:S(2)}, u32[]{:S(2)}) collective-permute-start(bf16[336,256]{1,0:T(8,128)(2,1)} %merge_pair.1.refs_0_), channel_id=1, source_target_pairs={{0,6},{1,7},{2,4},{3,5},{4,2},{5,3},{6,0},{7,1},{8,14},{9,15},{10,... | collective-permute-start | bytes 516104 | tf_op jit(solution)/shard_map/ppermute | solution.py:23
  66.3 5.4 %copy-start.6 = (bf16[32,2560]{1,0:T(8,128)(2,1)S(1)}, bf16[32,2560]{1,0:T(8,128)(2,1)}, u32[]{:S(2)}) copy-start(bf16[32,2560]{1,0:T(8,128)(2,1)} %merge_final.1) | copy-start | bytes 491524
  66.3 1.6 %collective-permute-start.11 = (bf16[32,2560]{1,0:T(8,128)(2,1)}, bf16[32,2560]{1,0:T(8,128)(2,1)S(1)}, u32[]{:S(2)}, u32[]{:S(2)}) collective-permute-start(bf16[32,2560]{1,0:T(8,128)(2,1)} %merge_final.1), channel_id=1, source_target_pairs={{0,1},{1,0},{2,3},{3,2},{4,5},{5,4},{6,7},{7,6},{8,9},{9,8},{10,11... | collective-permute-start | bytes 491528 | tf_op jit(solution)/shard_map/ppermute | solution.py:23
  69.1 12.0 %copy-start.7 = (f32[2560]{0:T(1024)S(1)}, f32[2560]{0:T(1024)}, u32[]{:S(2)}) copy-start(f32[2560]{0:T(1024)} %param.14) | copy-start | bytes 30724
  80.9 7.3 %slice-start = ((s8[4915200]{0:T(1024)(128)(4,1)}), s8[4194304]{0:T(1024)(128)(4,1)S(1)}, s32[]{:S(2)}) async-start(s8[4915200]{0:T(1024)(128)(4,1)} %bitcast.43), calls=%async_computation | async-start | bytes 8388608
  81.3 6.9 %slice-start.1 = ((s8[4915200]{0:T(1024)(128)(4,1)}), s8[720896]{0:T(1024)(128)(4,1)S(1)}, s32[]{:S(2)}) async-start(s8[4915200]{0:T(1024)(128)(4,1)} %bitcast.43), calls=%async_computation.1 | async-start | bytes 1441792
  89.2 1.5 %collective-permute-start.12 = (bf16[32,2560]{1,0:T(8,128)(2,1)S(1)}, bf16[32,2560]{1,0:T(8,128)(2,1)S(1)}, u32[]{:S(2)}, u32[]{:S(2)}) collective-permute-start(bf16[32,2560]{1,0:T(8,128)(2,1)S(1)} %select_convert_fusion), channel_id=1, source_target_pairs={{0,1},{1,0},{2,3},{3,2},{4,5},{5,4},{6,7},{7,6},{8,9},{9,8},{10,11... | collective-permute-start | bytes 491528 | tf_op jit(solution)/shard_map/ppermute | solution.py:23
  90.7 7.1 %collective-permute-start.13 = (bf16[32,2560]{1,0:T(8,128)(2,1)S(1)}, bf16[32,2560]{1,0:T(8,128)(2,1)S(1)}, u32[]{:S(2)}, u32[]{:S(2)}) collective-permute-start(bf16[32,2560]{1,0:T(8,128)(2,1)S(1)} %add_convert_fusion.1), channel_id=1, source_target_pairs={{0,2},{1,3},{2,0},{3,1},{4,6},{5,7},{6,4},{7,5},{8,10},{9,11},{10,... | collective-permute-start | bytes 491528 | tf_op jit(solution)/shard_map/ppermute | solution.py:23
  92.5 9.7 %collective-permute-start.14 = (bf16[32,2560]{1,0:T(8,128)(2,1)S(1)}, bf16[32,2560]{1,0:T(8,128)(2,1)S(1)}, u32[]{:S(2)}, u32[]{:S(2)}) collective-permute-start(bf16[32,2560]{1,0:T(8,128)(2,1)S(1)} %add_convert_fusion.1), channel_id=1, source_target_pairs={{0,4},{1,5},{2,6},{3,7},{4,0},{5,1},{6,2},{7,3},{8,12},{9,13},{10,... | collective-permute-start | bytes 491528 | tf_op jit(solution)/shard_map/ppermute | solution.py:23
  92.8 9.4 %collective-permute-start.15 = (bf16[32,2560]{1,0:T(8,128)(2,1)S(1)}, bf16[32,2560]{1,0:T(8,128)(2,1)S(1)}, u32[]{:S(2)}, u32[]{:S(2)}) collective-permute-start(bf16[32,2560]{1,0:T(8,128)(2,1)S(1)} %add_convert_fusion.1), channel_id=1, source_target_pairs={{0,6},{1,7},{2,4},{3,5},{4,2},{5,3},{6,0},{7,1},{8,14},{9,15},{10,... | collective-permute-start | bytes 491528 | tf_op jit(solution)/shard_map/ppermute | solution.py:23
  102.3 1.5 %collective-permute-start.16 = (bf16[32,2560]{1,0:T(8,128)(2,1)S(1)}, bf16[32,2560]{1,0:T(8,128)(2,1)S(1)}, u32[]{:S(2)}, u32[]{:S(2)}) collective-permute-start(bf16[32,2560]{1,0:T(8,128)(2,1)S(1)} %add_convert_fusion), channel_id=1, source_target_pairs={{0,1},{1,0},{2,3},{3,2},{4,5},{5,4},{6,7},{7,6},{8,9},{9,8},{10,11... | collective-permute-start | bytes 491528 | tf_op jit(solution)/shard_map/ppermute | solution.py:23
  (5 other events, 7.2 us)

commit v3 on v2

--- a/solution.py
+++ b/solution.py
@@ -29,8 +29,10 @@
     return terms[0]
 
 
-def copy_kernel(parts, source, target, buffer, in_sems, out_sems):
-    count = source.shape[0] // parts
+def write_kernel(dims, parts, patches, lengths, fresh, source, target, buffer, in_sems, out_sems):
+    requests, new_count, heads, pages, page_len, window, chunk, n_seq = dims
+    lines = requests * new_count
+    count = pages // parts
     spans = [pl.ds(i * count, count) for i in range(parts)]
     loads = [
         pltpu.make_async_copy(source.at[span], buffer.at[span], in_sems.at[i])
@@ -42,32 +44,59 @@
     ]
     for load in loads:
         load.start()
-    for load, store in zip(loads, stores):
+    for load in loads:
         load.wait()
+
+    def write_patch(i, carry):
+        slot = patches[0, i]
+
+        @pl.when(slot >= 0)
+        def _():
+            r = i // 2
+            row = pl.multiple_of(patches[1, i] * 16, 16)
+            old = buffer[slot, pl.ds(row, 16), :]
+            first = patches[2, i] * page_len + row - lengths[r]
+            line = lax.broadcasted_iota(jnp.int32, (16, lines), 0)
+            token = jnp.bitwise_and(first + line, window - 1)
+            column = lax.broadcasted_iota(jnp.int32, (16, lines), 1)
+            pick = (token < new_count) & (column == r * new_count + token)
+            new = jnp.dot(pick.astype(f32).astype(bf16), fresh[...], preferred_element_type=f32)
+            row_token = jnp.bitwise_and(
+                first + lax.broadcasted_iota(jnp.int32, (16, 1), 0), window - 1
+            )
+            buffer[slot, pl.ds(row, 16), :] = jnp.where(
+                row_token < new_count, new, old.astype(f32)
+            ).astype(bf16)
+
+        return carry
+
+    lax.fori_loop(0, 2 * requests, write_patch, 0)
+    for store in stores:
         store.start()
     for store in stores:
         store.wait()
 
 
-def copy_pool(kv_pool):
+def write_pool(dims, patches, lengths, fresh, kv_pool):
     parts = min(16, kv_pool.shape[0])
+    smem = pl.BlockSpec(memory_space=pltpu.SMEM)
     hbm = pl.BlockSpec(memory_space=pltpu.HBM)
     return pl.pallas_call(
-        functools.partial(copy_kernel, parts),
+        functools.partial(write_kernel, dims, parts),
         out_shape=pltpu.HBM(kv_pool.shape, kv_pool.dtype),
-        in_specs=[hbm],
+        in_specs=[smem, smem, pl.BlockSpec(memory_space=pltpu.VMEM), hbm],
         out_specs=hbm,
         scratch_shapes=[
             pltpu.VMEM(kv_pool.shape, kv_pool.dtype),
             pltpu.SemaphoreType.DMA((parts,)),
             pltpu.SemaphoreType.DMA((parts,)),
         ],
-        compiler_params=pltpu.CompilerParams(vmem_limit_bytes=24 * 1024 * 1024),
+        compiler_params=pltpu.CompilerParams(vmem_limit_bytes=12 * 1024 * 1024),
         cost_estimate=pl.CostEstimate(
             flops=0, bytes_accessed=2 * kv_pool.size * 2, transcendentals=0
         ),
-        name="copy_pool",
-    )(kv_pool)
+        name="write_pool",
+    )(patches, lengths, fresh, kv_pool)
 
 
 def split_three(values):
@@ -142,12 +171,13 @@
         out_shape=jax.ShapeDtypeStruct(mine.shape, bf16),
         in_specs=[pl.BlockSpec(memory_space=pltpu.VMEM)] * 2,
         out_specs=pl.BlockSpec(memory_space=pltpu.VMEM),
+        compiler_params=pltpu.CompilerParams(vmem_limit_bytes=8 * 1024 * 1024),
         name="merge_pair",
     )(mine, other)
 
 
 def final_kernel(count, requests, rows, heads, *refs):
-    packs, out, scratch_low, scratch_high = refs[:count], refs[count], refs[-2], refs[-1]
+    packs, out, scratch_low, scratch_high = refs[:count], refs[count + 1], refs[-2], refs[-1]
     results, unused = merge_parts(packs, requests, rows)
     body = jnp.concatenate(results, axis=0)
     scratch_low[...] = body[:, 0:128]
@@ -159,43 +189,38 @@
         out[:, h * 256 : (h + 1) * 256] = jnp.concatenate([low, high], axis=1).astype(bf16)
 
 
-def merge_final(packs, requests, rows, heads):
+def merge_final(packs, token, requests, rows, heads):
     lines = requests * rows // heads
     return pl.pallas_call(
         functools.partial(final_kernel, len(packs), requests, rows, heads),
         out_shape=jax.ShapeDtypeStruct((lines, heads * 256), bf16),
-        in_specs=[pl.BlockSpec(memory_space=pltpu.VMEM)] * len(packs),
+        in_specs=[pl.BlockSpec(memory_space=pltpu.VMEM)] * (len(packs) + 1),
         out_specs=pl.BlockSpec(memory_space=pltpu.VMEM),
         scratch_shapes=[pltpu.VMEM((requests * rows, 128), f32)] * 2,
+        compiler_params=pltpu.CompilerParams(vmem_limit_bytes=8 * 1024 * 1024),
         name="merge_final",
-    )(*packs)
+    )(*packs, token)
 
 
 def attention_kernel(
     dims,
     slots,
-    patches,
-    lengths,
     place,
     cosine,
     sine,
     projected,
     pool,
-    pool_copy,
     mine,
     theirs,
-    pool_out,
+    fresh,
     buffer,
     query_low,
     query_high,
     queries,
-    fresh,
     peak,
     norm,
     total,
-    patch_buffer,
     in_sems,
-    patch_sems,
 ):
     requests, new_count, heads, pages, page_len, window, chunk, n_seq = dims
     rows = new_count * heads
@@ -295,38 +320,6 @@
 
     lax.fori_loop(0, pages // chunk, one_chunk, 0)
 
-    def patch_copy(i):
-        row = pl.multiple_of(patches[1, i] * 16, 16)
-        return pltpu.make_async_copy(
-            patch_buffer.at[i],
-            pool_out.at[jnp.maximum(patches[0, i], 0), pl.ds(row, 16)],
-            patch_sems.at[i],
-        )
-
-    def write_patch(i, carry):
-        slot = patches[0, i]
-
-        @pl.when(slot >= 0)
-        def _():
-            r = i // 2
-            row = pl.multiple_of(patches[1, i] * 16, 16)
-            old = buffer[slot, pl.ds(row, 16), :]
-            cycle = patches[2, i] * page_len + row
-            line = lax.broadcasted_iota(jnp.int32, (16, lines), 0)
-            token = jnp.bitwise_and(cycle + line - lengths[r], window - 1)
-            column = lax.broadcasted_iota(jnp.int32, (16, lines), 1)
-            pick = (token < new_count) & (column == r * new_count + token)
-            new = jnp.dot(pick.astype(f32).astype(bf16), fresh[...], preferred_element_type=f32)
-            row_token = jnp.bitwise_and(
-                cycle + lax.broadcasted_iota(jnp.int32, (16, 1), 0) - lengths[r], window - 1
-            )
-            patch_buffer[i] = jnp.where(row_token < new_count, new, old.astype(f32)).astype(bf16)
-            patch_copy(i).start()
-
-        return carry
-
-    lax.fori_loop(0, 2 * requests, write_patch, 0)
-
     half = requests // 2
     core = place[1]
     for side, out in ((core, mine), (1 - core, theirs)):
@@ -343,54 +336,174 @@
         out[0 : half * rows, :] = total[span, :].astype(bf16)
         out[half * rows : half * rows + 16, :] = pack_logs(logs, rows).astype(bf16)
 
-    def wait_patch(i, carry):
-        @pl.when(patches[0, i] >= 0)
-        def _():
-            patch_copy(i).wait()
-
-        return carry
-
-    lax.fori_loop(0, 2 * requests, wait_patch, 0)
-
-
-def attention(dims, slots, patches, lengths, place, cosine, sine, projected, pool, pool_copy):
+
+def attention(dims, slots, place, cosine, sine, projected, pool):
     requests, new_count, heads, pages, page_len, window, chunk, n_seq = dims
     rows = new_count * heads
-    lines = requests * new_count
     smem = pl.BlockSpec(memory_space=pltpu.SMEM)
     vmem = pl.BlockSpec(memory_space=pltpu.VMEM)
-    hbm = pl.BlockSpec(memory_space=pltpu.HBM)
+    pack = jax.ShapeDtypeStruct((requests // 2 * rows + 16, 256), bf16)
     return pl.pallas_call(
         functools.partial(attention_kernel, dims),
-        out_shape=(
-            jax.ShapeDtypeStruct((requests // 2 * rows + 16, 256), bf16),
-            jax.ShapeDtypeStruct((requests // 2 * rows + 16, 256), bf16),
-            pltpu.HBM(pool.shape, pool.dtype),
-        ),
-        in_specs=[smem, smem, smem, smem, vmem, vmem, vmem, hbm, hbm],
-        out_specs=(vmem, vmem, hbm),
+        out_shape=(pack, pack, jax.ShapeDtypeStruct((requests * new_count, 512), bf16)),
+        in_specs=[smem, smem, vmem, vmem, vmem, pl.BlockSpec(memory_space=pltpu.HBM)],
+        out_specs=(vmem, vmem, vmem),
         scratch_shapes=[
             pltpu.VMEM(pool.shape, bf16),
             pltpu.VMEM((requests * rows, 128), f32),
             pltpu.VMEM((requests * rows, 128), f32),
             pltpu.VMEM((requests, -(-rows // 16) * 16, 256), bf16),
-            pltpu.VMEM((lines, 512), bf16),
             pltpu.VMEM((requests * rows, 128), f32),
             pltpu.VMEM((requests * rows, 128), f32),
             pltpu.VMEM((requests * rows, 256), f32),
-            pltpu.VMEM((2 * requests, 16, 512), bf16),
             pltpu.SemaphoreType.DMA((pages // chunk,)),
-            pltpu.SemaphoreType.DMA((2 * requests,)),
         ],
-        input_output_aliases={8: 2},
-        compiler_params=pltpu.CompilerParams(vmem_limit_bytes=24 * 1024 * 1024),
+        compiler_params=pltpu.CompilerParams(vmem_limit_bytes=20 * 1024 * 1024),
         cost_estimate=pl.CostEstimate(
             flops=4 * pages * rows * page_len * 256,
             bytes_accessed=pool.size * 2,
             transcendentals=pages * rows * page_len,
         ),
         name="page_attention",
-    )(slots, patches, lengths, place, cosine, sine, projected, pool, pool_copy)
+    )(slots, place, cosine, sine, projected, pool)
+
+
+def project_kernel(count, place, mine, other, *refs):
+    blocks, out = refs[:count], refs[count]
+    core, plane = place[1], place[2]
+    low = jnp.where(core == 0, mine[...], other[...])
+    high = jnp.where(core == 0, other[...], mine[...])
+    attended = jnp.concatenate([low, high], axis=0)
+    products = [
+        lax.dot_general(attended, block[...], contract, preferred_element_type=f32)
+        for block in blocks
+    ]
+    columns = []
+    for j in range(count):
+        column = products[0]
+        for k in range(1, count):
+            column = jnp.where((plane ^ k) == j, products[k], column)
+        columns.append(column)
+    out[...] = jnp.concatenate(columns, axis=1).astype(bf16)
+
+
+def project_out(place, mine, other, blocks):
+    vmem = pl.BlockSpec(memory_space=pltpu.VMEM)
+    shape = (2 * mine.shape[0], len(blocks) * blocks[0].shape[0])
+    return pl.pallas_call(
+        functools.partial(project_kernel, len(blocks)),
+        out_shape=jax.ShapeDtypeStruct(shape, bf16),
+        in_specs=[pl.BlockSpec(memory_space=pltpu.SMEM)] + [vmem] * (2 + len(blocks)),
+        out_specs=vmem,
+        compiler_params=pltpu.CompilerParams(vmem_limit_bytes=8 * 1024 * 1024),
+        name="project_out",
+    )(place, mine, other, *blocks)
+
+
+def fetch_kernel(parts, gate_up, down, after, gates, downs, token, sems):
+    units = down.shape[0]
+    size = units // parts
+    copies = []
+    for i in range(parts):
+        span = pl.ds(i * size, size)
+        copies.append(pltpu.make_async_copy(gate_up.at[0, span], gates.at[0, span], sems.at[0, i]))
+        copies.append(pltpu.make_async_copy(gate_up.at[1, span], gates.at[1, span], sems.at[1, i]))
+        copies.append(pltpu.make_async_copy(down.at[span], downs.at[span], sems.at[2, i]))
+    for copy in copies:
+        copy.start()
+    token[...] = jnp.zeros(token.shape, f32)
+    for copy in copies:
+        copy.wait()
+
+
+def fetch_weights(gate_up, down, after):
+    parts = max(c for c in (1, 2, 3, 4) if down.shape[0] % (16 * c) == 0)
+    hbm = pl.BlockSpec(memory_space=pltpu.HBM)
+    anywhere = pl.BlockSpec(memory_space=pl.ANY)
+    return pl.pallas_call(
+        functools.partial(fetch_kernel, parts),
+        out_shape=(
+            jax.ShapeDtypeStruct(gate_up.shape, bf16),
+            jax.ShapeDtypeStruct(down.shape, bf16),
+            jax.ShapeDtypeStruct((8, 128), f32),
+        ),
+        in_specs=[hbm, hbm, anywhere],
+        out_specs=(anywhere, anywhere, pl.BlockSpec(memory_space=pltpu.VMEM)),
+        scratch_shapes=[pltpu.SemaphoreType.DMA((3, parts))],
+        compiler_params=pltpu.CompilerParams(vmem_limit_bytes=2 * 1024 * 1024),
+        cost_estimate=pl.CostEstimate(
+            flops=0, bytes_accessed=2 * (gate_up.size + down.size), transcendentals=0
+        ),
+        name="fetch_weights",
+    )(
+        pltpu.with_memory_space_constraint(gate_up, pltpu.HBM),
+        pltpu.with_memory_space_constraint(down, pltpu.HBM),
+        after,
+    )
+
+
+def mlp_kernel(
+    chunk, place, stream, heads_out, gain, gates, downs, keep, give, kept_residual, residual, total
+):
+    units, width = downs.shape
+    count = units // chunk
+    gathered = jnp.concatenate(
+        [heads_out[i].astype(f32) for i in range(heads_out.shape[0])], axis=1
+    )
+    summed = stream[...].astype(f32) + gathered
+    residual[...] = summed.astype(bf16).astype(f32)
+    floats = residual[...]
+    spread = lax.rsqrt(jnp.mean(floats * floats, axis=-1, keepdims=True) + 1e-06)
+    inputs = (floats * spread * gain[...]).astype(bf16)
+    root = (2.0 / 3.141592653589793) ** 0.5
+
+    def rise(c):
+        span = slice(c * chunk, (c + 1) * chunk)
+        gate = lax.dot_general(inputs, gates[0, span, :], contract, preferred_element_type=f32)
+        up = lax.dot_general(inputs, gates[1, span, :], contract, preferred_element_type=f32)
+        inner = root * (gate + 0.044715 * (gate * gate * gate))
+        return (0.5 * gate * (1.0 + jnp.tanh(inner)) * up).astype(bf16)
+
+    def fall(c, hidden):
+        span = slice(c * chunk, (c + 1) * chunk)
+        product = jnp.dot(hidden, downs[span, :], preferred_element_type=f32)
+        if c == 0:
+            total[...] = product
+        else:
+            total[...] += product
+
+    before = rise(0)
+    for c in range(1, count):
+        after = rise(c)
+        fall(c - 1, before)
+        before = after
+    fall(count - 1, before)
+    half = total.shape[0] // 2
+    core = place[1]
+    mine = pl.ds(pl.multiple_of(core * half, 8), half)
+    keep[...] = total[mine, :]
+    kept_residual[...] = residual[mine, :].astype(bf16)
+    give[...] = total[pl.ds(pl.multiple_of((1 - core) * half, 8), half), :].astype(bf16)
+
+
+def feed_forward(place, stream, heads_out, gain, gates, downs):
+    lines, width = stream.shape
+    units = downs.shape[0]
+    chunk = max(c for c in range(16, 256, 16) if units % c == 0)
+    vmem = pl.BlockSpec(memory_space=pltpu.VMEM)
+    return pl.pallas_call(
+        functools.partial(mlp_kernel, chunk),
+        out_shape=(
+            jax.ShapeDtypeStruct((lines // 2, width), f32),
+            jax.ShapeDtypeStruct((lines // 2, width), bf16),
+            jax.ShapeDtypeStruct((lines // 2, width), bf16),
+        ),
+        in_specs=[pl.BlockSpec(memory_space=pltpu.SMEM)] + [vmem] * 5,
+        out_specs=(vmem, vmem, vmem),
+        scratch_shapes=[pltpu.VMEM((lines, width), f32), pltpu.VMEM((lines, width), f32)],
+        compiler_params=pltpu.CompilerParams(vmem_limit_bytes=12 * 1024 * 1024),
+        name="feed_forward",
+    )(place, stream, heads_out, gain.reshape(1, width), gates, downs)
 
 
 def body(
@@ -430,19 +543,22 @@
 
     stream = tokens.reshape(lines, width)
     partner_weight = swap(qkv_weight, "dp", n_dp, 1)
-    own_normed = rms_norm(stream, attn_gain).astype(bf16)
-    my_half = jnp.where(core == 0, own_normed[:half], own_normed[half:])
     far = list(range(2, n_dp, 2))
-    far_halves = [swap(my_half, "dp", n_dp, k) for k in far]
+    quarter_lines = lines // 4
+    quarter_index = seq_index % 4
+    my_quarter = lax.dynamic_slice_in_dim(stream, quarter_index * quarter_lines, quarter_lines)
+    far_parts = jnp.concatenate([swap(my_quarter, "dp", n_dp, k) for k in far], axis=0)
+    far_pairs = [far_parts, swap(far_parts, "seq", n_seq, 2)]
+    far_mine = jnp.concatenate(far_pairs, axis=0)
+    far_other = swap(far_mine, "seq", n_seq, 1)
     held_pool = pltpu.with_memory_space_constraint(kv_pool, pltpu.HBM)
-    pool_copy = copy_pool(held_pool)
-    far_half = jnp.concatenate(far_halves, axis=0)
-    far_other = swap(far_half, "seq", n_seq, 1)
-    groups = [own_normed]
+    groups = [stream]
+    stride = len(far) * quarter_lines
     for i in range(len(far)):
-        groups += [far_half[i * half : (i + 1) * half], far_other[i * half : (i + 1) * half]]
-    partner_weight, pool_copy = lax.optimization_barrier((partner_weight, pool_copy))
-    normed = jnp.concatenate(groups, axis=0)
+        for source in (far_mine, far_other):
+            for start in (i * quarter_lines, stride + i * quarter_lines):
+                groups.append(source[start : start + quarter_lines])
+    normed = rms_norm(jnp.concatenate(groups, axis=0), attn_gain).astype(bf16)
     by_mine = lax.dot_general(normed, qkv_weight, contract, preferred_element_type=f32)
     by_partner = lax.dot_general(normed, partner_weight, contract, preferred_element_type=f32)
     products = jnp.where(
@@ -450,14 +566,23 @@
         jnp.concatenate([by_mine, by_partner], axis=1),
         jnp.concatenate([by_partner, by_mine], axis=1),
     ).astype(bf16)
-    out_mine, far_half = lax.optimization_barrier((out_weight, far_half))
+    blocks = [products[:lines]]
+    for i, k in enumerate(far):
+        back = swap(products[(i + 1) * lines : (i + 2) * lines], "dp", n_dp, k)
+        pieces = {
+            m: back[n * quarter_lines : (n + 1) * quarter_lines] for n, m in enumerate((0, 2, 1, 3))
+        }
+        natural = []
+        for j in range(4):
+            piece = pieces[0]
+            for m in (1, 2, 3):
+                piece = jnp.where((quarter_index ^ m) == j, pieces[m], piece)
+            natural.append(piece)
+        blocks.append(jnp.concatenate(natural, axis=0))
+    out_mine, blocks = lax.optimization_barrier((out_weight, blocks))
     out_blocks = {0: out_mine, 1: swap(out_mine, "dp", n_dp, 1)}
     for k in far:
         out_blocks[k] = swap(out_mine, "dp", n_dp, k)
-    blocks = [products[:lines]]
-    for i, k in enumerate(far):
-        back = swap(products[(i + 1) * lines : (i + 2) * lines], "dp", n_dp, k)
-        blocks.append(ordered(back[:half], back[half:]))
     pair = dp_index // 2
     columns = []
     for j in range(n_dp // 2):
@@ -505,18 +630,11 @@
     )
 
     dims = (requests, new_count, heads, pages, page_len, window, min(16, pages), n_seq)
-    mine, theirs, written_pool = attention(
-        dims,
-        slots,
-        patches,
-        cache_len,
-        jnp.stack([seq_index, core]),
-        cosine,
-        sine,
-        projected,
-        held_pool,
-        pool_copy,
-    )
+    place, slots, patches, lengths = lax.optimization_barrier(
+        (jnp.stack([seq_index, core, dp_index]), slots, patches, cache_len)
+    )
+    mine, theirs, fresh = attention(dims, slots, place, cosine, sine, projected, held_pool)
+    written_pool = write_pool(dims, patches, lengths, fresh, held_pool)
 
     side = requests // 2
     merged = merge_pair(mine, swap(theirs, "seq", n_seq, 1), side, rows)
@@ -526,37 +644,25 @@
     for k in far:
         out_blocks[k ^ 1] = swap(out_blocks[k], "dp", n_dp, 1)
     packs = [merged] + [swap(merged, "seq", n_seq, 2 * c) for c in range(1, chips)]
+    gates, downs, token = fetch_weights(gate_up, down_weight, merged)
     packs, late = lax.optimization_barrier((packs, [out_blocks[k ^ 1] for k in far]))
     for k, block in zip(far, late):
         out_blocks[k ^ 1] = block
-    attended_half = merge_final(packs, side, rows, heads)
-    attended = ordered(attended_half, swap(attended_half, "seq", n_seq, 1))
-
-    by_block = [
-        lax.dot_general(attended, out_blocks[k], contract, preferred_element_type=f32).astype(bf16)
-        for k in range(n_dp)
-    ]
-    heads_part = []
-    for j in range(n_dp):
-        block = by_block[0]
-        for k in range(1, n_dp):
-            block = jnp.where((dp_index ^ k) == j, by_block[k], block)
-        heads_part.append(block)
-    heads_part = jnp.concatenate(heads_part, axis=1)
-    heads_out = lax.all_gather(heads_part, "seq", axis=1, tiled=True)
-    residual = (stream.astype(f32) + heads_out.astype(f32)).astype(bf16)
-    hidden_in = rms_norm(residual, mlp_gain).astype(bf16)
-    hidden_in = lax.optimization_barrier(hidden_in)
-    gate_and_up = jnp.einsum("rd,gfd->grf", hidden_in, gate_up, preferred_element_type=f32)
-    hidden = (jax.nn.gelu(gate_and_up[0], approximate=True) * gate_and_up[1]).astype(bf16)
-    partial_sum = jnp.dot(hidden, down_weight, preferred_element_type=f32)
-
-    keep = jnp.where(core == 0, partial_sum[:half], partial_sum[half:])
-    give = jnp.where(core == 0, partial_sum[half:], partial_sum[:half]).astype(bf16)
+    attended_half = merge_final(packs, token, side, rows, heads)
+    heads_part = project_out(
+        place,
+        attended_half,
+        swap(attended_half, "seq", n_seq, 1),
+        [out_blocks[k] for k in range(n_dp)],
+    )
+    heads_out = lax.all_gather(heads_part, "seq", axis=0)
+    keep, give, my_residual = feed_forward(
+        place, stream, heads_out, mlp_gain, gates, downs
+    )
     chip_sum = (keep + swap(give, "seq", n_seq, 1).astype(f32)).astype(bf16)
     terms = [chip_sum] + [swap(chip_sum, "seq", n_seq, 2 * c) for c in range(1, chips)]
+    terms, written_pool = lax.optimization_barrier((terms, written_pool))
     full_half = tree_sum([term.astype(f32) for term in terms])
-    my_residual = jnp.where(core == 0, residual[:half], residual[half:])
     out_half = (my_residual.astype(f32) + full_half).astype(bf16)
     layer_out = ordered(out_half, swap(out_half, "seq", n_seq, 1))
     return layer_out.reshape(requests, new_count, width), written_pool

time: 105 us -> 89.7 us (0.85)
  matrix products: 12.5 us -> 0.78 us
  waiting for transfers between devices: 24.3 us -> 16.2 us
  Pallas kernels: 17.4 us -> 24.9 us
  local copies, waits for them, and re-layouts: 4.85 us -> 2.39 us
  other arithmetic: 7.23 us -> 4.88 us
  blocking collectives: 18.3 us -> 19.5 us
    dot_general x6 -> x0, matrix products: 11.9 us -> none  [the longest x1 6.88 us: body(): jnp.einsum('rd,gfd->grf', hidden_in, gate_up, preferred_element_type=f32)]
    pallas_call x2 -> x5, Pallas kernels: 13.3 us -> 24.3 us  [the longest x1 7.49 us: write_pool(): pl.pallas_call(functools.partial(write_kernel, dims, parts), out_shape=pl...]
    ppermute x17 -> x18, waiting for transfers between devices: 24.3 us -> 16.2 us  [swap(): return lax.ppermute(values, axis, [(i, i ^ mask) for i in range(size)])]
    unnamed x24 -> x10, local copies, waits for them, and re-layouts: 2.08 us -> 0.03 us
    pallas_call x1, Pallas kernels: 2.22 us -> 0.38 us  [merge_final(): pl.pallas_call(functools.partial(final_kernel, len(packs), requests, rows...]
    pallas_call x1, Pallas kernels: 1.93 us -> 0.26 us  [merge_pair(): pl.pallas_call(functools.partial(pair_kernel, requests, rows), out_shape=...]
    convert_element_type x3 -> x0, local copies, waits for them, and re-layouts: 1.44 us -> none  [body(): residual = (stream.astype(f32) + heads_out.astype(f32)).astype(bf16)]
    all_gather x1, blocking collectives: 8.39 us -> 9.63 us  [body(): heads_out = lax.all_gather(heads_part, 'seq', axis=0)]
  transfers between devices with their start and end apart: 17 -> 18, of which waited for: 11 -> 10; matrix products, arithmetic and copies ran while one was open for 5% -> 6% of each run, Pallas kernels for 15% -> 21%
where the time goes in v3:
time: 89.7 us; the launch traced here: 89.5 us
  Pallas kernels  24.9 us (28%)
  starting transfers between devices  19.7 us (22%)
  blocking collectives  19.5 us (22%)
  waiting for transfers between devices  16.2 us (18%)
  other arithmetic  4.88 us (5%)
  local copies, waits for them, and re-layouts  2.39 us (3%)
  between operations  1.03 us (1%)
    ppermute x18, starting transfers between devices, swap(): return lax.ppermute(values, axis, [(i, i ^ mask) for i in range(size)])  19.7 us
    ppermute x18, waiting for transfers between devices, swap(): return lax.ppermute(values, axis, [(i, i ^ mask) for i in range(size)])  16.2 us
    all_gather x1, blocking collectives, body(): lax.all_gather(jnp.concatenate(columns, axis=1), 'seq', axis=1, tiled=True)  9.85 us
    all_gather x1, blocking collectives, body(): heads_out = lax.all_gather(heads_part, 'seq', axis=0)  9.63 us
    pallas_call x1, Pallas kernels, write_pool(): pl.pallas_call(functools.partial(write_kernel, dims, parts), out_shape=pl...  7.49 us
    pallas_call x1, Pallas kernels, attention(): pl.pallas_call(functools.partial(attention_kernel, dims), out_shape=(pack...  5.55 us
    pallas_call x1, Pallas kernels, fetch_weights(): pl.pallas_call(functools.partial(fetch_kernel, parts), out_shape=(jax.Sha...  5.33 us
    pallas_call x1, Pallas kernels, feed_forward(): pl.pallas_call(functools.partial(mlp_kernel, chunk), out_shape=(jax.Shape...  4.74 us
  transfers between devices with their start and end apart: 18, of which 10 were waited for; matrix products, arithmetic and copies ran while one was open for 6% of the time, Pallas kernels for 21%

profile of v3, /device:TPU:0, one launch (start us, length us, event | category | flops | bytes accessed | tf_op | source)
XLA Modules:
  0.0 89.5 jit_solution(17950966093618062967)
XLA Ops:
  0.7 1.1 %reshape.314.stream = bf16[64,2560]{1,0:T(8,128)(2,1)S(1)} reshape(bf16[16,4,2560]{2,1,0:T(4,128)(2,1)} %param.10) | data formatting | bytes 655360 | tf_op jit(solution)/shard_map/reshape | solution.py:544
  1.8 4.1 %collective-permute-start = (bf16[16,2560]{1,0:T(8,128)(2,1)S(1)}, bf16[16,2560]{1,0:T(8,128)(2,1)S(1)}, u32[]{:S(2)}, u32[]{:S(2)}) collective-permute-start(bf16[16,2560]{1,0:T(8,128)(2,1)S(1)} %constant_dynamic-slice_fusion), channel_id=1, source_target_pairs={{0,16},{8,24},{16,0},{24,8},{1,17},{9,25},{17,1},{25,9},{2,18},{10... | collective-permute-start | bytes 245768 | tf_op jit(solution)/shard_map/ppermute | solution.py:23
  5.9 1.6 %collective-permute-start.3 = (bf16[96,2560]{1,0:T(8,128)(2,1)}, bf16[96,2560]{1,0:T(8,128)(2,1)S(1)}, u32[]{:S(2)}, u32[]{:S(2)}) collective-permute-start(bf16[96,2560]{1,0:T(8,128)(2,1)} %param.12), channel_id=1, source_target_pairs={{0,8},{8,0},{16,24},{24,16},{1,9},{9,1},{17,25},{25,17},{2,10},{10... | collective-permute-start | bytes 1474568 | tf_op jit(solution)/shard_map/ppermute | solution.py:23
  12.0 1.6 %collective-permute-start.1 = (bf16[16,2560]{1,0:T(8,128)(2,1)S(1)}, bf16[16,2560]{1,0:T(8,128)(2,1)S(1)}, u32[]{:S(2)}, u32[]{:S(2)}) collective-permute-start(bf16[16,2560]{1,0:T(8,128)(2,1)S(1)} %collective-permute-done), channel_id=1, source_target_pairs={{0,2},{1,3},{2,0},{3,1},{4,6},{5,7},{6,4},{7,5},{8,10},{9,11},{10,... | collective-permute-start | bytes 245768 | tf_op jit(solution)/shard_map/ppermute | solution.py:23
  13.6 2.9 %collective-permute-done.1 = bf16[16,2560]{1,0:T(8,128)(2,1)S(1)} collective-permute-done((bf16[16,2560]{1,0:T(8,128)(2,1)S(1)}, bf16[16,2560]{1,0:T(8,128)(2,1)S(1)}, u32[]{:S(2)}, u32[]{:S(2)}) %collective-permute-start.1) | collective-permute-done | bytes 81952 | tf_op jit(solution)/shard_map/ppermute | solution.py:23
  16.7 1.2 %collective-permute-done.2 = bf16[32,2560]{1,0:T(8,128)(2,1)S(1)} collective-permute-done((bf16[32,2560]{1,0:T(8,128)(2,1)S(1)}, bf16[32,2560]{1,0:T(8,128)(2,1)S(1)}, u32[]{:S(2)}, u32[]{:S(2)}) %collective-permute-start.2) | collective-permute-done | bytes 163872 | tf_op jit(solution)/shard_map/ppermute | solution.py:23
  19.9 1.2 %collective-permute-start.4 = (bf16[64,192]{1,0:T(8,128)(2,1)S(1)}, bf16[64,192]{1,0:T(8,128)(2,1)S(1)}, u32[]{:S(2)}, u32[]{:S(2)}) collective-permute-start(bf16[64,192]{1,0:T(8,128)(2,1)S(1)} %get-tuple-element.65), channel_id=1, source_target_pairs={{0,16},{8,24},{16,0},{24,8},{1,17},{9,25},{17,1},{25,9},{2,18},{10... | collective-permute-start | bytes 73736 | tf_op jit(solution)/shard_map/ppermute | solution.py:23
  21.2 3.6 %collective-permute-done.4 = bf16[64,192]{1,0:T(8,128)(2,1)S(1)} collective-permute-done((bf16[64,192]{1,0:T(8,128)(2,1)S(1)}, bf16[64,192]{1,0:T(8,128)(2,1)S(1)}, u32[]{:S(2)}, u32[]{:S(2)}) %collective-permute-start.4) | collective-permute-done | bytes 24608 | tf_op jit(solution)/shard_map/ppermute | solution.py:23
  24.9 1.5 %collective-permute-start.6 = (bf16[80,2560]{1,0:T(8,128)(2,1)S(1)}, bf16[80,2560]{1,0:T(8,128)(2,1)S(1)}, u32[]{:S(2)}, u32[]{:S(2)}) collective-permute-start(bf16[80,2560]{1,0:T(8,128)(2,1)S(1)} %copy-done), channel_id=1, source_target_pairs={{0,8},{8,0},{16,24},{24,16},{1,9},{9,1},{17,25},{25,17},{2,10},{10... | collective-permute-start | bytes 1228808 | tf_op jit(solution)/shard_map/ppermute | solution.py:23
  26.4 1.6 %collective-permute-start.7 = (bf16[80,2560]{1,0:T(8,128)(2,1)S(1)}, bf16[80,2560]{1,0:T(8,128)(2,1)S(1)}, u32[]{:S(2)}, u32[]{:S(2)}) collective-permute-start(bf16[80,2560]{1,0:T(8,128)(2,1)S(1)} %copy-done), channel_id=1, source_target_pairs={{0,16},{8,24},{16,0},{24,8},{1,17},{9,25},{17,1},{25,9},{2,18},{10... | collective-permute-start | bytes 1228808 | tf_op jit(solution)/shard_map/ppermute | solution.py:23
  28.1 9.8 %all_gather.9.projected = bf16[64,3072]{1,0:T(8,128)(2,1)S(1)} all-gather(bf16[64,384]{1,0:T(8,128)(2,1)S(1)} %pad_maximum_fusion.2), channel_id=1, replica_groups=mesh['dp'=4,'seq'=8] {'seq'}, dimensions={1}, use_global_device_ids=true | all-gather | bytes 442368 | tf_op jit(solution)/shard_map/all_gather | solution.py:593
  38.0 5.6 %page_attention.1 = (bf16[336,256]{1,0:T(8,128)(2,1)S(1)}, bf16[336,256]{1,0:T(8,128)(2,1)S(1)}, bf16[64,512]{1,0:T(8,128)(2,1)S(1)}) custom-call(s32[3,64]{1,0:T(4,128)S(1)} %pad_add_fusion.slots, s32[3]{0:T(128)S(1)} %pad_add_fusion.3.place, f32[64,128]{1,0:T(8,128)S(1)} %get-tuple-element.79.cosine, f32[64,128]{1,0:T(8,128)S(1)} %get-tuple-element.80.sine, ...), custom_call_target="tpu_custom_call" | custom-call | flops 335544320 | bytes 8388608 | tf_op jit(solution)/shard_map/page_attention/pallas_call | solution.py:346
  43.9 1.1 %collective-permute-done.5.other = bf16[336,256]{1,0:T(8,128)(2,1)S(1)} collective-permute-done((bf16[336,256]{1,0:T(8,128)(2,1)S(1)}, bf16[336,256]{1,0:T(8,128)(2,1)S(1)}, u32[]{:S(2)}, u32[]{:S(2)}) %collective-permute-start.5) | collective-permute-done | bytes 172064 | tf_op jit(solution)/shard_map/ppermute | solution.py:23
  45.4 2.3 %collective-permute-start.10 = (bf16[336,256]{1,0:T(8,128)(2,1)S(1)}, bf16[336,256]{1,0:T(8,128)(2,1)S(1)}, u32[]{:S(2)}, u32[]{:S(2)}) collective-permute-start(bf16[336,256]{1,0:T(8,128)(2,1)S(1)} %merge_pair.1.after.refs_0_), channel_id=1, source_target_pairs={{0,6},{1,7},{2,4},{3,5},{4,2},{5,3},{6,0},{7,1},{8,14},{9,15},{10,... | collective-permute-start | bytes 516104 | tf_op jit(solution)/shard_map/ppermute | solution.py:23
  48.9 5.3 %fetch_weights.1 = (bf16[2,960,2560]{2,1,0:T(8,128)(2,1)S(1)}, bf16[960,2560]{1,0:T(8,128)(2,1)S(1)}, f32[8,128]{1,0:T(8,128)S(1)}) custom-call(bf16[2,960,2560]{2,1,0:T(8,128)(2,1)} %gate_up.1, bf16[960,2560]{1,0:T(8,128)(2,1)} %down.1, bf16[336,256]{1,0:T(8,128)(2,1)S(1)} %merge_pair.1.after.refs_0_), custom_call_target="tpu_custom_call" | custom-call | bytes 14745600 | tf_op jit(solution)/shard_map/fetch_weights/pallas_call | solution.py:423
  54.3 2.4 %collective-permute-done.8.refs_1_ = bf16[336,256]{1,0:T(8,128)(2,1)S(1)} collective-permute-done((bf16[336,256]{1,0:T(8,128)(2,1)S(1)}, bf16[336,256]{1,0:T(8,128)(2,1)S(1)}, u32[]{:S(2)}, u32[]{:S(2)}) %collective-permute-start.8) | collective-permute-done | bytes 172064 | tf_op jit(solution)/shard_map/ppermute | solution.py:23
  57.5 1.4 %collective-permute-done.12.other = bf16[32,2560]{1,0:T(8,128)(2,1)S(1)} collective-permute-done((bf16[32,2560]{1,0:T(8,128)(2,1)S(1)}, bf16[32,2560]{1,0:T(8,128)(2,1)S(1)}, u32[]{:S(2)}, u32[]{:S(2)}) %collective-permute-start.12) | collective-permute-done | bytes 163872 | tf_op jit(solution)/shard_map/ppermute | solution.py:23
  58.8 1.2 %project_out.1 = bf16[64,320]{1,0:T(8,128)(2,1)S(1)} custom-call(s32[3]{0:T(128)S(1)} %pad_add_fusion.3.place, bf16[32,2560]{1,0:T(8,128)(2,1)S(1)} %merge_final.1.mine, bf16[32,2560]{1,0:T(8,128)(2,1)S(1)} %collective-permute-done.12.other, bf16[80,2560]{1,0:T(8,128)(2,1)S(1)} %copy-done, bf16[80,2560]{1,0:T(8,128)(2,1)S(1)} %collective-permute-done.6.refs_1_, ...), custom_call_target="tpu_custom_call" | custom-call | tf_op jit(solution)/shard_map/project_out/pallas_call | solution.py:393
  60.0 9.6 %all-gather = bf16[512,320]{1,0:T(8,128)(2,1)S(1)} all-gather(bf16[64,320]{1,0:T(8,128)(2,1)S(1)} %project_out.1), channel_id=2, replica_groups=mesh['dp'=4,'seq'=8] {'seq'}, dimensions={0}, use_global_device_ids=true | all-gather | bytes 368640 | tf_op jit(solution)/shard_map/all_gather | solution.py:658
  69.7 4.7 %feed_forward.1 = (f32[32,2560]{1,0:T(8,128)S(1)}, bf16[32,2560]{1,0:T(8,128)(2,1)S(1)}, bf16[32,2560]{1,0:T(8,128)(2,1)S(1)}) custom-call(s32[3]{0:T(128)S(1)} %pad_add_fusion.3.place, bf16[64,2560]{1,0:T(8,128)(2,1)S(1)} %reshape.314.stream, bf16[8,64,320]{2,1,0:T(8,128)(2,1)S(1)} %bitcast.12, f32[1,2560]{1,0:T(1,128)S(1)} %reshape.315.gain, ...), custom_call_target="tpu_custom_call" | custom-call | tf_op jit(solution)/shard_map/feed_forward/pallas_call | solution.py:494
  76.5 1.5 %collective-permute-start.15 = (bf16[32,2560]{1,0:T(8,128)(2,1)S(1)}, bf16[32,2560]{1,0:T(8,128)(2,1)S(1)}, u32[]{:S(2)}, u32[]{:S(2)}) collective-permute-start(bf16[32,2560]{1,0:T(8,128)(2,1)S(1)} %add_convert_fusion.1), channel_id=1, source_target_pairs={{0,4},{1,5},{2,6},{3,7},{4,0},{5,1},{6,2},{7,3},{8,12},{9,13},{10,... | collective-permute-start | bytes 491528 | tf_op jit(solution)/shard_map/ppermute | solution.py:23
  78.0 1.4 %collective-permute-start.16 = (bf16[32,2560]{1,0:T(8,128)(2,1)S(1)}, bf16[32,2560]{1,0:T(8,128)(2,1)S(1)}, u32[]{:S(2)}, u32[]{:S(2)}) collective-permute-start(bf16[32,2560]{1,0:T(8,128)(2,1)S(1)} %add_convert_fusion.1), channel_id=1, source_target_pairs={{0,6},{1,7},{2,4},{3,5},{4,2},{5,3},{6,0},{7,1},{8,14},{9,15},{10,... | collective-permute-start | bytes 491528 | tf_op jit(solution)/shard_map/ppermute | solution.py:23
  79.5 7.5 %write_pool.1 = bf16[64,128,512]{2,1,0:T(8,128)(2,1)} custom-call(s32[3,32]{1,0:T(4,128)S(1)} %pad_add_fusion.1.patches, s32[16]{0:T(128)S(1)} %copy-done.1, bf16[64,512]{1,0:T(8,128)(2,1)S(1)} %get-tuple-element.54.fresh, bf16[64,128,512]{2,1,0:T(8,128)(2,1)} %source.1), custom_call_target="tpu_custom_call" | custom-call | bytes 16777216 | tf_op jit(solution)/shard_map/write_pool/pallas_call | solution.py:84
  87.2 1.4 %collective-permute-done.17 = bf16[32,2560]{1,0:T(8,128)(2,1)S(1)} collective-permute-done((bf16[32,2560]{1,0:T(8,128)(2,1)S(1)}, bf16[32,2560]{1,0:T(8,128)(2,1)S(1)}, u32[]{:S(2)}, u32[]{:S(2)}) %collective-permute-start.17) | collective-permute-done | bytes 163872 | tf_op jit(solution)/shard_map/ppermute | solution.py:23
  (70 shorter events, 12.6 us)
Async XLA Ops:
  0.6 17.6 %copy-start.3 = (bf16[96,2560]{1,0:T(8,128)(2,1)S(1)}, bf16[96,2560]{1,0:T(8,128)(2,1)}, u32[]{:S(2)}) copy-start(bf16[96,2560]{1,0:T(8,128)(2,1)} %param.12) | copy-start | bytes 1474564
  0.6 17.6 %copy-start.4 = (f32[2560]{0:T(1024)S(1)}, f32[2560]{0:T(1024)}, u32[]{:S(2)}) copy-start(f32[2560]{0:T(1024)} %param.11) | copy-start | bytes 30724
  1.8 10.2 %collective-permute-start = (bf16[16,2560]{1,0:T(8,128)(2,1)S(1)}, bf16[16,2560]{1,0:T(8,128)(2,1)S(1)}, u32[]{:S(2)}, u32[]{:S(2)}) collective-permute-start(bf16[16,2560]{1,0:T(8,128)(2,1)S(1)} %constant_dynamic-slice_fusion), channel_id=1, source_target_pairs={{0,16},{8,24},{16,0},{24,8},{1,17},{9,25},{17,1},{25,9},{2,18},{10... | collective-permute-start | bytes 245768 | tf_op jit(solution)/shard_map/ppermute | solution.py:23
  5.9 13.5 %collective-permute-start.3 = (bf16[96,2560]{1,0:T(8,128)(2,1)}, bf16[96,2560]{1,0:T(8,128)(2,1)S(1)}, u32[]{:S(2)}, u32[]{:S(2)}) collective-permute-start(bf16[96,2560]{1,0:T(8,128)(2,1)} %param.12), channel_id=1, source_target_pairs={{0,8},{8,0},{16,24},{24,16},{1,9},{9,1},{17,25},{25,17},{2,10},{10... | collective-permute-start | bytes 1474568 | tf_op jit(solution)/shard_map/ppermute | solution.py:23
  12.0 4.5 %collective-permute-start.1 = (bf16[16,2560]{1,0:T(8,128)(2,1)S(1)}, bf16[16,2560]{1,0:T(8,128)(2,1)S(1)}, u32[]{:S(2)}, u32[]{:S(2)}) collective-permute-start(bf16[16,2560]{1,0:T(8,128)(2,1)S(1)} %collective-permute-done), channel_id=1, source_target_pairs={{0,2},{1,3},{2,0},{3,1},{4,6},{5,7},{6,4},{7,5},{8,10},{9,11},{10,... | collective-permute-start | bytes 245768 | tf_op jit(solution)/shard_map/ppermute | solution.py:23
  16.5 1.5 %collective-permute-start.2 = (bf16[32,2560]{1,0:T(8,128)(2,1)S(1)}, bf16[32,2560]{1,0:T(8,128)(2,1)S(1)}, u32[]{:S(2)}, u32[]{:S(2)}) collective-permute-start(bf16[32,2560]{1,0:T(8,128)(2,1)S(1)} %pad_maximum_fusion.1), channel_id=1, source_target_pairs={{0,1},{1,0},{2,3},{3,2},{4,5},{5,4},{6,7},{7,6},{8,9},{9,8},{10,11... | collective-permute-start | bytes 491528 | tf_op jit(solution)/shard_map/ppermute | solution.py:23
  18.6 6.2 %copy-start = (bf16[80,2560]{1,0:T(8,128)(2,1)S(1)}, bf16[80,2560]{1,0:T(8,128)(2,1)}, u32[]{:S(2)}) copy-start(bf16[80,2560]{1,0:T(8,128)(2,1)} %refs_0_) | copy-start | bytes 1228804
  19.9 4.9 %collective-permute-start.4 = (bf16[64,192]{1,0:T(8,128)(2,1)S(1)}, bf16[64,192]{1,0:T(8,128)(2,1)S(1)}, u32[]{:S(2)}, u32[]{:S(2)}) collective-permute-start(bf16[64,192]{1,0:T(8,128)(2,1)S(1)} %get-tuple-element.65), channel_id=1, source_target_pairs={{0,16},{8,24},{16,0},{24,8},{1,17},{9,25},{17,1},{25,9},{2,18},{10... | collective-permute-start | bytes 73736 | tf_op jit(solution)/shard_map/ppermute | solution.py:23
  24.9 20.4 %collective-permute-start.6 = (bf16[80,2560]{1,0:T(8,128)(2,1)S(1)}, bf16[80,2560]{1,0:T(8,128)(2,1)S(1)}, u32[]{:S(2)}, u32[]{:S(2)}) collective-permute-start(bf16[80,2560]{1,0:T(8,128)(2,1)S(1)} %copy-done), channel_id=1, source_target_pairs={{0,8},{8,0},{16,24},{24,16},{1,9},{9,1},{17,25},{25,17},{2,10},{10... | collective-permute-start | bytes 1228808 | tf_op jit(solution)/shard_map/ppermute | solution.py:23
  26.4 18.9 %collective-permute-start.7 = (bf16[80,2560]{1,0:T(8,128)(2,1)S(1)}, bf16[80,2560]{1,0:T(8,128)(2,1)S(1)}, u32[]{:S(2)}, u32[]{:S(2)}) collective-permute-start(bf16[80,2560]{1,0:T(8,128)(2,1)S(1)} %copy-done), channel_id=1, source_target_pairs={{0,16},{8,24},{16,0},{24,8},{1,17},{9,25},{17,1},{25,9},{2,18},{10... | collective-permute-start | bytes 1228808 | tf_op jit(solution)/shard_map/ppermute | solution.py:23
  43.5 1.5 %collective-permute-start.5 = (bf16[336,256]{1,0:T(8,128)(2,1)S(1)}, bf16[336,256]{1,0:T(8,128)(2,1)S(1)}, u32[]{:S(2)}, u32[]{:S(2)}) collective-permute-start(bf16[336,256]{1,0:T(8,128)(2,1)S(1)} %get-tuple-element.36), channel_id=1, source_target_pairs={{0,1},{1,0},{2,3},{3,2},{4,5},{5,4},{6,7},{7,6},{8,9},{9,8},{10,11... | collective-permute-start | bytes 516104 | tf_op jit(solution)/shard_map/ppermute | solution.py:23
  45.2 12.2 %copy-start.2 = (f32[2560]{0:T(1024)S(1)}, f32[2560]{0:T(1024)}, u32[]{:S(2)}) copy-start(f32[2560]{0:T(1024)} %param.14) | copy-start | bytes 30724
  45.3 11.7 %collective-permute-start.11 = (bf16[80,2560]{1,0:T(8,128)(2,1)S(1)}, bf16[80,2560]{1,0:T(8,128)(2,1)S(1)}, u32[]{:S(2)}, u32[]{:S(2)}) collective-permute-start(bf16[80,2560]{1,0:T(8,128)(2,1)S(1)} %collective-permute-done.7.refs_2_), channel_id=1, source_target_pairs={{0,8},{8,0},{16,24},{24,16},{1,9},{9,1},{17,25},{25,17},{2,10},{10... | collective-permute-start | bytes 1228808 | tf_op jit(solution)/shard_map/ppermute | solution.py:23
  45.4 8.9 %collective-permute-start.10 = (bf16[336,256]{1,0:T(8,128)(2,1)S(1)}, bf16[336,256]{1,0:T(8,128)(2,1)S(1)}, u32[]{:S(2)}, u32[]{:S(2)}) collective-permute-start(bf16[336,256]{1,0:T(8,128)(2,1)S(1)} %merge_pair.1.after.refs_0_), channel_id=1, source_target_pairs={{0,6},{1,7},{2,4},{3,5},{4,2},{5,3},{6,0},{7,1},{8,14},{9,15},{10,... | collective-permute-start | bytes 516104 | tf_op jit(solution)/shard_map/ppermute | solution.py:23
  47.7 9.0 %collective-permute-start.8 = (bf16[336,256]{1,0:T(8,128)(2,1)S(1)}, bf16[336,256]{1,0:T(8,128)(2,1)S(1)}, u32[]{:S(2)}, u32[]{:S(2)}) collective-permute-start(bf16[336,256]{1,0:T(8,128)(2,1)S(1)} %merge_pair.1.after.refs_0_), channel_id=1, source_target_pairs={{0,2},{1,3},{2,0},{3,1},{4,6},{5,7},{6,4},{7,5},{8,10},{9,11},{10,... | collective-permute-start | bytes 516104 | tf_op jit(solution)/shard_map/ppermute | solution.py:23
  48.4 8.3 %collective-permute-start.9 = (bf16[336,256]{1,0:T(8,128)(2,1)S(1)}, bf16[336,256]{1,0:T(8,128)(2,1)S(1)}, u32[]{:S(2)}, u32[]{:S(2)}) collective-permute-start(bf16[336,256]{1,0:T(8,128)(2,1)S(1)} %merge_pair.1.after.refs_0_), channel_id=1, source_target_pairs={{0,4},{1,5},{2,6},{3,7},{4,0},{5,1},{6,2},{7,3},{8,12},{9,13},{10,... | collective-permute-start | bytes 516104 | tf_op jit(solution)/shard_map/ppermute | solution.py:23
  57.4 1.5 %collective-permute-start.12 = (bf16[32,2560]{1,0:T(8,128)(2,1)S(1)}, bf16[32,2560]{1,0:T(8,128)(2,1)S(1)}, u32[]{:S(2)}, u32[]{:S(2)}) collective-permute-start(bf16[32,2560]{1,0:T(8,128)(2,1)S(1)} %merge_final.1.mine), channel_id=1, source_target_pairs={{0,1},{1,0},{2,3},{3,2},{4,5},{5,4},{6,7},{7,6},{8,9},{9,8},{10,11... | collective-permute-start | bytes 491528 | tf_op jit(solution)/shard_map/ppermute | solution.py:23
  69.7 9.8 %copy-start.1 = (s32[16]{0:T(128)S(1)}, s32[16]{0:T(128)}, u32[]{:S(2)}) copy-start(s32[16]{0:T(128)} %lengths) | copy-start | bytes 196
  74.4 1.5 %collective-permute-start.13 = (bf16[32,2560]{1,0:T(8,128)(2,1)S(1)}, bf16[32,2560]{1,0:T(8,128)(2,1)S(1)}, u32[]{:S(2)}, u32[]{:S(2)}) collective-permute-start(bf16[32,2560]{1,0:T(8,128)(2,1)S(1)} %get-tuple-element.51), channel_id=1, source_target_pairs={{0,1},{1,0},{2,3},{3,2},{4,5},{5,4},{6,7},{7,6},{8,9},{9,8},{10,11... | collective-permute-start | bytes 491528 | tf_op jit(solution)/shard_map/ppermute | solution.py:23
  75.9 11.1 %collective-permute-start.14 = (bf16[32,2560]{1,0:T(8,128)(2,1)S(1)}, bf16[32,2560]{1,0:T(8,128)(2,1)S(1)}, u32[]{:S(2)}, u32[]{:S(2)}) collective-permute-start(bf16[32,2560]{1,0:T(8,128)(2,1)S(1)} %add_convert_fusion.1), channel_id=1, source_target_pairs={{0,2},{1,3},{2,0},{3,1},{4,6},{5,7},{6,4},{7,5},{8,10},{9,11},{10,... | collective-permute-start | bytes 491528 | tf_op jit(solution)/shard_map/ppermute | solution.py:23
  76.5 10.5 %collective-permute-start.15 = (bf16[32,2560]{1,0:T(8,128)(2,1)S(1)}, bf16[32,2560]{1,0:T(8,128)(2,1)S(1)}, u32[]{:S(2)}, u32[]{:S(2)}) collective-permute-start(bf16[32,2560]{1,0:T(8,128)(2,1)S(1)} %add_convert_fusion.1), channel_id=1, source_target_pairs={{0,4},{1,5},{2,6},{3,7},{4,0},{5,1},{6,2},{7,3},{8,12},{9,13},{10,... | collective-permute-start | bytes 491528 | tf_op jit(solution)/shard_map/ppermute | solution.py:23
  78.0 9.0 %collective-permute-start.16 = (bf16[32,2560]{1,0:T(8,128)(2,1)S(1)}, bf16[32,2560]{1,0:T(8,128)(2,1)S(1)}, u32[]{:S(2)}, u32[]{:S(2)}) collective-permute-start(bf16[32,2560]{1,0:T(8,128)(2,1)S(1)} %add_convert_fusion.1), channel_id=1, source_target_pairs={{0,6},{1,7},{2,4},{3,5},{4,2},{5,3},{6,0},{7,1},{8,14},{9,15},{10,... | collective-permute-start | bytes 491528 | tf_op jit(solution)/shard_map/ppermute | solution.py:23
  87.1 1.5 %collective-permute-start.17 = (bf16[32,2560]{1,0:T(8,128)(2,1)S(1)}, bf16[32,2560]{1,0:T(8,128)(2,1)S(1)}, u32[]{:S(2)}, u32[]{:S(2)}) collective-permute-start(bf16[32,2560]{1,0:T(8,128)(2,1)S(1)} %add_convert_fusion), channel_id=1, source_target_pairs={{0,1},{1,0},{2,3},{3,2},{4,5},{5,4},{6,7},{7,6},{8,9},{9,8},{10,11... | collective-permute-start | bytes 491528 | tf_op jit(solution)/shard_map/ppermute | solution.py:23

commit v4 on v3

--- a/solution.py
+++ b/solution.py
@@ -27,6 +27,25 @@
     while len(terms) > 1:
         terms = [terms[i] + terms[i + 1] for i in range(0, len(terms), 2)]
     return terms[0]
+
+
+def gather_pieces(values, n_seq):
+    if n_seq > 8:
+        return [lax.all_gather(values, "seq", axis=0)]
+    pieces = {0: values}
+    for mask in range(2, n_seq, 2):
+        pieces[mask] = swap(values, "seq", n_seq, mask)
+    for mask in range(0, n_seq, 2):
+        pieces[mask + 1] = swap(pieces[mask], "seq", n_seq, 1)
+    return [pieces[mask] for mask in range(n_seq)]
+
+
+def place_pieces(me, refs, scratch):
+    if len(refs) == 1:
+        return refs[0]
+    for mask, ref in enumerate(refs):
+        scratch[jnp.bitwise_xor(me, mask)] = ref[...]
+    return scratch
 
 
 def write_kernel(dims, parts, patches, lengths, fresh, source, target, buffer, in_sems, out_sems):
@@ -202,27 +221,11 @@
     )(*packs, token)
 
 
-def attention_kernel(
-    dims,
-    slots,
-    place,
-    cosine,
-    sine,
-    projected,
-    pool,
-    mine,
-    theirs,
-    fresh,
-    buffer,
-    query_low,
-    query_high,
-    queries,
-    peak,
-    norm,
-    total,
-    in_sems,
-):
+def attention_kernel(dims, count, slots, place, cosine, sine, *refs):
     requests, new_count, heads, pages, page_len, window, chunk, n_seq = dims
+    pieces, refs = refs[:count], refs[count:]
+    pool, mine, theirs, fresh, buffer, gathered, projected = refs[:7]
+    query_low, query_high, queries, peak, norm, total, in_sems = refs[7:]
     rows = new_count * heads
     lines = requests * new_count
 
@@ -233,6 +236,10 @@
     for c in range(pages // chunk):
         load(c).start()
 
+    ordered_pieces = place_pieces(place[0], pieces, gathered)
+    part_columns = projected.shape[1] // n_seq
+    for i in range(n_seq):
+        projected[:, i * part_columns : (i + 1) * part_columns] = ordered_pieces[i]
     cos = cosine[...]
     sin = sine[...]
 
@@ -298,11 +305,17 @@
             top, amount, weights = weigh(score(r, fresh[:, 0:256]), seen)
             add(r, top, amount, mix(weights, fresh[:, 256:512]))
 
-    def one_chunk(c, carry):
+    def chunk_scores(c):
         load(c).wait()
-        numbers = [c * chunk + k for k in range(chunk)]
-        owners = [slots[0, page] for page in numbers]
-        scores = [score(r, buffer[page, :, 0:256]) for r, page in zip(owners, numbers)]
+        numbers = range(c * chunk, (c + 1) * chunk)
+        return [score(slots[0, page], buffer[page, :, 0:256]) for page in numbers]
+
+    ahead = chunk_scores(0)
+    for c in range(pages // chunk):
+        scores = ahead
+        if (c + 1) * chunk < pages:
+            ahead = chunk_scores(c + 1)
+        numbers = range(c * chunk, (c + 1) * chunk)
         weighed = []
         for page, values in zip(numbers, scores):
             length = slots[1, page]
@@ -314,11 +327,8 @@
             mix(weights, buffer[page, :, 256:512])
             for page, (top, amount, weights) in zip(numbers, weighed)
         ]
-        for r, (top, amount, weights), values in zip(owners, weighed, mixed):
-            add(r, top, amount, values)
-        return carry
-
-    lax.fori_loop(0, pages // chunk, one_chunk, 0)
+        for page, (top, amount, weights), values in zip(numbers, weighed, mixed):
+            add(slots[0, page], top, amount, values)
 
     half = requests // 2
     core = place[1]
@@ -337,19 +347,25 @@
         out[half * rows : half * rows + 16, :] = pack_logs(logs, rows).astype(bf16)
 
 
-def attention(dims, slots, place, cosine, sine, projected, pool):
+def attention(dims, slots, place, cosine, sine, pieces, pool):
     requests, new_count, heads, pages, page_len, window, chunk, n_seq = dims
+    part_columns = pieces[0].shape[-1]
+    lines = requests * new_count
     rows = new_count * heads
     smem = pl.BlockSpec(memory_space=pltpu.SMEM)
     vmem = pl.BlockSpec(memory_space=pltpu.VMEM)
     pack = jax.ShapeDtypeStruct((requests // 2 * rows + 16, 256), bf16)
     return pl.pallas_call(
-        functools.partial(attention_kernel, dims),
+        functools.partial(attention_kernel, dims, len(pieces)),
         out_shape=(pack, pack, jax.ShapeDtypeStruct((requests * new_count, 512), bf16)),
-        in_specs=[smem, smem, vmem, vmem, vmem, pl.BlockSpec(memory_space=pltpu.HBM)],
+        in_specs=[smem, smem, vmem, vmem]
+        + [vmem] * len(pieces)
+        + [pl.BlockSpec(memory_space=pltpu.HBM)],
         out_specs=(vmem, vmem, vmem),
         scratch_shapes=[
             pltpu.VMEM(pool.shape, bf16),
+            pltpu.VMEM((n_seq, lines, part_columns), bf16),
+            pltpu.VMEM((lines, n_seq * part_columns), bf16),
             pltpu.VMEM((requests * rows, 128), f32),
             pltpu.VMEM((requests * rows, 128), f32),
             pltpu.VMEM((requests, -(-rows // 16) * 16, 256), bf16),
@@ -359,13 +375,9 @@
             pltpu.SemaphoreType.DMA((pages // chunk,)),
         ],
         compiler_params=pltpu.CompilerParams(vmem_limit_bytes=20 * 1024 * 1024),
-        cost_estimate=pl.CostEstimate(
-            flops=4 * pages * rows * page_len * 256,
-            bytes_accessed=pool.size * 2,
-            transcendentals=pages * rows * page_len,
-        ),
+        cost_estimate=pl.CostEstimate(flops=0, bytes_accessed=1024, transcendentals=0),
         name="page_attention",
-    )(slots, place, cosine, sine, projected, pool)
+    )(slots, place, cosine, sine, *pieces, pool)
 
 
 def project_kernel(count, place, mine, other, *refs):
@@ -442,10 +454,11 @@
     )
 
 
-def mlp_kernel(
-    chunk, place, stream, heads_out, gain, gates, downs, keep, give, kept_residual, residual, total
-):
+def mlp_kernel(chunk, pieces, place, stream, gain, gates, downs, *refs):
+    heads_out, refs = refs[:pieces], refs[pieces:]
+    keep, give, kept_residual, residual, total, heads_scratch = refs
     units, width = downs.shape
+    heads_out = place_pieces(place[0], heads_out, heads_scratch)
     count = units // chunk
     gathered = jnp.concatenate(
         [heads_out[i].astype(f32) for i in range(heads_out.shape[0])], axis=1
@@ -486,24 +499,28 @@
     give[...] = total[pl.ds(pl.multiple_of((1 - core) * half, 8), half), :].astype(bf16)
 
 
-def feed_forward(place, stream, heads_out, gain, gates, downs):
+def feed_forward(n_seq, place, stream, heads_out, gain, gates, downs):
     lines, width = stream.shape
     units = downs.shape[0]
     chunk = max(c for c in range(16, 256, 16) if units % c == 0)
     vmem = pl.BlockSpec(memory_space=pltpu.VMEM)
     return pl.pallas_call(
-        functools.partial(mlp_kernel, chunk),
+        functools.partial(mlp_kernel, chunk, len(heads_out)),
         out_shape=(
             jax.ShapeDtypeStruct((lines // 2, width), f32),
             jax.ShapeDtypeStruct((lines // 2, width), bf16),
             jax.ShapeDtypeStruct((lines // 2, width), bf16),
         ),
-        in_specs=[pl.BlockSpec(memory_space=pltpu.SMEM)] + [vmem] * 5,
+        in_specs=[pl.BlockSpec(memory_space=pltpu.SMEM)] + [vmem] * (4 + len(heads_out)),
         out_specs=(vmem, vmem, vmem),
-        scratch_shapes=[pltpu.VMEM((lines, width), f32), pltpu.VMEM((lines, width), f32)],
+        scratch_shapes=[
+            pltpu.VMEM((lines, width), f32),
+            pltpu.VMEM((lines, width), f32),
+            pltpu.VMEM((n_seq, lines, width // n_seq), bf16),
+        ],
         compiler_params=pltpu.CompilerParams(vmem_limit_bytes=12 * 1024 * 1024),
         name="feed_forward",
-    )(place, stream, heads_out, gain.reshape(1, width), gates, downs)
+    )(place, stream, gain.reshape(1, width), gates, downs, *heads_out)
 
 
 def body(
@@ -548,6 +565,8 @@
     quarter_index = seq_index % 4
     my_quarter = lax.dynamic_slice_in_dim(stream, quarter_index * quarter_lines, quarter_lines)
     far_parts = jnp.concatenate([swap(my_quarter, "dp", n_dp, k) for k in far], axis=0)
+    out_first, far_parts = lax.optimization_barrier((out_weight, far_parts))
+    out_neighbour = swap(out_first, "dp", n_dp, 1)
     far_pairs = [far_parts, swap(far_parts, "seq", n_seq, 2)]
     far_mine = jnp.concatenate(far_pairs, axis=0)
     far_other = swap(far_mine, "seq", n_seq, 1)
@@ -566,6 +585,8 @@
         jnp.concatenate([by_mine, by_partner], axis=1),
         jnp.concatenate([by_partner, by_mine], axis=1),
     ).astype(bf16)
+    out_early, products = lax.optimization_barrier((out_weight, products))
+    out_blocks = {k: swap(out_early, "dp", n_dp, k) for k in far}
     blocks = [products[:lines]]
     for i, k in enumerate(far):
         back = swap(products[(i + 1) * lines : (i + 2) * lines], "dp", n_dp, k)
@@ -579,10 +600,6 @@
                 piece = jnp.where((quarter_index ^ m) == j, pieces[m], piece)
             natural.append(piece)
         blocks.append(jnp.concatenate(natural, axis=0))
-    out_mine, blocks = lax.optimization_barrier((out_weight, blocks))
-    out_blocks = {0: out_mine, 1: swap(out_mine, "dp", n_dp, 1)}
-    for k in far:
-        out_blocks[k] = swap(out_mine, "dp", n_dp, k)
     pair = dp_index // 2
     columns = []
     for j in range(n_dp // 2):
@@ -590,9 +607,9 @@
         for k in range(1, n_dp // 2):
             block = jnp.where((pair ^ k) == j, blocks[k], block)
         columns.append(block)
-    projected = lax.all_gather(
-        jnp.concatenate(columns, axis=1), "seq", axis=1, tiled=True
-    )
+    pieces = gather_pieces(jnp.concatenate(columns, axis=1), n_seq)
+    out_blocks[0] = out_weight
+    out_blocks[1] = out_neighbour
 
     positions_int = cache_len[:, None] + jnp.arange(new_count, dtype=jnp.int32)[None, :]
     quarter = head_dim // 4
@@ -633,7 +650,7 @@
     place, slots, patches, lengths = lax.optimization_barrier(
         (jnp.stack([seq_index, core, dp_index]), slots, patches, cache_len)
     )
-    mine, theirs, fresh = attention(dims, slots, place, cosine, sine, projected, held_pool)
+    mine, theirs, fresh = attention(dims, slots, place, cosine, sine, pieces, held_pool)
     written_pool = write_pool(dims, patches, lengths, fresh, held_pool)
 
     side = requests // 2
@@ -655,17 +672,17 @@
         swap(attended_half, "seq", n_seq, 1),
         [out_blocks[k] for k in range(n_dp)],
     )
-    heads_out = lax.all_gather(heads_part, "seq", axis=0)
+    heads_out = gather_pieces(heads_part, n_seq)
     keep, give, my_residual = feed_forward(
-        place, stream, heads_out, mlp_gain, gates, downs
+        n_seq, place, stream, heads_out, mlp_gain, gates, downs
     )
     chip_sum = (keep + swap(give, "seq", n_seq, 1).astype(f32)).astype(bf16)
     terms = [chip_sum] + [swap(chip_sum, "seq", n_seq, 2 * c) for c in range(1, chips)]
     terms, written_pool = lax.optimization_barrier((terms, written_pool))
     full_half = tree_sum([term.astype(f32) for term in terms])
     out_half = (my_residual.astype(f32) + full_half).astype(bf16)
-    layer_out = ordered(out_half, swap(out_half, "seq", n_seq, 1))
-    return layer_out.reshape(requests, new_count, width), written_pool
+    out_half = out_half.reshape(requests // 2, new_count, width)
+    return ordered(out_half, swap(out_half, "seq", n_seq, 1)), written_pool
 
 
 def solution(mesh):

time: 89.7 us -> 86.4 us (0.963)
  blocking collectives: 19.5 us -> 0 us
  waiting for transfers between devices: 16.2 us -> 24.1 us
  starting transfers between devices: 19.7 us -> 27.5 us
    all_gather x2 -> x0, blocking collectives: 19.5 us -> none  [the longest x1 9.85 us: body(): lax.all_gather(jnp.concatenate(columns, axis=1), 'seq', axis=1, tiled=True)]
    ppermute x18 -> x32, waiting for transfers between devices: 16.2 us -> 24.1 us  [swap(): return lax.ppermute(values, axis, [(i, i ^ mask) for i in range(size)])]
    ppermute x18 -> x32, starting transfers between devices: 19.7 us -> 27.5 us  [swap(): return lax.ppermute(values, axis, [(i, i ^ mask) for i in range(size)])]
    select_n x1, other arithmetic: 0.06 us -> 1.09 us  [ordered(): jnp.where(core == 0, jnp.concatenate([mine, other], axis=axis), jnp.conca...]
  transfers between devices with their start and end apart: 18 -> 32, of which waited for: 10 -> 20; matrix products, arithmetic and copies ran while one was open for 6% -> 5% of each run, Pallas kernels for 21% -> 22%
where the time goes in v4:
time: 86.4 us; the launch traced here: 85.5 us
  starting transfers between devices  27.5 us (32%)
  Pallas kernels  25.2 us (29%)
  waiting for transfers between devices  24.1 us (28%)
  other arithmetic  5.21 us (6%)
  local copies, waits for them, and re-layouts  1.64 us (2%)
  between operations  1.12 us (1%)
    ppermute x32, starting transfers between devices, swap(): return lax.ppermute(values, axis, [(i, i ^ mask) for i in range(size)])  27.5 us
    ppermute x32, waiting for transfers between devices, swap(): return lax.ppermute(values, axis, [(i, i ^ mask) for i in range(size)])  24.1 us
    pallas_call x1, Pallas kernels, write_pool(): pl.pallas_call(functools.partial(write_kernel, dims, parts), out_shape=pl...  7.49 us
    pallas_call x1, Pallas kernels, attention(): pl.pallas_call(functools.partial(attention_kernel, dims, len(pieces)), ou...  5.74 us
    pallas_call x1, Pallas kernels, fetch_weights(): pl.pallas_call(functools.partial(fetch_kernel, parts), out_shape=(jax.Sha...  5.33 us
    pallas_call x1, Pallas kernels, feed_forward(): pl.pallas_call(functools.partial(mlp_kernel, chunk, len(heads_out)), out_...  4.79 us
  transfers between devices with their start and end apart: 32, of which 20 were waited for; matrix products, arithmetic and copies ran while one was open for 5% of the time, Pallas kernels for 22%

profile of v4, /device:TPU:0, one launch (start us, length us, event | category | flops | bytes accessed | tf_op | source)
XLA Modules:
  0.0 85.5 jit_solution(16059612394649327073)
XLA Ops:
  1.8 4.1 %collective-permute-start = (bf16[16,2560]{1,0:T(8,128)(2,1)S(1)}, bf16[16,2560]{1,0:T(8,128)(2,1)S(1)}, u32[]{:S(2)}, u32[]{:S(2)}) collective-permute-start(bf16[16,2560]{1,0:T(8,128)(2,1)S(1)} %constant_dynamic-slice_fusion), channel_id=1, source_target_pairs={{0,16},{8,24},{16,0},{24,8},{1,17},{9,25},{17,1},{25,9},{2,18},{10... | collective-permute-start | bytes 245768 | tf_op jit(solution)/shard_map/ppermute | solution.py:23
  5.9 1.6 %collective-permute-start.3 = (bf16[96,2560]{1,0:T(8,128)(2,1)}, bf16[96,2560]{1,0:T(8,128)(2,1)S(1)}, u32[]{:S(2)}, u32[]{:S(2)}) collective-permute-start(bf16[96,2560]{1,0:T(8,128)(2,1)} %param.12), channel_id=1, source_target_pairs={{0,8},{8,0},{16,24},{24,16},{1,9},{9,1},{17,25},{25,17},{2,10},{10... | collective-permute-start | bytes 1474568 | tf_op jit(solution)/shard_map/ppermute | solution.py:23
  11.0 1.6 %collective-permute-start.1 = (bf16[16,2560]{1,0:T(8,128)(2,1)S(1)}, bf16[16,2560]{1,0:T(8,128)(2,1)S(1)}, u32[]{:S(2)}, u32[]{:S(2)}) collective-permute-start(bf16[16,2560]{1,0:T(8,128)(2,1)S(1)} %collective-permute-done), channel_id=1, source_target_pairs={{0,2},{1,3},{2,0},{3,1},{4,6},{5,7},{6,4},{7,5},{8,10},{9,11},{10,... | collective-permute-start | bytes 245768 | tf_op jit(solution)/shard_map/ppermute | solution.py:23
  12.6 2.9 %collective-permute-done.1 = bf16[16,2560]{1,0:T(8,128)(2,1)S(1)} collective-permute-done((bf16[16,2560]{1,0:T(8,128)(2,1)S(1)}, bf16[16,2560]{1,0:T(8,128)(2,1)S(1)}, u32[]{:S(2)}, u32[]{:S(2)}) %collective-permute-start.1) | collective-permute-done | bytes 81952 | tf_op jit(solution)/shard_map/ppermute | solution.py:23
  17.6 1.8 %collective-permute-done.3 = bf16[96,2560]{1,0:T(8,128)(2,1)S(1)} collective-permute-done((bf16[96,2560]{1,0:T(8,128)(2,1)}, bf16[96,2560]{1,0:T(8,128)(2,1)S(1)}, u32[]{:S(2)}, u32[]{:S(2)}) %collective-permute-start.3) | collective-permute-done | bytes 491552 | tf_op jit(solution)/shard_map/ppermute | solution.py:23
  21.3 2.0 %collective-permute-start.13 = (bf16[80,2560]{1,0:T(8,128)(2,1)S(1)}, bf16[80,2560]{1,0:T(8,128)(2,1)S(1)}, u32[]{:S(2)}, u32[]{:S(2)}) collective-permute-start(bf16[80,2560]{1,0:T(8,128)(2,1)S(1)} %copy-done), channel_id=1, source_target_pairs={{0,8},{8,0},{16,24},{24,16},{1,9},{9,1},{17,25},{25,17},{2,10},{10... | collective-permute-start | bytes 1228808 | tf_op jit(solution)/shard_map/ppermute | solution.py:23
  23.3 1.3 %collective-permute-start.14 = (bf16[80,2560]{1,0:T(8,128)(2,1)S(1)}, bf16[80,2560]{1,0:T(8,128)(2,1)S(1)}, u32[]{:S(2)}, u32[]{:S(2)}) collective-permute-start(bf16[80,2560]{1,0:T(8,128)(2,1)S(1)} %copy-done), channel_id=1, source_target_pairs={{0,16},{8,24},{16,0},{24,8},{1,17},{9,25},{17,1},{25,9},{2,18},{10... | collective-permute-start | bytes 1228808 | tf_op jit(solution)/shard_map/ppermute | solution.py:23
  25.1 2.8 %collective-permute-start.10 = (bf16[64,384]{1,0:T(8,128)(2,1)S(1)}, bf16[64,384]{1,0:T(8,128)(2,1)S(1)}, u32[]{:S(2)}, u32[]{:S(2)}) collective-permute-start(bf16[64,384]{1,0:T(8,128)(2,1)S(1)} %pad_maximum_fusion.2.refs_0_), channel_id=1, source_target_pairs={{0,6},{1,7},{2,4},{3,5},{4,2},{5,3},{6,0},{7,1},{8,14},{9,15},{10,... | collective-permute-start | bytes 147464 | tf_op jit(solution)/shard_map/ppermute | solution.py:23
  28.9 1.2 %collective-permute-done.10.refs_6_ = bf16[64,384]{1,0:T(8,128)(2,1)S(1)} collective-permute-done((bf16[64,384]{1,0:T(8,128)(2,1)S(1)}, bf16[64,384]{1,0:T(8,128)(2,1)S(1)}, u32[]{:S(2)}, u32[]{:S(2)}) %collective-permute-start.10) | collective-permute-done | bytes 49184 | tf_op jit(solution)/shard_map/ppermute | solution.py:23
  30.1 2.1 %collective-permute-done.6.refs_2_ = bf16[64,384]{1,0:T(8,128)(2,1)S(1)} collective-permute-done((bf16[64,384]{1,0:T(8,128)(2,1)S(1)}, bf16[64,384]{1,0:T(8,128)(2,1)S(1)}, u32[]{:S(2)}, u32[]{:S(2)}) %collective-permute-start.6) | collective-permute-done | bytes 49184 | tf_op jit(solution)/shard_map/ppermute | solution.py:23
  34.1 5.7 %page_attention.1 = (bf16[336,256]{1,0:T(8,128)(2,1)S(1)}, bf16[336,256]{1,0:T(8,128)(2,1)S(1)}, bf16[64,512]{1,0:T(8,128)(2,1)S(1)}) custom-call(s32[3,64]{1,0:T(4,128)S(1)} %pad_add_fusion.slots, s32[3]{0:T(128)S(1)} %pad_add_fusion.3.place, f32[64,128]{1,0:T(8,128)S(1)} %get-tuple-element.79.cosine, f32[64,128]{1,0:T(8,128)S(1)} %get-tuple-element.80.sine, ...), custom_call_target="tpu_custom_call" | custom-call | bytes 1024 | tf_op jit(solution)/shard_map/page_attention/pallas_call | solution.py:358
  41.6 1.3 %collective-permute-done.14.refs_2_ = bf16[80,2560]{1,0:T(8,128)(2,1)S(1)} collective-permute-done((bf16[80,2560]{1,0:T(8,128)(2,1)S(1)}, bf16[80,2560]{1,0:T(8,128)(2,1)S(1)}, u32[]{:S(2)}, u32[]{:S(2)}) %collective-permute-start.14) | collective-permute-done | bytes 409632 | tf_op jit(solution)/shard_map/ppermute | solution.py:23
  43.1 1.5 %collective-permute-start.15 = (bf16[336,256]{1,0:T(8,128)(2,1)S(1)}, bf16[336,256]{1,0:T(8,128)(2,1)S(1)}, u32[]{:S(2)}, u32[]{:S(2)}) collective-permute-start(bf16[336,256]{1,0:T(8,128)(2,1)S(1)} %merge_pair.1.after.refs_0_), channel_id=1, source_target_pairs={{0,2},{1,3},{2,0},{3,1},{4,6},{5,7},{6,4},{7,5},{8,10},{9,11},{10,... | collective-permute-start | bytes 516104 | tf_op jit(solution)/shard_map/ppermute | solution.py:23
  44.6 1.4 %collective-permute-start.16 = (bf16[336,256]{1,0:T(8,128)(2,1)S(1)}, bf16[336,256]{1,0:T(8,128)(2,1)S(1)}, u32[]{:S(2)}, u32[]{:S(2)}) collective-permute-start(bf16[336,256]{1,0:T(8,128)(2,1)S(1)} %merge_pair.1.after.refs_0_), channel_id=1, source_target_pairs={{0,4},{1,5},{2,6},{3,7},{4,0},{5,1},{6,2},{7,3},{8,12},{9,13},{10,... | collective-permute-start | bytes 516104 | tf_op jit(solution)/shard_map/ppermute | solution.py:23
  46.6 5.3 %fetch_weights.1 = (bf16[2,960,2560]{2,1,0:T(8,128)(2,1)S(1)}, bf16[960,2560]{1,0:T(8,128)(2,1)S(1)}, f32[8,128]{1,0:T(8,128)S(1)}) custom-call(bf16[2,960,2560]{2,1,0:T(8,128)(2,1)} %gate_up.1, bf16[960,2560]{1,0:T(8,128)(2,1)} %down.1, bf16[336,256]{1,0:T(8,128)(2,1)S(1)} %merge_pair.1.after.refs_0_), custom_call_target="tpu_custom_call" | custom-call | bytes 14745600 | tf_op jit(solution)/shard_map/fetch_weights/pallas_call | solution.py:435
  52.0 2.3 %collective-permute-done.16.refs_2_ = bf16[336,256]{1,0:T(8,128)(2,1)S(1)} collective-permute-done((bf16[336,256]{1,0:T(8,128)(2,1)S(1)}, bf16[336,256]{1,0:T(8,128)(2,1)S(1)}, u32[]{:S(2)}, u32[]{:S(2)}) %collective-permute-start.16) | collective-permute-done | bytes 172064 | tf_op jit(solution)/shard_map/ppermute | solution.py:23
  54.8 1.4 %collective-permute-done.19.other = bf16[32,2560]{1,0:T(8,128)(2,1)S(1)} collective-permute-done((bf16[32,2560]{1,0:T(8,128)(2,1)S(1)}, bf16[32,2560]{1,0:T(8,128)(2,1)S(1)}, u32[]{:S(2)}, u32[]{:S(2)}) %collective-permute-start.19) | collective-permute-done | bytes 163872 | tf_op jit(solution)/shard_map/ppermute | solution.py:23
  59.2 1.8 %collective-permute-start.25 = (bf16[64,320]{1,0:T(8,128)(2,1)S(1)}, bf16[64,320]{1,0:T(8,128)(2,1)S(1)}, u32[]{:S(2)}, u32[]{:S(2)}) collective-permute-start(bf16[64,320]{1,0:T(8,128)(2,1)S(1)} %project_out.1.refs_0_), channel_id=1, source_target_pairs={{0,6},{1,7},{2,4},{3,5},{4,2},{5,3},{6,0},{7,1},{8,14},{9,15},{10,... | collective-permute-start | bytes 122888 | tf_op jit(solution)/shard_map/ppermute | solution.py:23
  62.1 2.0 %collective-permute-done.25.refs_6_ = bf16[64,320]{1,0:T(8,128)(2,1)S(1)} collective-permute-done((bf16[64,320]{1,0:T(8,128)(2,1)S(1)}, bf16[64,320]{1,0:T(8,128)(2,1)S(1)}, u32[]{:S(2)}, u32[]{:S(2)}) %collective-permute-start.25) | collective-permute-done | bytes 40992 | tf_op jit(solution)/shard_map/ppermute | solution.py:23
  65.4 4.8 %feed_forward.1 = (f32[32,2560]{1,0:T(8,128)S(1)}, bf16[32,2560]{1,0:T(8,128)(2,1)S(1)}, bf16[32,2560]{1,0:T(8,128)(2,1)S(1)}) custom-call(s32[3]{0:T(128)S(1)} %pad_add_fusion.3.place, bf16[64,2560]{1,0:T(8,128)(2,1)S(1)} %reshape.312.stream, f32[1,2560]{1,0:T(1,128)S(1)} %reshape.313.gain, bf16[2,960,2560]{2,1,0:T(8,128)(2,1)S(1)} %get-tuple-element.41.gates, ...), custom_call_target="tpu_custom_call" | custom-call | tf_op jit(solution)/shard_map/feed_forward/pallas_call | solution.py:507
  70.4 1.2 %collective-permute-done.27 = bf16[32,2560]{1,0:T(8,128)(2,1)S(1)} collective-permute-done((bf16[32,2560]{1,0:T(8,128)(2,1)S(1)}, bf16[32,2560]{1,0:T(8,128)(2,1)S(1)}, u32[]{:S(2)}, u32[]{:S(2)}) %collective-permute-start.27) | collective-permute-done | bytes 163872 | tf_op jit(solution)/shard_map/ppermute | solution.py:23
  72.9 1.2 %collective-permute-start.29 = (bf16[32,2560]{1,0:T(8,128)(2,1)S(1)}, bf16[32,2560]{1,0:T(8,128)(2,1)S(1)}, u32[]{:S(2)}, u32[]{:S(2)}) collective-permute-start(bf16[32,2560]{1,0:T(8,128)(2,1)S(1)} %add_convert_fusion.1), channel_id=1, source_target_pairs={{0,4},{1,5},{2,6},{3,7},{4,0},{5,1},{6,2},{7,3},{8,12},{9,13},{10,... | collective-permute-start | bytes 491528 | tf_op jit(solution)/shard_map/ppermute | solution.py:23
  75.2 7.5 %write_pool.1 = bf16[64,128,512]{2,1,0:T(8,128)(2,1)} custom-call(s32[3,32]{1,0:T(4,128)S(1)} %pad_add_fusion.1.patches, s32[16]{0:T(128)S(1)} %copy-done.1, bf16[64,512]{1,0:T(8,128)(2,1)S(1)} %get-tuple-element.56.fresh, bf16[64,128,512]{2,1,0:T(8,128)(2,1)} %source.1), custom_call_target="tpu_custom_call" | custom-call | bytes 16777216 | tf_op jit(solution)/shard_map/write_pool/pallas_call | solution.py:103
  83.0 1.4 %collective-permute-done.31 = bf16[8,4,2560]{2,1,0:T(4,128)(2,1)S(1)} collective-permute-done((bf16[8,4,2560]{2,1,0:T(4,128)(2,1)S(1)}, bf16[8,4,2560]{2,1,0:T(4,128)(2,1)S(1)}, u32[]{:S(2)}, u32[]{:S(2)}) %collective-permute-start.31) | collective-permute-done | bytes 163872 | tf_op jit(solution)/shard_map/ppermute | solution.py:23
  (97 shorter events, 24.1 us)
Async XLA Ops:
  1.8 9.1 %collective-permute-start = (bf16[16,2560]{1,0:T(8,128)(2,1)S(1)}, bf16[16,2560]{1,0:T(8,128)(2,1)S(1)}, u32[]{:S(2)}, u32[]{:S(2)}) collective-permute-start(bf16[16,2560]{1,0:T(8,128)(2,1)S(1)} %constant_dynamic-slice_fusion), channel_id=1, source_target_pairs={{0,16},{8,24},{16,0},{24,8},{1,17},{9,25},{17,1},{25,9},{2,18},{10... | collective-permute-start | bytes 245768 | tf_op jit(solution)/shard_map/ppermute | solution.py:23
  5.9 13.5 %collective-permute-start.3 = (bf16[96,2560]{1,0:T(8,128)(2,1)}, bf16[96,2560]{1,0:T(8,128)(2,1)S(1)}, u32[]{:S(2)}, u32[]{:S(2)}) collective-permute-start(bf16[96,2560]{1,0:T(8,128)(2,1)} %param.12), channel_id=1, source_target_pairs={{0,8},{8,0},{16,24},{24,16},{1,9},{9,1},{17,25},{25,17},{2,10},{10... | collective-permute-start | bytes 1474568 | tf_op jit(solution)/shard_map/ppermute | solution.py:23
  11.0 4.5 %collective-permute-start.1 = (bf16[16,2560]{1,0:T(8,128)(2,1)S(1)}, bf16[16,2560]{1,0:T(8,128)(2,1)S(1)}, u32[]{:S(2)}, u32[]{:S(2)}) collective-permute-start(bf16[16,2560]{1,0:T(8,128)(2,1)S(1)} %collective-permute-done), channel_id=1, source_target_pairs={{0,2},{1,3},{2,0},{3,1},{4,6},{5,7},{6,4},{7,5},{8,10},{9,11},{10,... | collective-permute-start | bytes 245768 | tf_op jit(solution)/shard_map/ppermute | solution.py:23
  19.9 5.0 %collective-permute-start.4 = (bf16[64,192]{1,0:T(8,128)(2,1)S(1)}, bf16[64,192]{1,0:T(8,128)(2,1)S(1)}, u32[]{:S(2)}, u32[]{:S(2)}) collective-permute-start(bf16[64,192]{1,0:T(8,128)(2,1)S(1)} %slice.37), channel_id=1, source_target_pairs={{0,16},{8,24},{16,0},{24,8},{1,17},{9,25},{17,1},{25,9},{2,18},{10... | collective-permute-start | bytes 73736 | tf_op jit(solution)/shard_map/ppermute | solution.py:23
  21.3 20.3 %collective-permute-start.13 = (bf16[80,2560]{1,0:T(8,128)(2,1)S(1)}, bf16[80,2560]{1,0:T(8,128)(2,1)S(1)}, u32[]{:S(2)}, u32[]{:S(2)}) collective-permute-start(bf16[80,2560]{1,0:T(8,128)(2,1)S(1)} %copy-done), channel_id=1, source_target_pairs={{0,8},{8,0},{16,24},{24,16},{1,9},{9,1},{17,25},{25,17},{2,10},{10... | collective-permute-start | bytes 1228808 | tf_op jit(solution)/shard_map/ppermute | solution.py:23
  23.3 19.6 %collective-permute-start.14 = (bf16[80,2560]{1,0:T(8,128)(2,1)S(1)}, bf16[80,2560]{1,0:T(8,128)(2,1)S(1)}, u32[]{:S(2)}, u32[]{:S(2)}) collective-permute-start(bf16[80,2560]{1,0:T(8,128)(2,1)S(1)} %copy-done), channel_id=1, source_target_pairs={{0,16},{8,24},{16,0},{24,8},{1,17},{9,25},{17,1},{25,9},{2,18},{10... | collective-permute-start | bytes 1228808 | tf_op jit(solution)/shard_map/ppermute | solution.py:23
  25.1 5.0 %collective-permute-start.10 = (bf16[64,384]{1,0:T(8,128)(2,1)S(1)}, bf16[64,384]{1,0:T(8,128)(2,1)S(1)}, u32[]{:S(2)}, u32[]{:S(2)}) collective-permute-start(bf16[64,384]{1,0:T(8,128)(2,1)S(1)} %pad_maximum_fusion.2.refs_0_), channel_id=1, source_target_pairs={{0,6},{1,7},{2,4},{3,5},{4,2},{5,3},{6,0},{7,1},{8,14},{9,15},{10,... | collective-permute-start | bytes 147464 | tf_op jit(solution)/shard_map/ppermute | solution.py:23
  28.1 4.2 %collective-permute-start.6 = (bf16[64,384]{1,0:T(8,128)(2,1)S(1)}, bf16[64,384]{1,0:T(8,128)(2,1)S(1)}, u32[]{:S(2)}, u32[]{:S(2)}) collective-permute-start(bf16[64,384]{1,0:T(8,128)(2,1)S(1)} %pad_maximum_fusion.2.refs_0_), channel_id=1, source_target_pairs={{0,2},{1,3},{2,0},{3,1},{4,6},{5,7},{6,4},{7,5},{8,10},{9,11},{10,... | collective-permute-start | bytes 147464 | tf_op jit(solution)/shard_map/ppermute | solution.py:23
  28.6 4.1 %collective-permute-start.8 = (bf16[64,384]{1,0:T(8,128)(2,1)S(1)}, bf16[64,384]{1,0:T(8,128)(2,1)S(1)}, u32[]{:S(2)}, u32[]{:S(2)}) collective-permute-start(bf16[64,384]{1,0:T(8,128)(2,1)S(1)} %pad_maximum_fusion.2.refs_0_), channel_id=1, source_target_pairs={{0,4},{1,5},{2,6},{3,7},{4,0},{5,1},{6,2},{7,3},{8,12},{9,13},{10,... | collective-permute-start | bytes 147464 | tf_op jit(solution)/shard_map/ppermute | solution.py:23
  30.1 2.6 %collective-permute-start.5 = (bf16[64,384]{1,0:T(8,128)(2,1)S(1)}, bf16[64,384]{1,0:T(8,128)(2,1)S(1)}, u32[]{:S(2)}, u32[]{:S(2)}) collective-permute-start(bf16[64,384]{1,0:T(8,128)(2,1)S(1)} %pad_maximum_fusion.2.refs_0_), channel_id=1, source_target_pairs={{0,1},{1,0},{2,3},{3,2},{4,5},{5,4},{6,7},{7,6},{8,9},{9,8},{10,11... | collective-permute-start | bytes 147464 | tf_op jit(solution)/shard_map/ppermute | solution.py:23
  39.9 1.5 %collective-permute-start.12 = (bf16[336,256]{1,0:T(8,128)(2,1)S(1)}, bf16[336,256]{1,0:T(8,128)(2,1)S(1)}, u32[]{:S(2)}, u32[]{:S(2)}) collective-permute-start(bf16[336,256]{1,0:T(8,128)(2,1)S(1)} %get-tuple-element.37), channel_id=1, source_target_pairs={{0,1},{1,0},{2,3},{3,2},{4,5},{5,4},{6,7},{7,6},{8,9},{9,8},{10,11... | collective-permute-start | bytes 516104 | tf_op jit(solution)/shard_map/ppermute | solution.py:23
  42.9 11.4 %collective-permute-start.18 = (bf16[80,2560]{1,0:T(8,128)(2,1)S(1)}, bf16[80,2560]{1,0:T(8,128)(2,1)S(1)}, u32[]{:S(2)}, u32[]{:S(2)}) collective-permute-start(bf16[80,2560]{1,0:T(8,128)(2,1)S(1)} %collective-permute-done.14.refs_2_), channel_id=1, source_target_pairs={{0,8},{8,0},{16,24},{24,16},{1,9},{9,1},{17,25},{25,17},{2,10},{10... | collective-permute-start | bytes 1228808 | tf_op jit(solution)/shard_map/ppermute | solution.py:23
  43.1 8.8 %collective-permute-start.15 = (bf16[336,256]{1,0:T(8,128)(2,1)S(1)}, bf16[336,256]{1,0:T(8,128)(2,1)S(1)}, u32[]{:S(2)}, u32[]{:S(2)}) collective-permute-start(bf16[336,256]{1,0:T(8,128)(2,1)S(1)} %merge_pair.1.after.refs_0_), channel_id=1, source_target_pairs={{0,2},{1,3},{2,0},{3,1},{4,6},{5,7},{6,4},{7,5},{8,10},{9,11},{10,... | collective-permute-start | bytes 516104 | tf_op jit(solution)/shard_map/ppermute | solution.py:23
  44.6 9.7 %collective-permute-start.16 = (bf16[336,256]{1,0:T(8,128)(2,1)S(1)}, bf16[336,256]{1,0:T(8,128)(2,1)S(1)}, u32[]{:S(2)}, u32[]{:S(2)}) collective-permute-start(bf16[336,256]{1,0:T(8,128)(2,1)S(1)} %merge_pair.1.after.refs_0_), channel_id=1, source_target_pairs={{0,4},{1,5},{2,6},{3,7},{4,0},{5,1},{6,2},{7,3},{8,12},{9,13},{10,... | collective-permute-start | bytes 516104 | tf_op jit(solution)/shard_map/ppermute | solution.py:23
  46.0 8.3 %collective-permute-start.17 = (bf16[336,256]{1,0:T(8,128)(2,1)S(1)}, bf16[336,256]{1,0:T(8,128)(2,1)S(1)}, u32[]{:S(2)}, u32[]{:S(2)}) collective-permute-start(bf16[336,256]{1,0:T(8,128)(2,1)S(1)} %merge_pair.1.after.refs_0_), channel_id=1, source_target_pairs={{0,6},{1,7},{2,4},{3,5},{4,2},{5,3},{6,0},{7,1},{8,14},{9,15},{10,... | collective-permute-start | bytes 516104 | tf_op jit(solution)/shard_map/ppermute | solution.py:23
  57.4 4.2 %collective-permute-start.21 = (bf16[64,320]{1,0:T(8,128)(2,1)S(1)}, bf16[64,320]{1,0:T(8,128)(2,1)S(1)}, u32[]{:S(2)}, u32[]{:S(2)}) collective-permute-start(bf16[64,320]{1,0:T(8,128)(2,1)S(1)} %project_out.1.refs_0_), channel_id=1, source_target_pairs={{0,2},{1,3},{2,0},{3,1},{4,6},{5,7},{6,4},{7,5},{8,10},{9,11},{10,... | collective-permute-start | bytes 122888 | tf_op jit(solution)/shard_map/ppermute | solution.py:23
  58.0 4.1 %collective-permute-start.23 = (bf16[64,320]{1,0:T(8,128)(2,1)S(1)}, bf16[64,320]{1,0:T(8,128)(2,1)S(1)}, u32[]{:S(2)}, u32[]{:S(2)}) collective-permute-start(bf16[64,320]{1,0:T(8,128)(2,1)S(1)} %project_out.1.refs_0_), channel_id=1, source_target_pairs={{0,4},{1,5},{2,6},{3,7},{4,0},{5,1},{6,2},{7,3},{8,12},{9,13},{10,... | collective-permute-start | bytes 122888 | tf_op jit(solution)/shard_map/ppermute | solution.py:23
  59.2 5.0 %collective-permute-start.25 = (bf16[64,320]{1,0:T(8,128)(2,1)S(1)}, bf16[64,320]{1,0:T(8,128)(2,1)S(1)}, u32[]{:S(2)}, u32[]{:S(2)}) collective-permute-start(bf16[64,320]{1,0:T(8,128)(2,1)S(1)} %project_out.1.refs_0_), channel_id=1, source_target_pairs={{0,6},{1,7},{2,4},{3,5},{4,2},{5,3},{6,0},{7,1},{8,14},{9,15},{10,... | collective-permute-start | bytes 122888 | tf_op jit(solution)/shard_map/ppermute | solution.py:23
  60.9 3.3 %collective-permute-start.20 = (bf16[64,320]{1,0:T(8,128)(2,1)S(1)}, bf16[64,320]{1,0:T(8,128)(2,1)S(1)}, u32[]{:S(2)}, u32[]{:S(2)}) collective-permute-start(bf16[64,320]{1,0:T(8,128)(2,1)S(1)} %project_out.1.refs_0_), channel_id=1, source_target_pairs={{0,1},{1,0},{2,3},{3,2},{4,5},{5,4},{6,7},{7,6},{8,9},{9,8},{10,11... | collective-permute-start | bytes 122888 | tf_op jit(solution)/shard_map/ppermute | solution.py:23
  61.5 2.7 %collective-permute-start.22 = (bf16[64,320]{1,0:T(8,128)(2,1)S(1)}, bf16[64,320]{1,0:T(8,128)(2,1)S(1)}, u32[]{:S(2)}, u32[]{:S(2)}) collective-permute-start(bf16[64,320]{1,0:T(8,128)(2,1)S(1)} %collective-permute-done.21.refs_2_), channel_id=1, source_target_pairs={{0,1},{1,0},{2,3},{3,2},{4,5},{5,4},{6,7},{7,6},{8,9},{9,8},{10,11... | collective-permute-start | bytes 122888 | tf_op jit(solution)/shard_map/ppermute | solution.py:23
  62.1 2.1 %collective-permute-start.24 = (bf16[64,320]{1,0:T(8,128)(2,1)S(1)}, bf16[64,320]{1,0:T(8,128)(2,1)S(1)}, u32[]{:S(2)}, u32[]{:S(2)}) collective-permute-start(bf16[64,320]{1,0:T(8,128)(2,1)S(1)} %collective-permute-done.23.refs_4_), channel_id=1, source_target_pairs={{0,1},{1,0},{2,3},{3,2},{4,5},{5,4},{6,7},{7,6},{8,9},{9,8},{10,11... | collective-permute-start | bytes 122888 | tf_op jit(solution)/shard_map/ppermute | solution.py:23
  71.7 11.1 %collective-permute-start.28 = (bf16[32,2560]{1,0:T(8,128)(2,1)S(1)}, bf16[32,2560]{1,0:T(8,128)(2,1)S(1)}, u32[]{:S(2)}, u32[]{:S(2)}) collective-permute-start(bf16[32,2560]{1,0:T(8,128)(2,1)S(1)} %add_convert_fusion.1), channel_id=1, source_target_pairs={{0,2},{1,3},{2,0},{3,1},{4,6},{5,7},{6,4},{7,5},{8,10},{9,11},{10,... | collective-permute-start | bytes 491528 | tf_op jit(solution)/shard_map/ppermute | solution.py:23
  72.9 9.9 %collective-permute-start.29 = (bf16[32,2560]{1,0:T(8,128)(2,1)S(1)}, bf16[32,2560]{1,0:T(8,128)(2,1)S(1)}, u32[]{:S(2)}, u32[]{:S(2)}) collective-permute-start(bf16[32,2560]{1,0:T(8,128)(2,1)S(1)} %add_convert_fusion.1), channel_id=1, source_target_pairs={{0,4},{1,5},{2,6},{3,7},{4,0},{5,1},{6,2},{7,3},{8,12},{9,13},{10,... | collective-permute-start | bytes 491528 | tf_op jit(solution)/shard_map/ppermute | solution.py:23
  74.1 8.7 %collective-permute-start.30 = (bf16[32,2560]{1,0:T(8,128)(2,1)S(1)}, bf16[32,2560]{1,0:T(8,128)(2,1)S(1)}, u32[]{:S(2)}, u32[]{:S(2)}) collective-permute-start(bf16[32,2560]{1,0:T(8,128)(2,1)S(1)} %add_convert_fusion.1), channel_id=1, source_target_pairs={{0,6},{1,7},{2,4},{3,5},{4,2},{5,3},{6,0},{7,1},{8,14},{9,15},{10,... | collective-permute-start | bytes 491528 | tf_op jit(solution)/shard_map/ppermute | solution.py:23
  (14 other events, 87.5 us)

commit v5 on v4

--- a/solution.py
+++ b/solution.py
@@ -502,7 +502,7 @@
 def feed_forward(n_seq, place, stream, heads_out, gain, gates, downs):
     lines, width = stream.shape
     units = downs.shape[0]
-    chunk = max(c for c in range(16, 256, 16) if units % c == 0)
+    chunk = max(c for c in range(16, 512, 16) if units % c == 0)
     vmem = pl.BlockSpec(memory_space=pltpu.VMEM)
     return pl.pallas_call(
         functools.partial(mlp_kernel, chunk, len(heads_out)),
@@ -563,13 +563,14 @@
     far = list(range(2, n_dp, 2))
     quarter_lines = lines // 4
     quarter_index = seq_index % 4
-    my_quarter = lax.dynamic_slice_in_dim(stream, quarter_index * quarter_lines, quarter_lines)
+    some = requests // 4
+    my_quarter = lax.dynamic_slice_in_dim(tokens, quarter_index * some, some)
     far_parts = jnp.concatenate([swap(my_quarter, "dp", n_dp, k) for k in far], axis=0)
-    out_first, far_parts = lax.optimization_barrier((out_weight, far_parts))
-    out_neighbour = swap(out_first, "dp", n_dp, 1)
+    cache_len, page_table, far_parts = lax.optimization_barrier((cache_len, page_table, far_parts))
     far_pairs = [far_parts, swap(far_parts, "seq", n_seq, 2)]
     far_mine = jnp.concatenate(far_pairs, axis=0)
-    far_other = swap(far_mine, "seq", n_seq, 1)
+    far_other = swap(far_mine, "seq", n_seq, 1).reshape(-1, width)
+    far_mine = far_mine.reshape(-1, width)
     held_pool = pltpu.with_memory_space_constraint(kv_pool, pltpu.HBM)
     groups = [stream]
     stride = len(far) * quarter_lines
@@ -586,7 +587,7 @@
         jnp.concatenate([by_partner, by_mine], axis=1),
     ).astype(bf16)
     out_early, products = lax.optimization_barrier((out_weight, products))
-    out_blocks = {k: swap(out_early, "dp", n_dp, k) for k in far}
+    out_blocks = {k: swap(out_early, "dp", n_dp, k) for k in [1, *far]}
     blocks = [products[:lines]]
     for i, k in enumerate(far):
         back = swap(products[(i + 1) * lines : (i + 2) * lines], "dp", n_dp, k)
@@ -609,7 +610,6 @@
         columns.append(block)
     pieces = gather_pieces(jnp.concatenate(columns, axis=1), n_seq)
     out_blocks[0] = out_weight
-    out_blocks[1] = out_neighbour
 
     positions_int = cache_len[:, None] + jnp.arange(new_count, dtype=jnp.int32)[None, :]
     quarter = head_dim // 4

time: 86.4 us -> 85.8 us (level)
  other arithmetic: 5.21 us -> 2.64 us
  local copies, waits for them, and re-layouts: 1.64 us -> 2.68 us
  waiting for transfers between devices: 24.1 us -> 25 us
    dynamic_slice x1, local copies, waits for them, and re-layouts: 0.01 us -> 0.92 us  [body(): my_quarter = lax.dynamic_slice_in_dim(tokens, quarter_index * some, some)]
    ppermute x32, waiting for transfers between devices: 24.1 us -> 25 us  [swap(): return lax.ppermute(values, axis, [(i, i ^ mask) for i in range(size)])]
  transfers between devices with their start and end apart: 32 -> 32, of which waited for: 20 -> 21; matrix products, arithmetic and copies ran while one was open for 5% -> 4% of each run, Pallas kernels for 22% -> 23%
where the time goes in v5:
time: 85.8 us; the launch traced here: 85.6 us
  starting transfers between devices  28 us (33%)
  Pallas kernels  25.3 us (29%)
  waiting for transfers between devices  25 us (29%)
  local copies, waits for them, and re-layouts  2.68 us (3%)
  other arithmetic  2.64 us (3%)
  between operations  1.15 us (1%)
    ppermute x32, starting transfers between devices, swap(): return lax.ppermute(values, axis, [(i, i ^ mask) for i in range(size)])  28 us
    ppermute x32, waiting for transfers between devices, swap(): return lax.ppermute(values, axis, [(i, i ^ mask) for i in range(size)])  25 us
    pallas_call x1, Pallas kernels, write_pool(): pl.pallas_call(functools.partial(write_kernel, dims, parts), out_shape=pl...  8.18 us
    pallas_call x1, Pallas kernels, attention(): pl.pallas_call(functools.partial(attention_kernel, dims, len(pieces)), ou...  5.63 us
    pallas_call x1, Pallas kernels, fetch_weights(): pl.pallas_call(functools.partial(fetch_kernel, parts), out_shape=(jax.Sha...  5.33 us
    pallas_call x1, Pallas kernels, feed_forward(): pl.pallas_call(functools.partial(mlp_kernel, chunk, len(heads_out)), out_...  4.38 us
  transfers between devices with their start and end apart: 32, of which 21 were waited for; matrix products, arithmetic and copies ran while one was open for 4% of the time, Pallas kernels for 23%

profile of v5, /device:TPU:0, one launch (start us, length us, event | category | flops | bytes accessed | tf_op | source)
XLA Modules:
  0.0 85.6 jit_solution(2130265984742137478)
XLA Ops:
  1.6 4.1 %collective-permute-start = (bf16[4,4,2560]{2,1,0:T(4,128)(2,1)S(1)}, bf16[4,4,2560]{2,1,0:T(4,128)(2,1)S(1)}, u32[]{:S(2)}, u32[]{:S(2)}) collective-permute-start(bf16[4,4,2560]{2,1,0:T(4,128)(2,1)S(1)} %constant_dynamic-slice_fusion), channel_id=1, source_target_pairs={{0,16},{8,24},{16,0},{24,8},{1,17},{9,25},{17,1},{25,9},{2,18},{10... | collective-permute-start | bytes 245768 | tf_op jit(solution)/shard_map/ppermute | solution.py:23
  5.7 1.6 %collective-permute-start.3 = (bf16[96,2560]{1,0:T(8,128)(2,1)}, bf16[96,2560]{1,0:T(8,128)(2,1)S(1)}, u32[]{:S(2)}, u32[]{:S(2)}) collective-permute-start(bf16[96,2560]{1,0:T(8,128)(2,1)} %param.12), channel_id=1, source_target_pairs={{0,8},{8,0},{16,24},{24,16},{1,9},{9,1},{17,25},{25,17},{2,10},{10... | collective-permute-start | bytes 1474568 | tf_op jit(solution)/shard_map/ppermute | solution.py:23
  9.5 1.9 %collective-permute-start.1 = (bf16[4,4,2560]{2,1,0:T(4,128)(2,1)S(1)}, bf16[4,4,2560]{2,1,0:T(4,128)(2,1)S(1)}, u32[]{:S(2)}, u32[]{:S(2)}) collective-permute-start(bf16[4,4,2560]{2,1,0:T(4,128)(2,1)S(1)} %collective-permute-done), channel_id=1, source_target_pairs={{0,2},{1,3},{2,0},{3,1},{4,6},{5,7},{6,4},{7,5},{8,10},{9,11},{10,... | collective-permute-start | bytes 245768 | tf_op jit(solution)/shard_map/ppermute | solution.py:23
  12.2 1.7 %collective-permute-done.1 = bf16[4,4,2560]{2,1,0:T(4,128)(2,1)S(1)} collective-permute-done((bf16[4,4,2560]{2,1,0:T(4,128)(2,1)S(1)}, bf16[4,4,2560]{2,1,0:T(4,128)(2,1)S(1)}, u32[]{:S(2)}, u32[]{:S(2)}) %collective-permute-start.1) | collective-permute-done | bytes 81952 | tf_op jit(solution)/shard_map/ppermute | solution.py:23
  14.2 1.3 %collective-permute-done.2 = bf16[8,4,2560]{2,1,0:T(4,128)(2,1)S(1)} collective-permute-done((bf16[8,4,2560]{2,1,0:T(4,128)(2,1)S(1)}, bf16[8,4,2560]{2,1,0:T(4,128)(2,1)S(1)}, u32[]{:S(2)}, u32[]{:S(2)}) %collective-permute-start.2) | collective-permute-done | bytes 163872 | tf_op jit(solution)/shard_map/ppermute | solution.py:23
  16.4 2.8 %collective-permute-done.3 = bf16[96,2560]{1,0:T(8,128)(2,1)S(1)} collective-permute-done((bf16[96,2560]{1,0:T(8,128)(2,1)}, bf16[96,2560]{1,0:T(8,128)(2,1)S(1)}, u32[]{:S(2)}, u32[]{:S(2)}) %collective-permute-start.3) | collective-permute-done | bytes 491552 | tf_op jit(solution)/shard_map/ppermute | solution.py:23
  21.0 2.0 %collective-permute-start.13 = (bf16[80,2560]{1,0:T(8,128)(2,1)S(1)}, bf16[80,2560]{1,0:T(8,128)(2,1)S(1)}, u32[]{:S(2)}, u32[]{:S(2)}) collective-permute-start(bf16[80,2560]{1,0:T(8,128)(2,1)S(1)} %copy-done), channel_id=1, source_target_pairs={{0,8},{8,0},{16,24},{24,16},{1,9},{9,1},{17,25},{25,17},{2,10},{10... | collective-permute-start | bytes 1228808 | tf_op jit(solution)/shard_map/ppermute | solution.py:23
  23.1 1.3 %collective-permute-start.14 = (bf16[80,2560]{1,0:T(8,128)(2,1)S(1)}, bf16[80,2560]{1,0:T(8,128)(2,1)S(1)}, u32[]{:S(2)}, u32[]{:S(2)}) collective-permute-start(bf16[80,2560]{1,0:T(8,128)(2,1)S(1)} %copy-done), channel_id=1, source_target_pairs={{0,16},{8,24},{16,0},{24,8},{1,17},{9,25},{17,1},{25,9},{2,18},{10... | collective-permute-start | bytes 1228808 | tf_op jit(solution)/shard_map/ppermute | solution.py:23
  24.8 2.7 %collective-permute-start.10 = (bf16[64,384]{1,0:T(8,128)(2,1)S(1)}, bf16[64,384]{1,0:T(8,128)(2,1)S(1)}, u32[]{:S(2)}, u32[]{:S(2)}) collective-permute-start(bf16[64,384]{1,0:T(8,128)(2,1)S(1)} %pad_maximum_fusion.1.refs_0_), channel_id=1, source_target_pairs={{0,6},{1,7},{2,4},{3,5},{4,2},{5,3},{6,0},{7,1},{8,14},{9,15},{10,... | collective-permute-start | bytes 147464 | tf_op jit(solution)/shard_map/ppermute | solution.py:23
  29.9 2.1 %collective-permute-done.6.refs_2_ = bf16[64,384]{1,0:T(8,128)(2,1)S(1)} collective-permute-done((bf16[64,384]{1,0:T(8,128)(2,1)S(1)}, bf16[64,384]{1,0:T(8,128)(2,1)S(1)}, u32[]{:S(2)}, u32[]{:S(2)}) %collective-permute-start.6) | collective-permute-done | bytes 49184 | tf_op jit(solution)/shard_map/ppermute | solution.py:23
  33.9 5.6 %page_attention.1 = (bf16[336,256]{1,0:T(8,128)(2,1)S(1)}, bf16[336,256]{1,0:T(8,128)(2,1)S(1)}, bf16[64,512]{1,0:T(8,128)(2,1)S(1)}) custom-call(s32[3,64]{1,0:T(4,128)S(1)} %pad_add_fusion.slots, s32[3]{0:T(128)S(1)} %pad_add_fusion.3.place, f32[64,128]{1,0:T(8,128)S(1)} %get-tuple-element.83.cosine, f32[64,128]{1,0:T(8,128)S(1)} %get-tuple-element.84.sine, ...), custom_call_target="tpu_custom_call" | custom-call | bytes 1024 | tf_op jit(solution)/shard_map/page_attention/pallas_call | solution.py:358
  41.3 1.4 %collective-permute-done.14.refs_2_ = bf16[80,2560]{1,0:T(8,128)(2,1)S(1)} collective-permute-done((bf16[80,2560]{1,0:T(8,128)(2,1)S(1)}, bf16[80,2560]{1,0:T(8,128)(2,1)S(1)}, u32[]{:S(2)}, u32[]{:S(2)}) %collective-permute-start.14) | collective-permute-done | bytes 409632 | tf_op jit(solution)/shard_map/ppermute | solution.py:23
  43.0 1.4 %collective-permute-start.15 = (bf16[336,256]{1,0:T(8,128)(2,1)S(1)}, bf16[336,256]{1,0:T(8,128)(2,1)S(1)}, u32[]{:S(2)}, u32[]{:S(2)}) collective-permute-start(bf16[336,256]{1,0:T(8,128)(2,1)S(1)} %merge_pair.1.after.refs_0_), channel_id=1, source_target_pairs={{0,2},{1,3},{2,0},{3,1},{4,6},{5,7},{6,4},{7,5},{8,10},{9,11},{10,... | collective-permute-start | bytes 516104 | tf_op jit(solution)/shard_map/ppermute | solution.py:23
  44.4 1.4 %collective-permute-start.16 = (bf16[336,256]{1,0:T(8,128)(2,1)S(1)}, bf16[336,256]{1,0:T(8,128)(2,1)S(1)}, u32[]{:S(2)}, u32[]{:S(2)}) collective-permute-start(bf16[336,256]{1,0:T(8,128)(2,1)S(1)} %merge_pair.1.after.refs_0_), channel_id=1, source_target_pairs={{0,4},{1,5},{2,6},{3,7},{4,0},{5,1},{6,2},{7,3},{8,12},{9,13},{10,... | collective-permute-start | bytes 516104 | tf_op jit(solution)/shard_map/ppermute | solution.py:23
  46.5 5.3 %fetch_weights.1 = (bf16[2,960,2560]{2,1,0:T(8,128)(2,1)S(1)}, bf16[960,2560]{1,0:T(8,128)(2,1)S(1)}, f32[8,128]{1,0:T(8,128)S(1)}) custom-call(bf16[2,960,2560]{2,1,0:T(8,128)(2,1)} %gate_up.1, bf16[960,2560]{1,0:T(8,128)(2,1)} %down.1, bf16[336,256]{1,0:T(8,128)(2,1)S(1)} %merge_pair.1.after.refs_0_), custom_call_target="tpu_custom_call" | custom-call | bytes 14745600 | tf_op jit(solution)/shard_map/fetch_weights/pallas_call | solution.py:435
  51.8 2.3 %collective-permute-done.16.refs_2_ = bf16[336,256]{1,0:T(8,128)(2,1)S(1)} collective-permute-done((bf16[336,256]{1,0:T(8,128)(2,1)S(1)}, bf16[336,256]{1,0:T(8,128)(2,1)S(1)}, u32[]{:S(2)}, u32[]{:S(2)}) %collective-permute-start.16) | collective-permute-done | bytes 172064 | tf_op jit(solution)/shard_map/ppermute | solution.py:23
  54.6 1.4 %collective-permute-done.19.other = bf16[32,2560]{1,0:T(8,128)(2,1)S(1)} collective-permute-done((bf16[32,2560]{1,0:T(8,128)(2,1)S(1)}, bf16[32,2560]{1,0:T(8,128)(2,1)S(1)}, u32[]{:S(2)}, u32[]{:S(2)}) %collective-permute-start.19) | collective-permute-done | bytes 163872 | tf_op jit(solution)/shard_map/ppermute | solution.py:23
  59.0 1.8 %collective-permute-start.25 = (bf16[64,320]{1,0:T(8,128)(2,1)S(1)}, bf16[64,320]{1,0:T(8,128)(2,1)S(1)}, u32[]{:S(2)}, u32[]{:S(2)}) collective-permute-start(bf16[64,320]{1,0:T(8,128)(2,1)S(1)} %project_out.1.refs_0_), channel_id=1, source_target_pairs={{0,6},{1,7},{2,4},{3,5},{4,2},{5,3},{6,0},{7,1},{8,14},{9,15},{10,... | collective-permute-start | bytes 122888 | tf_op jit(solution)/shard_map/ppermute | solution.py:23
  62.0 2.0 %collective-permute-done.25.refs_6_ = bf16[64,320]{1,0:T(8,128)(2,1)S(1)} collective-permute-done((bf16[64,320]{1,0:T(8,128)(2,1)S(1)}, bf16[64,320]{1,0:T(8,128)(2,1)S(1)}, u32[]{:S(2)}, u32[]{:S(2)}) %collective-permute-start.25) | collective-permute-done | bytes 40992 | tf_op jit(solution)/shard_map/ppermute | solution.py:23
  65.2 4.4 %feed_forward.1 = (f32[32,2560]{1,0:T(8,128)S(1)}, bf16[32,2560]{1,0:T(8,128)(2,1)S(1)}, bf16[32,2560]{1,0:T(8,128)(2,1)S(1)}) custom-call(s32[3]{0:T(128)S(1)} %pad_add_fusion.3.place, bf16[64,2560]{1,0:T(8,128)(2,1)S(1)} %reshape.318.stream, f32[1,2560]{1,0:T(1,128)S(1)} %reshape.319.gain, bf16[2,960,2560]{2,1,0:T(8,128)(2,1)S(1)} %get-tuple-element.43.gates, ...), custom_call_target="tpu_custom_call" | custom-call | tf_op jit(solution)/shard_map/feed_forward/pallas_call | solution.py:507
  69.8 1.2 %collective-permute-done.27 = bf16[32,2560]{1,0:T(8,128)(2,1)S(1)} collective-permute-done((bf16[32,2560]{1,0:T(8,128)(2,1)S(1)}, bf16[32,2560]{1,0:T(8,128)(2,1)S(1)}, u32[]{:S(2)}, u32[]{:S(2)}) %collective-permute-start.27) | collective-permute-done | bytes 163872 | tf_op jit(solution)/shard_map/ppermute | solution.py:23
  72.2 1.3 %collective-permute-start.29 = (bf16[32,2560]{1,0:T(8,128)(2,1)S(1)}, bf16[32,2560]{1,0:T(8,128)(2,1)S(1)}, u32[]{:S(2)}, u32[]{:S(2)}) collective-permute-start(bf16[32,2560]{1,0:T(8,128)(2,1)S(1)} %add_convert_fusion.1), channel_id=1, source_target_pairs={{0,4},{1,5},{2,6},{3,7},{4,0},{5,1},{6,2},{7,3},{8,12},{9,13},{10,... | collective-permute-start | bytes 491528 | tf_op jit(solution)/shard_map/ppermute | solution.py:23
  74.6 8.2 %write_pool.1 = bf16[64,128,512]{2,1,0:T(8,128)(2,1)} custom-call(s32[3,32]{1,0:T(4,128)S(1)} %pad_add_fusion.1.patches, s32[16]{0:T(128)S(1)} %copy-done.1, bf16[64,512]{1,0:T(8,128)(2,1)S(1)} %get-tuple-element.58.fresh, bf16[64,128,512]{2,1,0:T(8,128)(2,1)} %source.1), custom_call_target="tpu_custom_call" | custom-call | bytes 16777216 | tf_op jit(solution)/shard_map/write_pool/pallas_call | solution.py:103
  83.1 1.4 %collective-permute-done.31 = bf16[8,4,2560]{2,1,0:T(4,128)(2,1)S(1)} collective-permute-done((bf16[8,4,2560]{2,1,0:T(4,128)(2,1)S(1)}, bf16[8,4,2560]{2,1,0:T(4,128)(2,1)S(1)}, u32[]{:S(2)}, u32[]{:S(2)}) %collective-permute-start.31) | collective-permute-done | bytes 163872 | tf_op jit(solution)/shard_map/ppermute | solution.py:23
  (107 shorter events, 23.6 us)
Async XLA Ops:
  1.6 7.8 %collective-permute-start = (bf16[4,4,2560]{2,1,0:T(4,128)(2,1)S(1)}, bf16[4,4,2560]{2,1,0:T(4,128)(2,1)S(1)}, u32[]{:S(2)}, u32[]{:S(2)}) collective-permute-start(bf16[4,4,2560]{2,1,0:T(4,128)(2,1)S(1)} %constant_dynamic-slice_fusion), channel_id=1, source_target_pairs={{0,16},{8,24},{16,0},{24,8},{1,17},{9,25},{17,1},{25,9},{2,18},{10... | collective-permute-start | bytes 245768 | tf_op jit(solution)/shard_map/ppermute | solution.py:23
  5.7 13.5 %collective-permute-start.3 = (bf16[96,2560]{1,0:T(8,128)(2,1)}, bf16[96,2560]{1,0:T(8,128)(2,1)S(1)}, u32[]{:S(2)}, u32[]{:S(2)}) collective-permute-start(bf16[96,2560]{1,0:T(8,128)(2,1)} %param.12), channel_id=1, source_target_pairs={{0,8},{8,0},{16,24},{24,16},{1,9},{9,1},{17,25},{25,17},{2,10},{10... | collective-permute-start | bytes 1474568 | tf_op jit(solution)/shard_map/ppermute | solution.py:23
  9.5 4.5 %collective-permute-start.1 = (bf16[4,4,2560]{2,1,0:T(4,128)(2,1)S(1)}, bf16[4,4,2560]{2,1,0:T(4,128)(2,1)S(1)}, u32[]{:S(2)}, u32[]{:S(2)}) collective-permute-start(bf16[4,4,2560]{2,1,0:T(4,128)(2,1)S(1)} %collective-permute-done), channel_id=1, source_target_pairs={{0,2},{1,3},{2,0},{3,1},{4,6},{5,7},{6,4},{7,5},{8,10},{9,11},{10,... | collective-permute-start | bytes 245768 | tf_op jit(solution)/shard_map/ppermute | solution.py:23
  19.7 5.0 %collective-permute-start.4 = (bf16[64,192]{1,0:T(8,128)(2,1)S(1)}, bf16[64,192]{1,0:T(8,128)(2,1)S(1)}, u32[]{:S(2)}, u32[]{:S(2)}) collective-permute-start(bf16[64,192]{1,0:T(8,128)(2,1)S(1)} %slice.60), channel_id=1, source_target_pairs={{0,16},{8,24},{16,0},{24,8},{1,17},{9,25},{17,1},{25,9},{2,18},{10... | collective-permute-start | bytes 73736 | tf_op jit(solution)/shard_map/ppermute | solution.py:23
  21.0 20.3 %collective-permute-start.13 = (bf16[80,2560]{1,0:T(8,128)(2,1)S(1)}, bf16[80,2560]{1,0:T(8,128)(2,1)S(1)}, u32[]{:S(2)}, u32[]{:S(2)}) collective-permute-start(bf16[80,2560]{1,0:T(8,128)(2,1)S(1)} %copy-done), channel_id=1, source_target_pairs={{0,8},{8,0},{16,24},{24,16},{1,9},{9,1},{17,25},{25,17},{2,10},{10... | collective-permute-start | bytes 1228808 | tf_op jit(solution)/shard_map/ppermute | solution.py:23
  23.1 19.7 %collective-permute-start.14 = (bf16[80,2560]{1,0:T(8,128)(2,1)S(1)}, bf16[80,2560]{1,0:T(8,128)(2,1)S(1)}, u32[]{:S(2)}, u32[]{:S(2)}) collective-permute-start(bf16[80,2560]{1,0:T(8,128)(2,1)S(1)} %copy-done), channel_id=1, source_target_pairs={{0,16},{8,24},{16,0},{24,8},{1,17},{9,25},{17,1},{25,9},{2,18},{10... | collective-permute-start | bytes 1228808 | tf_op jit(solution)/shard_map/ppermute | solution.py:23
  24.8 5.0 %collective-permute-start.10 = (bf16[64,384]{1,0:T(8,128)(2,1)S(1)}, bf16[64,384]{1,0:T(8,128)(2,1)S(1)}, u32[]{:S(2)}, u32[]{:S(2)}) collective-permute-start(bf16[64,384]{1,0:T(8,128)(2,1)S(1)} %pad_maximum_fusion.1.refs_0_), channel_id=1, source_target_pairs={{0,6},{1,7},{2,4},{3,5},{4,2},{5,3},{6,0},{7,1},{8,14},{9,15},{10,... | collective-permute-start | bytes 147464 | tf_op jit(solution)/shard_map/ppermute | solution.py:23
  27.8 4.2 %collective-permute-start.6 = (bf16[64,384]{1,0:T(8,128)(2,1)S(1)}, bf16[64,384]{1,0:T(8,128)(2,1)S(1)}, u32[]{:S(2)}, u32[]{:S(2)}) collective-permute-start(bf16[64,384]{1,0:T(8,128)(2,1)S(1)} %pad_maximum_fusion.1.refs_0_), channel_id=1, source_target_pairs={{0,2},{1,3},{2,0},{3,1},{4,6},{5,7},{6,4},{7,5},{8,10},{9,11},{10,... | collective-permute-start | bytes 147464 | tf_op jit(solution)/shard_map/ppermute | solution.py:23
  28.4 4.1 %collective-permute-start.8 = (bf16[64,384]{1,0:T(8,128)(2,1)S(1)}, bf16[64,384]{1,0:T(8,128)(2,1)S(1)}, u32[]{:S(2)}, u32[]{:S(2)}) collective-permute-start(bf16[64,384]{1,0:T(8,128)(2,1)S(1)} %pad_maximum_fusion.1.refs_0_), channel_id=1, source_target_pairs={{0,4},{1,5},{2,6},{3,7},{4,0},{5,1},{6,2},{7,3},{8,12},{9,13},{10,... | collective-permute-start | bytes 147464 | tf_op jit(solution)/shard_map/ppermute | solution.py:23
  29.9 2.7 %collective-permute-start.5 = (bf16[64,384]{1,0:T(8,128)(2,1)S(1)}, bf16[64,384]{1,0:T(8,128)(2,1)S(1)}, u32[]{:S(2)}, u32[]{:S(2)}) collective-permute-start(bf16[64,384]{1,0:T(8,128)(2,1)S(1)} %pad_maximum_fusion.1.refs_0_), channel_id=1, source_target_pairs={{0,1},{1,0},{2,3},{3,2},{4,5},{5,4},{6,7},{7,6},{8,9},{9,8},{10,11... | collective-permute-start | bytes 147464 | tf_op jit(solution)/shard_map/ppermute | solution.py:23
  39.6 1.5 %collective-permute-start.12 = (bf16[336,256]{1,0:T(8,128)(2,1)S(1)}, bf16[336,256]{1,0:T(8,128)(2,1)S(1)}, u32[]{:S(2)}, u32[]{:S(2)}) collective-permute-start(bf16[336,256]{1,0:T(8,128)(2,1)S(1)} %get-tuple-element.40), channel_id=1, source_target_pairs={{0,1},{1,0},{2,3},{3,2},{4,5},{5,4},{6,7},{7,6},{8,9},{9,8},{10,11... | collective-permute-start | bytes 516104 | tf_op jit(solution)/shard_map/ppermute | solution.py:23
  42.8 11.4 %collective-permute-start.18 = (bf16[80,2560]{1,0:T(8,128)(2,1)S(1)}, bf16[80,2560]{1,0:T(8,128)(2,1)S(1)}, u32[]{:S(2)}, u32[]{:S(2)}) collective-permute-start(bf16[80,2560]{1,0:T(8,128)(2,1)S(1)} %collective-permute-done.14.refs_2_), channel_id=1, source_target_pairs={{0,8},{8,0},{16,24},{24,16},{1,9},{9,1},{17,25},{25,17},{2,10},{10... | collective-permute-start | bytes 1228808 | tf_op jit(solution)/shard_map/ppermute | solution.py:23
  43.0 8.8 %collective-permute-start.15 = (bf16[336,256]{1,0:T(8,128)(2,1)S(1)}, bf16[336,256]{1,0:T(8,128)(2,1)S(1)}, u32[]{:S(2)}, u32[]{:S(2)}) collective-permute-start(bf16[336,256]{1,0:T(8,128)(2,1)S(1)} %merge_pair.1.after.refs_0_), channel_id=1, source_target_pairs={{0,2},{1,3},{2,0},{3,1},{4,6},{5,7},{6,4},{7,5},{8,10},{9,11},{10,... | collective-permute-start | bytes 516104 | tf_op jit(solution)/shard_map/ppermute | solution.py:23
  44.4 9.7 %collective-permute-start.16 = (bf16[336,256]{1,0:T(8,128)(2,1)S(1)}, bf16[336,256]{1,0:T(8,128)(2,1)S(1)}, u32[]{:S(2)}, u32[]{:S(2)}) collective-permute-start(bf16[336,256]{1,0:T(8,128)(2,1)S(1)} %merge_pair.1.after.refs_0_), channel_id=1, source_target_pairs={{0,4},{1,5},{2,6},{3,7},{4,0},{5,1},{6,2},{7,3},{8,12},{9,13},{10,... | collective-permute-start | bytes 516104 | tf_op jit(solution)/shard_map/ppermute | solution.py:23
  45.8 8.3 %collective-permute-start.17 = (bf16[336,256]{1,0:T(8,128)(2,1)S(1)}, bf16[336,256]{1,0:T(8,128)(2,1)S(1)}, u32[]{:S(2)}, u32[]{:S(2)}) collective-permute-start(bf16[336,256]{1,0:T(8,128)(2,1)S(1)} %merge_pair.1.after.refs_0_), channel_id=1, source_target_pairs={{0,6},{1,7},{2,4},{3,5},{4,2},{5,3},{6,0},{7,1},{8,14},{9,15},{10,... | collective-permute-start | bytes 516104 | tf_op jit(solution)/shard_map/ppermute | solution.py:23
  57.2 4.2 %collective-permute-start.21 = (bf16[64,320]{1,0:T(8,128)(2,1)S(1)}, bf16[64,320]{1,0:T(8,128)(2,1)S(1)}, u32[]{:S(2)}, u32[]{:S(2)}) collective-permute-start(bf16[64,320]{1,0:T(8,128)(2,1)S(1)} %project_out.1.refs_0_), channel_id=1, source_target_pairs={{0,2},{1,3},{2,0},{3,1},{4,6},{5,7},{6,4},{7,5},{8,10},{9,11},{10,... | collective-permute-start | bytes 122888 | tf_op jit(solution)/shard_map/ppermute | solution.py:23
  57.9 4.1 %collective-permute-start.23 = (bf16[64,320]{1,0:T(8,128)(2,1)S(1)}, bf16[64,320]{1,0:T(8,128)(2,1)S(1)}, u32[]{:S(2)}, u32[]{:S(2)}) collective-permute-start(bf16[64,320]{1,0:T(8,128)(2,1)S(1)} %project_out.1.refs_0_), channel_id=1, source_target_pairs={{0,4},{1,5},{2,6},{3,7},{4,0},{5,1},{6,2},{7,3},{8,12},{9,13},{10,... | collective-permute-start | bytes 122888 | tf_op jit(solution)/shard_map/ppermute | solution.py:23
  59.0 5.0 %collective-permute-start.25 = (bf16[64,320]{1,0:T(8,128)(2,1)S(1)}, bf16[64,320]{1,0:T(8,128)(2,1)S(1)}, u32[]{:S(2)}, u32[]{:S(2)}) collective-permute-start(bf16[64,320]{1,0:T(8,128)(2,1)S(1)} %project_out.1.refs_0_), channel_id=1, source_target_pairs={{0,6},{1,7},{2,4},{3,5},{4,2},{5,3},{6,0},{7,1},{8,14},{9,15},{10,... | collective-permute-start | bytes 122888 | tf_op jit(solution)/shard_map/ppermute | solution.py:23
  60.7 3.3 %collective-permute-start.20 = (bf16[64,320]{1,0:T(8,128)(2,1)S(1)}, bf16[64,320]{1,0:T(8,128)(2,1)S(1)}, u32[]{:S(2)}, u32[]{:S(2)}) collective-permute-start(bf16[64,320]{1,0:T(8,128)(2,1)S(1)} %project_out.1.refs_0_), channel_id=1, source_target_pairs={{0,1},{1,0},{2,3},{3,2},{4,5},{5,4},{6,7},{7,6},{8,9},{9,8},{10,11... | collective-permute-start | bytes 122888 | tf_op jit(solution)/shard_map/ppermute | solution.py:23
  61.3 2.7 %collective-permute-start.22 = (bf16[64,320]{1,0:T(8,128)(2,1)S(1)}, bf16[64,320]{1,0:T(8,128)(2,1)S(1)}, u32[]{:S(2)}, u32[]{:S(2)}) collective-permute-start(bf16[64,320]{1,0:T(8,128)(2,1)S(1)} %collective-permute-done.21.refs_2_), channel_id=1, source_target_pairs={{0,1},{1,0},{2,3},{3,2},{4,5},{5,4},{6,7},{7,6},{8,9},{9,8},{10,11... | collective-permute-start | bytes 122888 | tf_op jit(solution)/shard_map/ppermute | solution.py:23
  62.0 2.0 %collective-permute-start.24 = (bf16[64,320]{1,0:T(8,128)(2,1)S(1)}, bf16[64,320]{1,0:T(8,128)(2,1)S(1)}, u32[]{:S(2)}, u32[]{:S(2)}) collective-permute-start(bf16[64,320]{1,0:T(8,128)(2,1)S(1)} %collective-permute-done.23.refs_4_), channel_id=1, source_target_pairs={{0,1},{1,0},{2,3},{3,2},{4,5},{5,4},{6,7},{7,6},{8,9},{9,8},{10,11... | collective-permute-start | bytes 122888 | tf_op jit(solution)/shard_map/ppermute | solution.py:23
  71.1 11.7 %collective-permute-start.28 = (bf16[32,2560]{1,0:T(8,128)(2,1)S(1)}, bf16[32,2560]{1,0:T(8,128)(2,1)S(1)}, u32[]{:S(2)}, u32[]{:S(2)}) collective-permute-start(bf16[32,2560]{1,0:T(8,128)(2,1)S(1)} %add_convert_fusion.1), channel_id=1, source_target_pairs={{0,2},{1,3},{2,0},{3,1},{4,6},{5,7},{6,4},{7,5},{8,10},{9,11},{10,... | collective-permute-start | bytes 491528 | tf_op jit(solution)/shard_map/ppermute | solution.py:23
  72.2 10.6 %collective-permute-start.29 = (bf16[32,2560]{1,0:T(8,128)(2,1)S(1)}, bf16[32,2560]{1,0:T(8,128)(2,1)S(1)}, u32[]{:S(2)}, u32[]{:S(2)}) collective-permute-start(bf16[32,2560]{1,0:T(8,128)(2,1)S(1)} %add_convert_fusion.1), channel_id=1, source_target_pairs={{0,4},{1,5},{2,6},{3,7},{4,0},{5,1},{6,2},{7,3},{8,12},{9,13},{10,... | collective-permute-start | bytes 491528 | tf_op jit(solution)/shard_map/ppermute | solution.py:23
  73.5 9.4 %collective-permute-start.30 = (bf16[32,2560]{1,0:T(8,128)(2,1)S(1)}, bf16[32,2560]{1,0:T(8,128)(2,1)S(1)}, u32[]{:S(2)}, u32[]{:S(2)}) collective-permute-start(bf16[32,2560]{1,0:T(8,128)(2,1)S(1)} %add_convert_fusion.1), channel_id=1, source_target_pairs={{0,6},{1,7},{2,4},{3,5},{4,2},{5,3},{6,0},{7,1},{8,14},{9,15},{10,... | collective-permute-start | bytes 491528 | tf_op jit(solution)/shard_map/ppermute | solution.py:23
  (14 other events, 56.1 us)

commit v6 on v5

--- a/solution.py
+++ b/solution.py
@@ -48,7 +48,8 @@
     return scratch
 
 
-def write_kernel(dims, parts, patches, lengths, fresh, source, target, buffer, in_sems, out_sems):
+def write_kernel(dims, parts, patch_source, fresh, source, target, buffer, patches, *sems):
+    patch_sem, in_sems, out_sems = sems
     requests, new_count, heads, pages, page_len, window, chunk, n_seq = dims
     lines = requests * new_count
     count = pages // parts
@@ -61,20 +62,21 @@
         pltpu.make_async_copy(buffer.at[span], target.at[span], out_sems.at[i])
         for i, span in enumerate(spans)
     ]
+    patch_load = pltpu.make_async_copy(patch_source, patches, patch_sem)
+    patch_load.start()
     for load in loads:
         load.start()
-    for load in loads:
-        load.wait()
-
-    def write_patch(i, carry):
+    patch_load.wait()
+
+    def write_patch(part, i):
         slot = patches[0, i]
 
-        @pl.when(slot >= 0)
+        @pl.when((slot >= part * count) & (slot < (part + 1) * count))
         def _():
             r = i // 2
             row = pl.multiple_of(patches[1, i] * 16, 16)
             old = buffer[slot, pl.ds(row, 16), :]
-            first = patches[2, i] * page_len + row - lengths[r]
+            first = patches[2, i] * page_len + row - patches[3, i]
             line = lax.broadcasted_iota(jnp.int32, (16, lines), 0)
             token = jnp.bitwise_and(first + line, window - 1)
             column = lax.broadcasted_iota(jnp.int32, (16, lines), 1)
@@ -87,26 +89,30 @@
                 row_token < new_count, new, old.astype(f32)
             ).astype(bf16)
 
-        return carry
-
-    lax.fori_loop(0, 2 * requests, write_patch, 0)
-    for store in stores:
+    for part, (load, store) in enumerate(zip(loads, stores)):
+        load.wait()
+        pl.loop(0, 2 * requests)(functools.partial(write_patch, part))
         store.start()
     for store in stores:
         store.wait()
 
 
-def write_pool(dims, patches, lengths, fresh, kv_pool):
-    parts = min(16, kv_pool.shape[0])
-    smem = pl.BlockSpec(memory_space=pltpu.SMEM)
+def write_pool(dims, patches, fresh, kv_pool):
+    parts = 4
     hbm = pl.BlockSpec(memory_space=pltpu.HBM)
     return pl.pallas_call(
         functools.partial(write_kernel, dims, parts),
         out_shape=pltpu.HBM(kv_pool.shape, kv_pool.dtype),
-        in_specs=[smem, smem, pl.BlockSpec(memory_space=pltpu.VMEM), hbm],
+        in_specs=[
+            pl.BlockSpec(memory_space=pl.ANY),
+            pl.BlockSpec(memory_space=pltpu.VMEM),
+            hbm,
+        ],
         out_specs=hbm,
         scratch_shapes=[
             pltpu.VMEM(kv_pool.shape, kv_pool.dtype),
+            pltpu.SMEM(patches.shape, jnp.int32),
+            pltpu.SemaphoreType.DMA,
             pltpu.SemaphoreType.DMA((parts,)),
             pltpu.SemaphoreType.DMA((parts,)),
         ],
@@ -115,7 +121,7 @@
             flops=0, bytes_accessed=2 * kv_pool.size * 2, transcendentals=0
         ),
         name="write_pool",
-    )(patches, lengths, fresh, kv_pool)
+    )(patches, fresh, kv_pool)
 
 
 def split_three(values):
@@ -221,11 +227,13 @@
     )(*packs, token)
 
 
-def attention_kernel(dims, count, slots, place, cosine, sine, *refs):
+def attention_kernel(dims, count, slot_source, cosine, sine, *refs):
     requests, new_count, heads, pages, page_len, window, chunk, n_seq = dims
     pieces, refs = refs[:count], refs[count:]
     pool, mine, theirs, fresh, buffer, gathered, projected = refs[:7]
-    query_low, query_high, queries, peak, norm, total, in_sems = refs[7:]
+    query_low, query_high, queries, peak, norm, total, slots, slot_sem, in_sems = refs[7:]
+    slot_load = pltpu.make_async_copy(slot_source, slots, slot_sem)
+    slot_load.start()
     rows = new_count * heads
     lines = requests * new_count
 
@@ -236,7 +244,8 @@
     for c in range(pages // chunk):
         load(c).start()
 
-    ordered_pieces = place_pieces(place[0], pieces, gathered)
+    me = lax.axis_index("seq")
+    ordered_pieces = place_pieces(me, pieces, gathered)
     part_columns = projected.shape[1] // n_seq
     for i in range(n_seq):
         projected[:, i * part_columns : (i + 1) * part_columns] = ordered_pieces[i]
@@ -293,7 +302,6 @@
             [keep, keep], axis=1
         ) + mixed * jnp.concatenate([take, take], axis=1)
 
-    me = place[0]
     fresh_lane = lax.broadcasted_iota(jnp.int32, (1, lines), 1)
     for step in range(-(-requests // n_seq)):
         r = me + step * n_seq
@@ -304,6 +312,8 @@
             seen = (index >= 0) & (index <= token_of)
             top, amount, weights = weigh(score(r, fresh[:, 0:256]), seen)
             add(r, top, amount, mix(weights, fresh[:, 256:512]))
+
+    slot_load.wait()
 
     def chunk_scores(c):
         load(c).wait()
@@ -331,7 +341,7 @@
             add(slots[0, page], top, amount, values)
 
     half = requests // 2
-    core = place[1]
+    core = me % 2
     for side, out in ((core, mine), (1 - core, theirs)):
         logs = []
         for k in range(half):
@@ -347,18 +357,17 @@
         out[half * rows : half * rows + 16, :] = pack_logs(logs, rows).astype(bf16)
 
 
-def attention(dims, slots, place, cosine, sine, pieces, pool):
+def attention(dims, slots, cosine, sine, pieces, pool):
     requests, new_count, heads, pages, page_len, window, chunk, n_seq = dims
     part_columns = pieces[0].shape[-1]
     lines = requests * new_count
     rows = new_count * heads
-    smem = pl.BlockSpec(memory_space=pltpu.SMEM)
     vmem = pl.BlockSpec(memory_space=pltpu.VMEM)
     pack = jax.ShapeDtypeStruct((requests // 2 * rows + 16, 256), bf16)
     return pl.pallas_call(
         functools.partial(attention_kernel, dims, len(pieces)),
         out_shape=(pack, pack, jax.ShapeDtypeStruct((requests * new_count, 512), bf16)),
-        in_specs=[smem, smem, vmem, vmem]
+        in_specs=[pl.BlockSpec(memory_space=pl.ANY), vmem, vmem]
         + [vmem] * len(pieces)
         + [pl.BlockSpec(memory_space=pltpu.HBM)],
         out_specs=(vmem, vmem, vmem),
@@ -372,20 +381,31 @@
             pltpu.VMEM((requests * rows, 128), f32),
             pltpu.VMEM((requests * rows, 128), f32),
             pltpu.VMEM((requests * rows, 256), f32),
+            pltpu.SMEM(slots.shape, jnp.int32),
+            pltpu.SemaphoreType.DMA,
             pltpu.SemaphoreType.DMA((pages // chunk,)),
         ],
         compiler_params=pltpu.CompilerParams(vmem_limit_bytes=20 * 1024 * 1024),
         cost_estimate=pl.CostEstimate(flops=0, bytes_accessed=1024, transcendentals=0),
         name="page_attention",
-    )(slots, place, cosine, sine, *pieces, pool)
-
-
-def project_kernel(count, place, mine, other, *refs):
-    blocks, out = refs[:count], refs[count]
-    core, plane = place[1], place[2]
+    )(slots, cosine, sine, *pieces, pool)
+
+
+def project_kernel(count, joined, mine, other, *refs):
+    blocks, out, scratch = refs[:count], refs[count], refs[count + 1]
+    core, plane = lax.axis_index("seq") % 2, lax.axis_index("dp")
     low = jnp.where(core == 0, mine[...], other[...])
     high = jnp.where(core == 0, other[...], mine[...])
     attended = jnp.concatenate([low, high], axis=0)
+    if joined:
+        rows = blocks[0].shape[0]
+        for k, block in enumerate(blocks):
+            span = pl.ds(pl.multiple_of((plane ^ k) * rows, 16), rows)
+            scratch[span, :] = block[...]
+        out[...] = lax.dot_general(
+            attended, scratch[...], contract, preferred_element_type=f32
+        ).astype(bf16)
+        return
     products = [
         lax.dot_general(attended, block[...], contract, preferred_element_type=f32)
         for block in blocks
@@ -399,17 +419,19 @@
     out[...] = jnp.concatenate(columns, axis=1).astype(bf16)
 
 
-def project_out(place, mine, other, blocks):
+def project_out(mine, other, blocks):
     vmem = pl.BlockSpec(memory_space=pltpu.VMEM)
-    shape = (2 * mine.shape[0], len(blocks) * blocks[0].shape[0])
+    rows, width = blocks[0].shape
+    total = len(blocks) * rows
     return pl.pallas_call(
-        functools.partial(project_kernel, len(blocks)),
-        out_shape=jax.ShapeDtypeStruct(shape, bf16),
-        in_specs=[pl.BlockSpec(memory_space=pltpu.SMEM)] + [vmem] * (2 + len(blocks)),
+        functools.partial(project_kernel, len(blocks), rows % 16 == 0),
+        out_shape=jax.ShapeDtypeStruct((2 * mine.shape[0], total), bf16),
+        in_specs=[vmem] * (2 + len(blocks)),
         out_specs=vmem,
+        scratch_shapes=[pltpu.VMEM((-(-total // 16) * 16, width), bf16)],
         compiler_params=pltpu.CompilerParams(vmem_limit_bytes=8 * 1024 * 1024),
         name="project_out",
-    )(place, mine, other, *blocks)
+    )(mine, other, *blocks)
 
 
 def fetch_kernel(parts, gate_up, down, after, gates, downs, token, sems):
@@ -454,11 +476,12 @@
     )
 
 
-def mlp_kernel(chunk, pieces, place, stream, gain, gates, downs, *refs):
+def mlp_kernel(chunk, pieces, stream, gain, gates, downs, *refs):
     heads_out, refs = refs[:pieces], refs[pieces:]
     keep, give, kept_residual, residual, total, heads_scratch = refs
     units, width = downs.shape
-    heads_out = place_pieces(place[0], heads_out, heads_scratch)
+    me = lax.axis_index("seq")
+    heads_out = place_pieces(me, heads_out, heads_scratch)
     count = units // chunk
     gathered = jnp.concatenate(
         [heads_out[i].astype(f32) for i in range(heads_out.shape[0])], axis=1
@@ -492,14 +515,14 @@
         before = after
     fall(count - 1, before)
     half = total.shape[0] // 2
-    core = place[1]
+    core = me % 2
     mine = pl.ds(pl.multiple_of(core * half, 8), half)
     keep[...] = total[mine, :]
     kept_residual[...] = residual[mine, :].astype(bf16)
     give[...] = total[pl.ds(pl.multiple_of((1 - core) * half, 8), half), :].astype(bf16)
 
 
-def feed_forward(n_seq, place, stream, heads_out, gain, gates, downs):
+def feed_forward(n_seq, stream, heads_out, gain, gates, downs):
     lines, width = stream.shape
     units = downs.shape[0]
     chunk = max(c for c in range(16, 512, 16) if units % c == 0)
@@ -511,7 +534,7 @@
             jax.ShapeDtypeStruct((lines // 2, width), bf16),
             jax.ShapeDtypeStruct((lines // 2, width), bf16),
         ),
-        in_specs=[pl.BlockSpec(memory_space=pltpu.SMEM)] + [vmem] * (4 + len(heads_out)),
+        in_specs=[vmem] * (4 + len(heads_out)),
         out_specs=(vmem, vmem, vmem),
         scratch_shapes=[
             pltpu.VMEM((lines, width), f32),
@@ -520,7 +543,7 @@
         ],
         compiler_params=pltpu.CompilerParams(vmem_limit_bytes=12 * 1024 * 1024),
         name="feed_forward",
-    )(place, stream, gain.reshape(1, width), gates, downs, *heads_out)
+    )(stream, gain.reshape(1, width), gates, downs, *heads_out)
 
 
 def body(
@@ -643,15 +666,14 @@
             jnp.where(good, end_slot, -1).reshape(-1),
             end_block.reshape(-1),
             end_page.reshape(-1),
+            jnp.repeat(cache_len, 2),
         ]
     )
 
     dims = (requests, new_count, heads, pages, page_len, window, min(16, pages), n_seq)
-    place, slots, patches, lengths = lax.optimization_barrier(
-        (jnp.stack([seq_index, core, dp_index]), slots, patches, cache_len)
-    )
-    mine, theirs, fresh = attention(dims, slots, place, cosine, sine, pieces, held_pool)
-    written_pool = write_pool(dims, patches, lengths, fresh, held_pool)
+    slots, patches = lax.optimization_barrier((slots, patches))
+    mine, theirs, fresh = attention(dims, slots, cosine, sine, pieces, held_pool)
+    written_pool = write_pool(dims, patches, fresh, held_pool)
 
     side = requests // 2
     merged = merge_pair(mine, swap(theirs, "seq", n_seq, 1), side, rows)
@@ -667,15 +689,12 @@
         out_blocks[k ^ 1] = block
     attended_half = merge_final(packs, token, side, rows, heads)
     heads_part = project_out(
-        place,
         attended_half,
         swap(attended_half, "seq", n_seq, 1),
         [out_blocks[k] for k in range(n_dp)],
     )
     heads_out = gather_pieces(heads_part, n_seq)
-    keep, give, my_residual = feed_forward(
-        n_seq, place, stream, heads_out, mlp_gain, gates, downs
-    )
+    keep, give, my_residual = feed_forward(n_seq, stream, heads_out, mlp_gain, gates, downs)
     chip_sum = (keep + swap(give, "seq", n_seq, 1).astype(f32)).astype(bf16)
     terms = [chip_sum] + [swap(chip_sum, "seq", n_seq, 2 * c) for c in range(1, chips)]
     terms, written_pool = lax.optimization_barrier((terms, written_pool))

time: 85.8 us -> 83.3 us (0.971)
  Pallas kernels: 25.3 us -> 21.5 us
  waiting for transfers between devices: 25 us -> 26.5 us
    pallas_call x1, Pallas kernels: 8.18 us -> 5.96 us  [write_pool(): pl.pallas_call(functools.partial(write_kernel, dims, parts), out_shape=pl...]
    ppermute x32, waiting for transfers between devices: 25 us -> 26.5 us  [swap(): return lax.ppermute(values, axis, [(i, i ^ mask) for i in range(size)])]
  transfers between devices with their start and end apart: 32 -> 32, of which waited for: 21 -> 22; matrix products, arithmetic and copies ran while one was open for 4% -> 4% of each run, Pallas kernels for 23% -> 20%
where the time goes in v6:
time: 83.3 us; the launch traced here: 83.1 us
  starting transfers between devices  27.8 us (33%)
  waiting for transfers between devices  26.5 us (32%)
  Pallas kernels  21.5 us (26%)
  local copies, waits for them, and re-layouts  2.85 us (3%)
  other arithmetic  2.56 us (3%)
  between operations  1.12 us (1%)
    ppermute x32, starting transfers between devices, swap(): return lax.ppermute(values, axis, [(i, i ^ mask) for i in range(size)])  27.8 us
    ppermute x32, waiting for transfers between devices, swap(): return lax.ppermute(values, axis, [(i, i ^ mask) for i in range(size)])  26.5 us
    pallas_call x1, Pallas kernels, write_pool(): pl.pallas_call(functools.partial(write_kernel, dims, parts), out_shape=pl...  5.96 us
    pallas_call x1, Pallas kernels, fetch_weights(): pl.pallas_call(functools.partial(fetch_kernel, parts), out_shape=(jax.Sha...  5.33 us
    pallas_call x1, Pallas kernels, attention(): pl.pallas_call(functools.partial(attention_kernel, dims, len(pieces)), ou...  5 us
    pallas_call x1, Pallas kernels, feed_forward(): pl.pallas_call(functools.partial(mlp_kernel, chunk, len(heads_out)), out_...  3.88 us
  transfers between devices with their start and end apart: 32, of which 22 were waited for; matrix products, arithmetic and copies ran while one was open for 4% of the time, Pallas kernels for 20%

profile of v6, /device:TPU:0, one launch (start us, length us, event | category | flops | bytes accessed | tf_op | source)
XLA Modules:
  0.0 83.1 jit_solution(5251246751157968947)
XLA Ops:
  1.6 4.1 %collective-permute-start = (bf16[4,4,2560]{2,1,0:T(4,128)(2,1)S(1)}, bf16[4,4,2560]{2,1,0:T(4,128)(2,1)S(1)}, u32[]{:S(2)}, u32[]{:S(2)}) collective-permute-start(bf16[4,4,2560]{2,1,0:T(4,128)(2,1)S(1)} %constant_dynamic-slice_fusion), channel_id=1, source_target_pairs={{0,16},{8,24},{16,0},{24,8},{1,17},{9,25},{17,1},{25,9},{2,18},{10... | collective-permute-start | bytes 245768 | tf_op jit(solution)/shard_map/ppermute | solution.py:23
  5.7 1.6 %collective-permute-start.3 = (bf16[96,2560]{1,0:T(8,128)(2,1)}, bf16[96,2560]{1,0:T(8,128)(2,1)S(1)}, u32[]{:S(2)}, u32[]{:S(2)}) collective-permute-start(bf16[96,2560]{1,0:T(8,128)(2,1)} %param.12), channel_id=1, source_target_pairs={{0,8},{8,0},{16,24},{24,16},{1,9},{9,1},{17,25},{25,17},{2,10},{10... | collective-permute-start | bytes 1474568 | tf_op jit(solution)/shard_map/ppermute | solution.py:23
  9.5 1.9 %collective-permute-start.1 = (bf16[4,4,2560]{2,1,0:T(4,128)(2,1)S(1)}, bf16[4,4,2560]{2,1,0:T(4,128)(2,1)S(1)}, u32[]{:S(2)}, u32[]{:S(2)}) collective-permute-start(bf16[4,4,2560]{2,1,0:T(4,128)(2,1)S(1)} %collective-permute-done), channel_id=1, source_target_pairs={{0,2},{1,3},{2,0},{3,1},{4,6},{5,7},{6,4},{7,5},{8,10},{9,11},{10,... | collective-permute-start | bytes 245768 | tf_op jit(solution)/shard_map/ppermute | solution.py:23
  12.2 1.7 %collective-permute-done.1 = bf16[4,4,2560]{2,1,0:T(4,128)(2,1)S(1)} collective-permute-done((bf16[4,4,2560]{2,1,0:T(4,128)(2,1)S(1)}, bf16[4,4,2560]{2,1,0:T(4,128)(2,1)S(1)}, u32[]{:S(2)}, u32[]{:S(2)}) %collective-permute-start.1) | collective-permute-done | bytes 81952 | tf_op jit(solution)/shard_map/ppermute | solution.py:23
  14.2 1.3 %collective-permute-done.2 = bf16[8,4,2560]{2,1,0:T(4,128)(2,1)S(1)} collective-permute-done((bf16[8,4,2560]{2,1,0:T(4,128)(2,1)S(1)}, bf16[8,4,2560]{2,1,0:T(4,128)(2,1)S(1)}, u32[]{:S(2)}, u32[]{:S(2)}) %collective-permute-start.2) | collective-permute-done | bytes 163872 | tf_op jit(solution)/shard_map/ppermute | solution.py:23
  16.4 2.8 %collective-permute-done.3 = bf16[96,2560]{1,0:T(8,128)(2,1)S(1)} collective-permute-done((bf16[96,2560]{1,0:T(8,128)(2,1)}, bf16[96,2560]{1,0:T(8,128)(2,1)S(1)}, u32[]{:S(2)}, u32[]{:S(2)}) %collective-permute-start.3) | collective-permute-done | bytes 491552 | tf_op jit(solution)/shard_map/ppermute | solution.py:23
  21.0 2.0 %collective-permute-start.13 = (bf16[80,2560]{1,0:T(8,128)(2,1)S(1)}, bf16[80,2560]{1,0:T(8,128)(2,1)S(1)}, u32[]{:S(2)}, u32[]{:S(2)}) collective-permute-start(bf16[80,2560]{1,0:T(8,128)(2,1)S(1)} %copy-done), channel_id=1, source_target_pairs={{0,8},{8,0},{16,24},{24,16},{1,9},{9,1},{17,25},{25,17},{2,10},{10... | collective-permute-start | bytes 1228808 | tf_op jit(solution)/shard_map/ppermute | solution.py:23
  24.8 2.7 %collective-permute-start.10 = (bf16[64,384]{1,0:T(8,128)(2,1)S(1)}, bf16[64,384]{1,0:T(8,128)(2,1)S(1)}, u32[]{:S(2)}, u32[]{:S(2)}) collective-permute-start(bf16[64,384]{1,0:T(8,128)(2,1)S(1)} %pad_maximum_fusion.1.refs_0_), channel_id=1, source_target_pairs={{0,6},{1,7},{2,4},{3,5},{4,2},{5,3},{6,0},{7,1},{8,14},{9,15},{10,... | collective-permute-start | bytes 147464 | tf_op jit(solution)/shard_map/ppermute | solution.py:23
  28.5 1.3 %collective-permute-done.10.refs_6_ = bf16[64,384]{1,0:T(8,128)(2,1)S(1)} collective-permute-done((bf16[64,384]{1,0:T(8,128)(2,1)S(1)}, bf16[64,384]{1,0:T(8,128)(2,1)S(1)}, u32[]{:S(2)}, u32[]{:S(2)}) %collective-permute-start.10) | collective-permute-done | bytes 49184 | tf_op jit(solution)/shard_map/ppermute | solution.py:23
  30.2 1.6 %collective-permute-done.6.refs_2_ = bf16[64,384]{1,0:T(8,128)(2,1)S(1)} collective-permute-done((bf16[64,384]{1,0:T(8,128)(2,1)S(1)}, bf16[64,384]{1,0:T(8,128)(2,1)S(1)}, u32[]{:S(2)}, u32[]{:S(2)}) %collective-permute-start.6) | collective-permute-done | bytes 49184 | tf_op jit(solution)/shard_map/ppermute | solution.py:23
  33.7 5.0 %page_attention.1 = (bf16[336,256]{1,0:T(8,128)(2,1)S(1)}, bf16[336,256]{1,0:T(8,128)(2,1)S(1)}, bf16[64,512]{1,0:T(8,128)(2,1)S(1)}) custom-call(s32[3,64]{1,0:T(4,128)S(1)} %pad_add_fusion.slot_source, f32[64,128]{1,0:T(8,128)S(1)} %get-tuple-element.79.cosine, f32[64,128]{1,0:T(8,128)S(1)} %get-tuple-element.80.sine, ...), custom_call_target="tpu_custom_call" | custom-call | bytes 1024 | tf_op jit(solution)/shard_map/page_attention/pallas_call | solution.py:367
  40.5 2.3 %collective-permute-done.14.refs_2_ = bf16[80,2560]{1,0:T(8,128)(2,1)S(1)} collective-permute-done((bf16[80,2560]{1,0:T(8,128)(2,1)S(1)}, bf16[80,2560]{1,0:T(8,128)(2,1)S(1)}, u32[]{:S(2)}, u32[]{:S(2)}) %collective-permute-start.14) | collective-permute-done | bytes 409632 | tf_op jit(solution)/shard_map/ppermute | solution.py:23
  42.8 1.5 %collective-permute-start.15 = (bf16[336,256]{1,0:T(8,128)(2,1)S(1)}, bf16[336,256]{1,0:T(8,128)(2,1)S(1)}, u32[]{:S(2)}, u32[]{:S(2)}) collective-permute-start(bf16[336,256]{1,0:T(8,128)(2,1)S(1)} %merge_pair.1.after.refs_0_), channel_id=1, source_target_pairs={{0,2},{1,3},{2,0},{3,1},{4,6},{5,7},{6,4},{7,5},{8,10},{9,11},{10,... | collective-permute-start | bytes 516104 | tf_op jit(solution)/shard_map/ppermute | solution.py:23
  44.3 1.5 %collective-permute-start.16 = (bf16[336,256]{1,0:T(8,128)(2,1)S(1)}, bf16[336,256]{1,0:T(8,128)(2,1)S(1)}, u32[]{:S(2)}, u32[]{:S(2)}) collective-permute-start(bf16[336,256]{1,0:T(8,128)(2,1)S(1)} %merge_pair.1.after.refs_0_), channel_id=1, source_target_pairs={{0,4},{1,5},{2,6},{3,7},{4,0},{5,1},{6,2},{7,3},{8,12},{9,13},{10,... | collective-permute-start | bytes 516104 | tf_op jit(solution)/shard_map/ppermute | solution.py:23
  46.3 5.3 %fetch_weights.1 = (bf16[2,960,2560]{2,1,0:T(8,128)(2,1)S(1)}, bf16[960,2560]{1,0:T(8,128)(2,1)S(1)}, f32[8,128]{1,0:T(8,128)S(1)}) custom-call(bf16[2,960,2560]{2,1,0:T(8,128)(2,1)} %gate_up.1, bf16[960,2560]{1,0:T(8,128)(2,1)} %down.1, bf16[336,256]{1,0:T(8,128)(2,1)S(1)} %merge_pair.1.after.refs_0_), custom_call_target="tpu_custom_call" | custom-call | bytes 14745600 | tf_op jit(solution)/shard_map/fetch_weights/pallas_call | solution.py:457
  51.6 1.8 %collective-permute-done.16.refs_2_ = bf16[336,256]{1,0:T(8,128)(2,1)S(1)} collective-permute-done((bf16[336,256]{1,0:T(8,128)(2,1)S(1)}, bf16[336,256]{1,0:T(8,128)(2,1)S(1)}, u32[]{:S(2)}, u32[]{:S(2)}) %collective-permute-start.16) | collective-permute-done | bytes 172064 | tf_op jit(solution)/shard_map/ppermute | solution.py:23
  53.9 1.4 %collective-permute-done.19.other = bf16[32,2560]{1,0:T(8,128)(2,1)S(1)} collective-permute-done((bf16[32,2560]{1,0:T(8,128)(2,1)S(1)}, bf16[32,2560]{1,0:T(8,128)(2,1)S(1)}, u32[]{:S(2)}, u32[]{:S(2)}) %collective-permute-start.19) | collective-permute-done | bytes 163872 | tf_op jit(solution)/shard_map/ppermute | solution.py:23
  56.6 1.5 %collective-permute-start.23 = (bf16[64,320]{1,0:T(8,128)(2,1)S(1)}, bf16[64,320]{1,0:T(8,128)(2,1)S(1)}, u32[]{:S(2)}, u32[]{:S(2)}) collective-permute-start(bf16[64,320]{1,0:T(8,128)(2,1)S(1)} %project_out.1.refs_0_), channel_id=1, source_target_pairs={{0,4},{1,5},{2,6},{3,7},{4,0},{5,1},{6,2},{7,3},{8,12},{9,13},{10,... | collective-permute-start | bytes 122888 | tf_op jit(solution)/shard_map/ppermute | solution.py:23
  58.1 1.5 %collective-permute-start.25 = (bf16[64,320]{1,0:T(8,128)(2,1)S(1)}, bf16[64,320]{1,0:T(8,128)(2,1)S(1)}, u32[]{:S(2)}, u32[]{:S(2)}) collective-permute-start(bf16[64,320]{1,0:T(8,128)(2,1)S(1)} %project_out.1.refs_0_), channel_id=1, source_target_pairs={{0,6},{1,7},{2,4},{3,5},{4,2},{5,3},{6,0},{7,1},{8,14},{9,15},{10,... | collective-permute-start | bytes 122888 | tf_op jit(solution)/shard_map/ppermute | solution.py:23
  60.7 2.4 %collective-permute-done.25.refs_6_ = bf16[64,320]{1,0:T(8,128)(2,1)S(1)} collective-permute-done((bf16[64,320]{1,0:T(8,128)(2,1)S(1)}, bf16[64,320]{1,0:T(8,128)(2,1)S(1)}, u32[]{:S(2)}, u32[]{:S(2)}) %collective-permute-start.25) | collective-permute-done | bytes 40992 | tf_op jit(solution)/shard_map/ppermute | solution.py:23
  64.3 3.9 %feed_forward.1 = (f32[32,2560]{1,0:T(8,128)S(1)}, bf16[32,2560]{1,0:T(8,128)(2,1)S(1)}, bf16[32,2560]{1,0:T(8,128)(2,1)S(1)}) custom-call(bf16[64,2560]{1,0:T(8,128)(2,1)S(1)} %reshape.318.stream, f32[1,2560]{1,0:T(1,128)S(1)} %reshape.319.gain, bf16[2,960,2560]{2,1,0:T(8,128)(2,1)S(1)} %get-tuple-element.40.gates, ...), custom_call_target="tpu_custom_call" | custom-call | tf_op jit(solution)/shard_map/feed_forward/pallas_call | solution.py:530
  71.8 1.5 %collective-permute-start.30 = (bf16[32,2560]{1,0:T(8,128)(2,1)S(1)}, bf16[32,2560]{1,0:T(8,128)(2,1)S(1)}, u32[]{:S(2)}, u32[]{:S(2)}) collective-permute-start(bf16[32,2560]{1,0:T(8,128)(2,1)S(1)} %add_convert_fusion.1), channel_id=1, source_target_pairs={{0,6},{1,7},{2,4},{3,5},{4,2},{5,3},{6,0},{7,1},{8,14},{9,15},{10,... | collective-permute-start | bytes 491528 | tf_op jit(solution)/shard_map/ppermute | solution.py:23
  73.2 6.0 %write_pool.1 = bf16[64,128,512]{2,1,0:T(8,128)(2,1)} custom-call(s32[4,32]{1,0:T(4,128)S(1)} %pad_add_fusion.1.patch_source, bf16[64,512]{1,0:T(8,128)(2,1)S(1)} %get-tuple-element.54.fresh, bf16[64,128,512]{2,1,0:T(8,128)(2,1)} %source.1), custom_call_target="tpu_custom_call" | custom-call | bytes 16777216 | tf_op jit(solution)/shard_map/write_pool/pallas_call | solution.py:103
  80.7 1.4 %collective-permute-done.31 = bf16[8,4,2560]{2,1,0:T(4,128)(2,1)S(1)} collective-permute-done((bf16[8,4,2560]{2,1,0:T(4,128)(2,1)S(1)}, bf16[8,4,2560]{2,1,0:T(4,128)(2,1)S(1)}, u32[]{:S(2)}, u32[]{:S(2)}) %collective-permute-start.31) | collective-permute-done | bytes 163872 | tf_op jit(solution)/shard_map/ppermute | solution.py:23
  (108 shorter events, 23.9 us)
Async XLA Ops:
  1.6 7.8 %collective-permute-start = (bf16[4,4,2560]{2,1,0:T(4,128)(2,1)S(1)}, bf16[4,4,2560]{2,1,0:T(4,128)(2,1)S(1)}, u32[]{:S(2)}, u32[]{:S(2)}) collective-permute-start(bf16[4,4,2560]{2,1,0:T(4,128)(2,1)S(1)} %constant_dynamic-slice_fusion), channel_id=1, source_target_pairs={{0,16},{8,24},{16,0},{24,8},{1,17},{9,25},{17,1},{25,9},{2,18},{10... | collective-permute-start | bytes 245768 | tf_op jit(solution)/shard_map/ppermute | solution.py:23
  5.7 13.5 %collective-permute-start.3 = (bf16[96,2560]{1,0:T(8,128)(2,1)}, bf16[96,2560]{1,0:T(8,128)(2,1)S(1)}, u32[]{:S(2)}, u32[]{:S(2)}) collective-permute-start(bf16[96,2560]{1,0:T(8,128)(2,1)} %param.12), channel_id=1, source_target_pairs={{0,8},{8,0},{16,24},{24,16},{1,9},{9,1},{17,25},{25,17},{2,10},{10... | collective-permute-start | bytes 1474568 | tf_op jit(solution)/shard_map/ppermute | solution.py:23
  9.5 4.5 %collective-permute-start.1 = (bf16[4,4,2560]{2,1,0:T(4,128)(2,1)S(1)}, bf16[4,4,2560]{2,1,0:T(4,128)(2,1)S(1)}, u32[]{:S(2)}, u32[]{:S(2)}) collective-permute-start(bf16[4,4,2560]{2,1,0:T(4,128)(2,1)S(1)} %collective-permute-done), channel_id=1, source_target_pairs={{0,2},{1,3},{2,0},{3,1},{4,6},{5,7},{6,4},{7,5},{8,10},{9,11},{10,... | collective-permute-start | bytes 245768 | tf_op jit(solution)/shard_map/ppermute | solution.py:23
  19.7 5.0 %collective-permute-start.4 = (bf16[64,192]{1,0:T(8,128)(2,1)S(1)}, bf16[64,192]{1,0:T(8,128)(2,1)S(1)}, u32[]{:S(2)}, u32[]{:S(2)}) collective-permute-start(bf16[64,192]{1,0:T(8,128)(2,1)S(1)} %slice.60), channel_id=1, source_target_pairs={{0,16},{8,24},{16,0},{24,8},{1,17},{9,25},{17,1},{25,9},{2,18},{10... | collective-permute-start | bytes 73736 | tf_op jit(solution)/shard_map/ppermute | solution.py:23
  21.0 19.4 %collective-permute-start.13 = (bf16[80,2560]{1,0:T(8,128)(2,1)S(1)}, bf16[80,2560]{1,0:T(8,128)(2,1)S(1)}, u32[]{:S(2)}, u32[]{:S(2)}) collective-permute-start(bf16[80,2560]{1,0:T(8,128)(2,1)S(1)} %copy-done), channel_id=1, source_target_pairs={{0,8},{8,0},{16,24},{24,16},{1,9},{9,1},{17,25},{25,17},{2,10},{10... | collective-permute-start | bytes 1228808 | tf_op jit(solution)/shard_map/ppermute | solution.py:23
  23.1 19.7 %collective-permute-start.14 = (bf16[80,2560]{1,0:T(8,128)(2,1)S(1)}, bf16[80,2560]{1,0:T(8,128)(2,1)S(1)}, u32[]{:S(2)}, u32[]{:S(2)}) collective-permute-start(bf16[80,2560]{1,0:T(8,128)(2,1)S(1)} %copy-done), channel_id=1, source_target_pairs={{0,16},{8,24},{16,0},{24,8},{1,17},{9,25},{17,1},{25,9},{2,18},{10... | collective-permute-start | bytes 1228808 | tf_op jit(solution)/shard_map/ppermute | solution.py:23
  24.8 5.0 %collective-permute-start.10 = (bf16[64,384]{1,0:T(8,128)(2,1)S(1)}, bf16[64,384]{1,0:T(8,128)(2,1)S(1)}, u32[]{:S(2)}, u32[]{:S(2)}) collective-permute-start(bf16[64,384]{1,0:T(8,128)(2,1)S(1)} %pad_maximum_fusion.1.refs_0_), channel_id=1, source_target_pairs={{0,6},{1,7},{2,4},{3,5},{4,2},{5,3},{6,0},{7,1},{8,14},{9,15},{10,... | collective-permute-start | bytes 147464 | tf_op jit(solution)/shard_map/ppermute | solution.py:23
  27.7 4.2 %collective-permute-start.6 = (bf16[64,384]{1,0:T(8,128)(2,1)S(1)}, bf16[64,384]{1,0:T(8,128)(2,1)S(1)}, u32[]{:S(2)}, u32[]{:S(2)}) collective-permute-start(bf16[64,384]{1,0:T(8,128)(2,1)S(1)} %pad_maximum_fusion.1.refs_0_), channel_id=1, source_target_pairs={{0,2},{1,3},{2,0},{3,1},{4,6},{5,7},{6,4},{7,5},{8,10},{9,11},{10,... | collective-permute-start | bytes 147464 | tf_op jit(solution)/shard_map/ppermute | solution.py:23
  28.3 4.1 %collective-permute-start.8 = (bf16[64,384]{1,0:T(8,128)(2,1)S(1)}, bf16[64,384]{1,0:T(8,128)(2,1)S(1)}, u32[]{:S(2)}, u32[]{:S(2)}) collective-permute-start(bf16[64,384]{1,0:T(8,128)(2,1)S(1)} %pad_maximum_fusion.1.refs_0_), channel_id=1, source_target_pairs={{0,4},{1,5},{2,6},{3,7},{4,0},{5,1},{6,2},{7,3},{8,12},{9,13},{10,... | collective-permute-start | bytes 147464 | tf_op jit(solution)/shard_map/ppermute | solution.py:23
  29.9 2.5 %collective-permute-start.5 = (bf16[64,384]{1,0:T(8,128)(2,1)S(1)}, bf16[64,384]{1,0:T(8,128)(2,1)S(1)}, u32[]{:S(2)}, u32[]{:S(2)}) collective-permute-start(bf16[64,384]{1,0:T(8,128)(2,1)S(1)} %pad_maximum_fusion.1.refs_0_), channel_id=1, source_target_pairs={{0,1},{1,0},{2,3},{3,2},{4,5},{5,4},{6,7},{7,6},{8,9},{9,8},{10,11... | collective-permute-start | bytes 147464 | tf_op jit(solution)/shard_map/ppermute | solution.py:23
  38.7 1.5 %collective-permute-start.12 = (bf16[336,256]{1,0:T(8,128)(2,1)S(1)}, bf16[336,256]{1,0:T(8,128)(2,1)S(1)}, u32[]{:S(2)}, u32[]{:S(2)}) collective-permute-start(bf16[336,256]{1,0:T(8,128)(2,1)S(1)} %get-tuple-element.37), channel_id=1, source_target_pairs={{0,1},{1,0},{2,3},{3,2},{4,5},{5,4},{6,7},{7,6},{8,9},{9,8},{10,11... | collective-permute-start | bytes 516104 | tf_op jit(solution)/shard_map/ppermute | solution.py:23
  42.8 10.6 %collective-permute-start.18 = (bf16[80,2560]{1,0:T(8,128)(2,1)S(1)}, bf16[80,2560]{1,0:T(8,128)(2,1)S(1)}, u32[]{:S(2)}, u32[]{:S(2)}) collective-permute-start(bf16[80,2560]{1,0:T(8,128)(2,1)S(1)} %collective-permute-done.14.refs_2_), channel_id=1, source_target_pairs={{0,8},{8,0},{16,24},{24,16},{1,9},{9,1},{17,25},{25,17},{2,10},{10... | collective-permute-start | bytes 1228808 | tf_op jit(solution)/shard_map/ppermute | solution.py:23
  42.8 8.8 %collective-permute-start.15 = (bf16[336,256]{1,0:T(8,128)(2,1)S(1)}, bf16[336,256]{1,0:T(8,128)(2,1)S(1)}, u32[]{:S(2)}, u32[]{:S(2)}) collective-permute-start(bf16[336,256]{1,0:T(8,128)(2,1)S(1)} %merge_pair.1.after.refs_0_), channel_id=1, source_target_pairs={{0,2},{1,3},{2,0},{3,1},{4,6},{5,7},{6,4},{7,5},{8,10},{9,11},{10,... | collective-permute-start | bytes 516104 | tf_op jit(solution)/shard_map/ppermute | solution.py:23
  44.3 9.1 %collective-permute-start.16 = (bf16[336,256]{1,0:T(8,128)(2,1)S(1)}, bf16[336,256]{1,0:T(8,128)(2,1)S(1)}, u32[]{:S(2)}, u32[]{:S(2)}) collective-permute-start(bf16[336,256]{1,0:T(8,128)(2,1)S(1)} %merge_pair.1.after.refs_0_), channel_id=1, source_target_pairs={{0,4},{1,5},{2,6},{3,7},{4,0},{5,1},{6,2},{7,3},{8,12},{9,13},{10,... | collective-permute-start | bytes 516104 | tf_op jit(solution)/shard_map/ppermute | solution.py:23
  45.8 7.6 %collective-permute-start.17 = (bf16[336,256]{1,0:T(8,128)(2,1)S(1)}, bf16[336,256]{1,0:T(8,128)(2,1)S(1)}, u32[]{:S(2)}, u32[]{:S(2)}) collective-permute-start(bf16[336,256]{1,0:T(8,128)(2,1)S(1)} %merge_pair.1.after.refs_0_), channel_id=1, source_target_pairs={{0,6},{1,7},{2,4},{3,5},{4,2},{5,3},{6,0},{7,1},{8,14},{9,15},{10,... | collective-permute-start | bytes 516104 | tf_op jit(solution)/shard_map/ppermute | solution.py:23
  56.0 4.2 %collective-permute-start.21 = (bf16[64,320]{1,0:T(8,128)(2,1)S(1)}, bf16[64,320]{1,0:T(8,128)(2,1)S(1)}, u32[]{:S(2)}, u32[]{:S(2)}) collective-permute-start(bf16[64,320]{1,0:T(8,128)(2,1)S(1)} %project_out.1.refs_0_), channel_id=1, source_target_pairs={{0,2},{1,3},{2,0},{3,1},{4,6},{5,7},{6,4},{7,5},{8,10},{9,11},{10,... | collective-permute-start | bytes 122888 | tf_op jit(solution)/shard_map/ppermute | solution.py:23
  56.6 4.1 %collective-permute-start.23 = (bf16[64,320]{1,0:T(8,128)(2,1)S(1)}, bf16[64,320]{1,0:T(8,128)(2,1)S(1)}, u32[]{:S(2)}, u32[]{:S(2)}) collective-permute-start(bf16[64,320]{1,0:T(8,128)(2,1)S(1)} %project_out.1.refs_0_), channel_id=1, source_target_pairs={{0,4},{1,5},{2,6},{3,7},{4,0},{5,1},{6,2},{7,3},{8,12},{9,13},{10,... | collective-permute-start | bytes 122888 | tf_op jit(solution)/shard_map/ppermute | solution.py:23
  58.1 5.0 %collective-permute-start.25 = (bf16[64,320]{1,0:T(8,128)(2,1)S(1)}, bf16[64,320]{1,0:T(8,128)(2,1)S(1)}, u32[]{:S(2)}, u32[]{:S(2)}) collective-permute-start(bf16[64,320]{1,0:T(8,128)(2,1)S(1)} %project_out.1.refs_0_), channel_id=1, source_target_pairs={{0,6},{1,7},{2,4},{3,5},{4,2},{5,3},{6,0},{7,1},{8,14},{9,15},{10,... | collective-permute-start | bytes 122888 | tf_op jit(solution)/shard_map/ppermute | solution.py:23
  59.5 3.5 %collective-permute-start.20 = (bf16[64,320]{1,0:T(8,128)(2,1)S(1)}, bf16[64,320]{1,0:T(8,128)(2,1)S(1)}, u32[]{:S(2)}, u32[]{:S(2)}) collective-permute-start(bf16[64,320]{1,0:T(8,128)(2,1)S(1)} %project_out.1.refs_0_), channel_id=1, source_target_pairs={{0,1},{1,0},{2,3},{3,2},{4,5},{5,4},{6,7},{7,6},{8,9},{9,8},{10,11... | collective-permute-start | bytes 122888 | tf_op jit(solution)/shard_map/ppermute | solution.py:23
  60.1 2.9 %collective-permute-start.22 = (bf16[64,320]{1,0:T(8,128)(2,1)S(1)}, bf16[64,320]{1,0:T(8,128)(2,1)S(1)}, u32[]{:S(2)}, u32[]{:S(2)}) collective-permute-start(bf16[64,320]{1,0:T(8,128)(2,1)S(1)} %collective-permute-done.21.refs_2_), channel_id=1, source_target_pairs={{0,1},{1,0},{2,3},{3,2},{4,5},{5,4},{6,7},{7,6},{8,9},{9,8},{10,11... | collective-permute-start | bytes 122888 | tf_op jit(solution)/shard_map/ppermute | solution.py:23
  60.7 2.4 %collective-permute-start.24 = (bf16[64,320]{1,0:T(8,128)(2,1)S(1)}, bf16[64,320]{1,0:T(8,128)(2,1)S(1)}, u32[]{:S(2)}, u32[]{:S(2)}) collective-permute-start(bf16[64,320]{1,0:T(8,128)(2,1)S(1)} %collective-permute-done.23.refs_4_), channel_id=1, source_target_pairs={{0,1},{1,0},{2,3},{3,2},{4,5},{5,4},{6,7},{7,6},{8,9},{9,8},{10,11... | collective-permute-start | bytes 122888 | tf_op jit(solution)/shard_map/ppermute | solution.py:23
  69.7 9.5 %collective-permute-start.28 = (bf16[32,2560]{1,0:T(8,128)(2,1)S(1)}, bf16[32,2560]{1,0:T(8,128)(2,1)S(1)}, u32[]{:S(2)}, u32[]{:S(2)}) collective-permute-start(bf16[32,2560]{1,0:T(8,128)(2,1)S(1)} %add_convert_fusion.1), channel_id=1, source_target_pairs={{0,2},{1,3},{2,0},{3,1},{4,6},{5,7},{6,4},{7,5},{8,10},{9,11},{10,... | collective-permute-start | bytes 491528 | tf_op jit(solution)/shard_map/ppermute | solution.py:23
  70.9 9.5 %collective-permute-start.29 = (bf16[32,2560]{1,0:T(8,128)(2,1)S(1)}, bf16[32,2560]{1,0:T(8,128)(2,1)S(1)}, u32[]{:S(2)}, u32[]{:S(2)}) collective-permute-start(bf16[32,2560]{1,0:T(8,128)(2,1)S(1)} %add_convert_fusion.1), channel_id=1, source_target_pairs={{0,4},{1,5},{2,6},{3,7},{4,0},{5,1},{6,2},{7,3},{8,12},{9,13},{10,... | collective-permute-start | bytes 491528 | tf_op jit(solution)/shard_map/ppermute | solution.py:23
  71.8 8.6 %collective-permute-start.30 = (bf16[32,2560]{1,0:T(8,128)(2,1)S(1)}, bf16[32,2560]{1,0:T(8,128)(2,1)S(1)}, u32[]{:S(2)}, u32[]{:S(2)}) collective-permute-start(bf16[32,2560]{1,0:T(8,128)(2,1)S(1)} %add_convert_fusion.1), channel_id=1, source_target_pairs={{0,6},{1,7},{2,4},{3,5},{4,2},{5,3},{6,0},{7,1},{8,14},{9,15},{10,... | collective-permute-start | bytes 491528 | tf_op jit(solution)/shard_map/ppermute | solution.py:23
  (14 other events, 55.9 us)

commit v7 on v6

--- a/solution.py
+++ b/solution.py
@@ -546,6 +546,31 @@
     )(stream, gain.reshape(1, width), gates, downs, *heads_out)
 
 
+def half_kernel(flip, part, *refs):
+    target, sem = refs[-2], refs[-1]
+    count = part.shape[0]
+    side = jnp.bitwise_xor(lax.axis_index("seq") % 2, flip)
+    copy = pltpu.make_async_copy(part, target.at[pl.ds(side * count, count)], sem)
+    copy.start()
+    copy.wait()
+
+
+def write_half(flip, part, started=None):
+    hbm = pl.BlockSpec(memory_space=pltpu.HBM)
+    earlier = [] if started is None else [started]
+    return pl.pallas_call(
+        functools.partial(half_kernel, flip),
+        out_shape=pltpu.HBM((2 * part.shape[0], *part.shape[1:]), part.dtype),
+        in_specs=[pl.BlockSpec(memory_space=pltpu.VMEM), *[hbm for _ in earlier]],
+        out_specs=hbm,
+        scratch_shapes=[pltpu.SemaphoreType.DMA],
+        input_output_aliases={} if started is None else {1: 0},
+        compiler_params=pltpu.CompilerParams(vmem_limit_bytes=2 * 1024 * 1024),
+        cost_estimate=pl.CostEstimate(flops=0, bytes_accessed=4 * part.size, transcendentals=0),
+        name="write_half",
+    )(part, *earlier)
+
+
 def body(
     n_dp,
     n_seq,
@@ -573,13 +598,6 @@
     lines = requests * new_count
     half = lines // 2
     rows = new_count * heads
-
-    def ordered(mine, other, axis=0):
-        return jnp.where(
-            core == 0,
-            jnp.concatenate([mine, other], axis=axis),
-            jnp.concatenate([other, mine], axis=axis),
-        )
 
     stream = tokens.reshape(lines, width)
     partner_weight = swap(qkv_weight, "dp", n_dp, 1)
@@ -701,7 +719,9 @@
     full_half = tree_sum([term.astype(f32) for term in terms])
     out_half = (my_residual.astype(f32) + full_half).astype(bf16)
     out_half = out_half.reshape(requests // 2, new_count, width)
-    return ordered(out_half, swap(out_half, "seq", n_seq, 1)), written_pool
+    started = write_half(0, out_half)
+    layer_out = write_half(1, swap(out_half, "seq", n_seq, 1), started)
+    return layer_out, written_pool
 
 
 def solution(mesh):

time: 83.3 us -> 82.9 us (level)
  Pallas kernels: 21.5 us -> 23.7 us
  waiting for transfers between devices: 26.5 us -> 24.9 us
  other arithmetic: 2.56 us -> 1.47 us
    ppermute x32, waiting for transfers between devices: 26.5 us -> 24.9 us  [swap(): return lax.ppermute(values, axis, [(i, i ^ mask) for i in range(size)])]
    pallas_call x0 -> x2, Pallas kernels: none -> 1.36 us  [write_half(): pl.pallas_call(functools.partial(half_kernel, flip), out_shape=pltpu.HBM(...]
    select_n x1 -> x0, other arithmetic: 1.09 us -> none  [ordered(): jnp.where(core == 0, jnp.concatenate([mine, other], axis=axis), jnp.conca...]
  transfers between devices with their start and end apart: 32 -> 32, of which waited for: 22 -> 22; matrix products, arithmetic and copies ran while one was open for 4% -> 4% of each run, Pallas kernels for 20% -> 22%
where the time goes in v7:
time: 82.9 us; the launch traced here: 82.6 us
  starting transfers between devices  27.8 us (34%)
  waiting for transfers between devices  24.9 us (30%)
  Pallas kernels  23.7 us (29%)
  local copies, waits for them, and re-layouts  2.85 us (3%)
  other arithmetic  1.47 us (2%)
  between operations  1.12 us (1%)
    ppermute x32, starting transfers between devices, swap(): return lax.ppermute(values, axis, [(i, i ^ mask) for i in range(size)])  27.8 us
    ppermute x32, waiting for transfers between devices, swap(): return lax.ppermute(values, axis, [(i, i ^ mask) for i in range(size)])  24.9 us
    pallas_call x1, Pallas kernels, write_pool(): pl.pallas_call(functools.partial(write_kernel, dims, parts), out_shape=pl...  6.79 us
    pallas_call x1, Pallas kernels, fetch_weights(): pl.pallas_call(functools.partial(fetch_kernel, parts), out_shape=(jax.Sha...  5.33 us
    pallas_call x1, Pallas kernels, attention(): pl.pallas_call(functools.partial(attention_kernel, dims, len(pieces)), ou...  5 us
    pallas_call x1, Pallas kernels, feed_forward(): pl.pallas_call(functools.partial(mlp_kernel, chunk, len(heads_out)), out_...  3.88 us
  transfers between devices with their start and end apart: 32, of which 22 were waited for; matrix products, arithmetic and copies ran while one was open for 4% of the time, Pallas kernels for 22%

profile of v7, /device:TPU:0, one launch (start us, length us, event | category | flops | bytes accessed | tf_op | source)
XLA Modules:
  0.0 82.6 jit_solution(6796331690434869527)
XLA Ops:
  1.6 4.1 %collective-permute-start = (bf16[4,4,2560]{2,1,0:T(4,128)(2,1)S(1)}, bf16[4,4,2560]{2,1,0:T(4,128)(2,1)S(1)}, u32[]{:S(2)}, u32[]{:S(2)}) collective-permute-start(bf16[4,4,2560]{2,1,0:T(4,128)(2,1)S(1)} %constant_dynamic-slice_fusion), channel_id=1, source_target_pairs={{0,16},{8,24},{16,0},{24,8},{1,17},{9,25},{17,1},{25,9},{2,18},{10... | collective-permute-start | bytes 245768 | tf_op jit(solution)/shard_map/ppermute | solution.py:23
  5.7 1.6 %collective-permute-start.3 = (bf16[96,2560]{1,0:T(8,128)(2,1)}, bf16[96,2560]{1,0:T(8,128)(2,1)S(1)}, u32[]{:S(2)}, u32[]{:S(2)}) collective-permute-start(bf16[96,2560]{1,0:T(8,128)(2,1)} %param.12), channel_id=1, source_target_pairs={{0,8},{8,0},{16,24},{24,16},{1,9},{9,1},{17,25},{25,17},{2,10},{10... | collective-permute-start | bytes 1474568 | tf_op jit(solution)/shard_map/ppermute | solution.py:23
  9.5 1.9 %collective-permute-start.1 = (bf16[4,4,2560]{2,1,0:T(4,128)(2,1)S(1)}, bf16[4,4,2560]{2,1,0:T(4,128)(2,1)S(1)}, u32[]{:S(2)}, u32[]{:S(2)}) collective-permute-start(bf16[4,4,2560]{2,1,0:T(4,128)(2,1)S(1)} %collective-permute-done), channel_id=1, source_target_pairs={{0,2},{1,3},{2,0},{3,1},{4,6},{5,7},{6,4},{7,5},{8,10},{9,11},{10,... | collective-permute-start | bytes 245768 | tf_op jit(solution)/shard_map/ppermute | solution.py:23
  12.2 1.7 %collective-permute-done.1 = bf16[4,4,2560]{2,1,0:T(4,128)(2,1)S(1)} collective-permute-done((bf16[4,4,2560]{2,1,0:T(4,128)(2,1)S(1)}, bf16[4,4,2560]{2,1,0:T(4,128)(2,1)S(1)}, u32[]{:S(2)}, u32[]{:S(2)}) %collective-permute-start.1) | collective-permute-done | bytes 81952 | tf_op jit(solution)/shard_map/ppermute | solution.py:23
  14.2 1.3 %collective-permute-done.2 = bf16[8,4,2560]{2,1,0:T(4,128)(2,1)S(1)} collective-permute-done((bf16[8,4,2560]{2,1,0:T(4,128)(2,1)S(1)}, bf16[8,4,2560]{2,1,0:T(4,128)(2,1)S(1)}, u32[]{:S(2)}, u32[]{:S(2)}) %collective-permute-start.2) | collective-permute-done | bytes 163872 | tf_op jit(solution)/shard_map/ppermute | solution.py:23
  16.4 2.8 %collective-permute-done.3 = bf16[96,2560]{1,0:T(8,128)(2,1)S(1)} collective-permute-done((bf16[96,2560]{1,0:T(8,128)(2,1)}, bf16[96,2560]{1,0:T(8,128)(2,1)S(1)}, u32[]{:S(2)}, u32[]{:S(2)}) %collective-permute-start.3) | collective-permute-done | bytes 491552 | tf_op jit(solution)/shard_map/ppermute | solution.py:23
  21.1 2.0 %collective-permute-start.13 = (bf16[80,2560]{1,0:T(8,128)(2,1)S(1)}, bf16[80,2560]{1,0:T(8,128)(2,1)S(1)}, u32[]{:S(2)}, u32[]{:S(2)}) collective-permute-start(bf16[80,2560]{1,0:T(8,128)(2,1)S(1)} %copy-done), channel_id=1, source_target_pairs={{0,8},{8,0},{16,24},{24,16},{1,9},{9,1},{17,25},{25,17},{2,10},{10... | collective-permute-start | bytes 1228808 | tf_op jit(solution)/shard_map/ppermute | solution.py:23
  23.1 1.3 %collective-permute-start.14 = (bf16[80,2560]{1,0:T(8,128)(2,1)S(1)}, bf16[80,2560]{1,0:T(8,128)(2,1)S(1)}, u32[]{:S(2)}, u32[]{:S(2)}) collective-permute-start(bf16[80,2560]{1,0:T(8,128)(2,1)S(1)} %copy-done), channel_id=1, source_target_pairs={{0,16},{8,24},{16,0},{24,8},{1,17},{9,25},{17,1},{25,9},{2,18},{10... | collective-permute-start | bytes 1228808 | tf_op jit(solution)/shard_map/ppermute | solution.py:23
  24.8 2.7 %collective-permute-start.10 = (bf16[64,384]{1,0:T(8,128)(2,1)S(1)}, bf16[64,384]{1,0:T(8,128)(2,1)S(1)}, u32[]{:S(2)}, u32[]{:S(2)}) collective-permute-start(bf16[64,384]{1,0:T(8,128)(2,1)S(1)} %pad_maximum_fusion.1.refs_0_), channel_id=1, source_target_pairs={{0,6},{1,7},{2,4},{3,5},{4,2},{5,3},{6,0},{7,1},{8,14},{9,15},{10,... | collective-permute-start | bytes 147464 | tf_op jit(solution)/shard_map/ppermute | solution.py:23
  28.5 1.3 %collective-permute-done.10.refs_6_ = bf16[64,384]{1,0:T(8,128)(2,1)S(1)} collective-permute-done((bf16[64,384]{1,0:T(8,128)(2,1)S(1)}, bf16[64,384]{1,0:T(8,128)(2,1)S(1)}, u32[]{:S(2)}, u32[]{:S(2)}) %collective-permute-start.10) | collective-permute-done | bytes 49184 | tf_op jit(solution)/shard_map/ppermute | solution.py:23
  30.2 1.6 %collective-permute-done.6.refs_2_ = bf16[64,384]{1,0:T(8,128)(2,1)S(1)} collective-permute-done((bf16[64,384]{1,0:T(8,128)(2,1)S(1)}, bf16[64,384]{1,0:T(8,128)(2,1)S(1)}, u32[]{:S(2)}, u32[]{:S(2)}) %collective-permute-start.6) | collective-permute-done | bytes 49184 | tf_op jit(solution)/shard_map/ppermute | solution.py:23
  33.7 5.0 %page_attention.1 = (bf16[336,256]{1,0:T(8,128)(2,1)S(1)}, bf16[336,256]{1,0:T(8,128)(2,1)S(1)}, bf16[64,512]{1,0:T(8,128)(2,1)S(1)}) custom-call(s32[3,64]{1,0:T(4,128)S(1)} %pad_add_fusion.slot_source, f32[64,128]{1,0:T(8,128)S(1)} %get-tuple-element.79.cosine, f32[64,128]{1,0:T(8,128)S(1)} %get-tuple-element.80.sine, ...), custom_call_target="tpu_custom_call" | custom-call | bytes 1024 | tf_op jit(solution)/shard_map/page_attention/pallas_call | solution.py:367
  40.5 2.3 %collective-permute-done.14.refs_2_ = bf16[80,2560]{1,0:T(8,128)(2,1)S(1)} collective-permute-done((bf16[80,2560]{1,0:T(8,128)(2,1)S(1)}, bf16[80,2560]{1,0:T(8,128)(2,1)S(1)}, u32[]{:S(2)}, u32[]{:S(2)}) %collective-permute-start.14) | collective-permute-done | bytes 409632 | tf_op jit(solution)/shard_map/ppermute | solution.py:23
  42.8 1.5 %collective-permute-start.15 = (bf16[336,256]{1,0:T(8,128)(2,1)S(1)}, bf16[336,256]{1,0:T(8,128)(2,1)S(1)}, u32[]{:S(2)}, u32[]{:S(2)}) collective-permute-start(bf16[336,256]{1,0:T(8,128)(2,1)S(1)} %merge_pair.1.after.refs_0_), channel_id=1, source_target_pairs={{0,2},{1,3},{2,0},{3,1},{4,6},{5,7},{6,4},{7,5},{8,10},{9,11},{10,... | collective-permute-start | bytes 516104 | tf_op jit(solution)/shard_map/ppermute | solution.py:23
  44.3 1.5 %collective-permute-start.16 = (bf16[336,256]{1,0:T(8,128)(2,1)S(1)}, bf16[336,256]{1,0:T(8,128)(2,1)S(1)}, u32[]{:S(2)}, u32[]{:S(2)}) collective-permute-start(bf16[336,256]{1,0:T(8,128)(2,1)S(1)} %merge_pair.1.after.refs_0_), channel_id=1, source_target_pairs={{0,4},{1,5},{2,6},{3,7},{4,0},{5,1},{6,2},{7,3},{8,12},{9,13},{10,... | collective-permute-start | bytes 516104 | tf_op jit(solution)/shard_map/ppermute | solution.py:23
  46.3 5.3 %fetch_weights.1 = (bf16[2,960,2560]{2,1,0:T(8,128)(2,1)S(1)}, bf16[960,2560]{1,0:T(8,128)(2,1)S(1)}, f32[8,128]{1,0:T(8,128)S(1)}) custom-call(bf16[2,960,2560]{2,1,0:T(8,128)(2,1)} %gate_up.1, bf16[960,2560]{1,0:T(8,128)(2,1)} %down.1, bf16[336,256]{1,0:T(8,128)(2,1)S(1)} %merge_pair.1.after.refs_0_), custom_call_target="tpu_custom_call" | custom-call | bytes 14745600 | tf_op jit(solution)/shard_map/fetch_weights/pallas_call | solution.py:457
  51.6 1.7 %collective-permute-done.16.refs_2_ = bf16[336,256]{1,0:T(8,128)(2,1)S(1)} collective-permute-done((bf16[336,256]{1,0:T(8,128)(2,1)S(1)}, bf16[336,256]{1,0:T(8,128)(2,1)S(1)}, u32[]{:S(2)}, u32[]{:S(2)}) %collective-permute-start.16) | collective-permute-done | bytes 172064 | tf_op jit(solution)/shard_map/ppermute | solution.py:23
  53.8 1.4 %collective-permute-done.19.other = bf16[32,2560]{1,0:T(8,128)(2,1)S(1)} collective-permute-done((bf16[32,2560]{1,0:T(8,128)(2,1)S(1)}, bf16[32,2560]{1,0:T(8,128)(2,1)S(1)}, u32[]{:S(2)}, u32[]{:S(2)}) %collective-permute-start.19) | collective-permute-done | bytes 163872 | tf_op jit(solution)/shard_map/ppermute | solution.py:23
  56.6 1.4 %collective-permute-start.23 = (bf16[64,320]{1,0:T(8,128)(2,1)S(1)}, bf16[64,320]{1,0:T(8,128)(2,1)S(1)}, u32[]{:S(2)}, u32[]{:S(2)}) collective-permute-start(bf16[64,320]{1,0:T(8,128)(2,1)S(1)} %project_out.1.refs_0_), channel_id=1, source_target_pairs={{0,4},{1,5},{2,6},{3,7},{4,0},{5,1},{6,2},{7,3},{8,12},{9,13},{10,... | collective-permute-start | bytes 122888 | tf_op jit(solution)/shard_map/ppermute | solution.py:23
  58.0 1.5 %collective-permute-start.25 = (bf16[64,320]{1,0:T(8,128)(2,1)S(1)}, bf16[64,320]{1,0:T(8,128)(2,1)S(1)}, u32[]{:S(2)}, u32[]{:S(2)}) collective-permute-start(bf16[64,320]{1,0:T(8,128)(2,1)S(1)} %project_out.1.refs_0_), channel_id=1, source_target_pairs={{0,6},{1,7},{2,4},{3,5},{4,2},{5,3},{6,0},{7,1},{8,14},{9,15},{10,... | collective-permute-start | bytes 122888 | tf_op jit(solution)/shard_map/ppermute | solution.py:23
  60.7 2.3 %collective-permute-done.25.refs_6_ = bf16[64,320]{1,0:T(8,128)(2,1)S(1)} collective-permute-done((bf16[64,320]{1,0:T(8,128)(2,1)S(1)}, bf16[64,320]{1,0:T(8,128)(2,1)S(1)}, u32[]{:S(2)}, u32[]{:S(2)}) %collective-permute-start.25) | collective-permute-done | bytes 40992 | tf_op jit(solution)/shard_map/ppermute | solution.py:23
  64.2 3.9 %feed_forward.1 = (f32[32,2560]{1,0:T(8,128)S(1)}, bf16[32,2560]{1,0:T(8,128)(2,1)S(1)}, bf16[32,2560]{1,0:T(8,128)(2,1)S(1)}) custom-call(bf16[64,2560]{1,0:T(8,128)(2,1)S(1)} %reshape.318.stream, f32[1,2560]{1,0:T(1,128)S(1)} %reshape.319.gain, bf16[2,960,2560]{2,1,0:T(8,128)(2,1)S(1)} %get-tuple-element.40.gates, ...), custom_call_target="tpu_custom_call" | custom-call | tf_op jit(solution)/shard_map/feed_forward/pallas_call | solution.py:530
  71.7 1.5 %collective-permute-start.30 = (bf16[32,2560]{1,0:T(8,128)(2,1)S(1)}, bf16[32,2560]{1,0:T(8,128)(2,1)S(1)}, u32[]{:S(2)}, u32[]{:S(2)}) collective-permute-start(bf16[32,2560]{1,0:T(8,128)(2,1)S(1)} %add_convert_fusion.1), channel_id=1, source_target_pairs={{0,6},{1,7},{2,4},{3,5},{4,2},{5,3},{6,0},{7,1},{8,14},{9,15},{10,... | collective-permute-start | bytes 491528 | tf_op jit(solution)/shard_map/ppermute | solution.py:23
  73.2 6.8 %write_pool.1 = bf16[64,128,512]{2,1,0:T(8,128)(2,1)} custom-call(s32[4,32]{1,0:T(4,128)S(1)} %pad_add_fusion.1.patch_source, bf16[64,512]{1,0:T(8,128)(2,1)S(1)} %get-tuple-element.54.fresh, bf16[64,128,512]{2,1,0:T(8,128)(2,1)} %source.1), custom_call_target="tpu_custom_call" | custom-call | bytes 16777216 | tf_op jit(solution)/shard_map/write_pool/pallas_call | solution.py:103
  (109 shorter events, 23.0 us)
Async XLA Ops:
  1.6 7.8 %collective-permute-start = (bf16[4,4,2560]{2,1,0:T(4,128)(2,1)S(1)}, bf16[4,4,2560]{2,1,0:T(4,128)(2,1)S(1)}, u32[]{:S(2)}, u32[]{:S(2)}) collective-permute-start(bf16[4,4,2560]{2,1,0:T(4,128)(2,1)S(1)} %constant_dynamic-slice_fusion), channel_id=1, source_target_pairs={{0,16},{8,24},{16,0},{24,8},{1,17},{9,25},{17,1},{25,9},{2,18},{10... | collective-permute-start | bytes 245768 | tf_op jit(solution)/shard_map/ppermute | solution.py:23
  5.7 13.5 %collective-permute-start.3 = (bf16[96,2560]{1,0:T(8,128)(2,1)}, bf16[96,2560]{1,0:T(8,128)(2,1)S(1)}, u32[]{:S(2)}, u32[]{:S(2)}) collective-permute-start(bf16[96,2560]{1,0:T(8,128)(2,1)} %param.12), channel_id=1, source_target_pairs={{0,8},{8,0},{16,24},{24,16},{1,9},{9,1},{17,25},{25,17},{2,10},{10... | collective-permute-start | bytes 1474568 | tf_op jit(solution)/shard_map/ppermute | solution.py:23
  9.5 4.5 %collective-permute-start.1 = (bf16[4,4,2560]{2,1,0:T(4,128)(2,1)S(1)}, bf16[4,4,2560]{2,1,0:T(4,128)(2,1)S(1)}, u32[]{:S(2)}, u32[]{:S(2)}) collective-permute-start(bf16[4,4,2560]{2,1,0:T(4,128)(2,1)S(1)} %collective-permute-done), channel_id=1, source_target_pairs={{0,2},{1,3},{2,0},{3,1},{4,6},{5,7},{6,4},{7,5},{8,10},{9,11},{10,... | collective-permute-start | bytes 245768 | tf_op jit(solution)/shard_map/ppermute | solution.py:23
  19.7 5.0 %collective-permute-start.4 = (bf16[64,192]{1,0:T(8,128)(2,1)S(1)}, bf16[64,192]{1,0:T(8,128)(2,1)S(1)}, u32[]{:S(2)}, u32[]{:S(2)}) collective-permute-start(bf16[64,192]{1,0:T(8,128)(2,1)S(1)} %slice.60), channel_id=1, source_target_pairs={{0,16},{8,24},{16,0},{24,8},{1,17},{9,25},{17,1},{25,9},{2,18},{10... | collective-permute-start | bytes 73736 | tf_op jit(solution)/shard_map/ppermute | solution.py:23
  21.1 19.4 %collective-permute-start.13 = (bf16[80,2560]{1,0:T(8,128)(2,1)S(1)}, bf16[80,2560]{1,0:T(8,128)(2,1)S(1)}, u32[]{:S(2)}, u32[]{:S(2)}) collective-permute-start(bf16[80,2560]{1,0:T(8,128)(2,1)S(1)} %copy-done), channel_id=1, source_target_pairs={{0,8},{8,0},{16,24},{24,16},{1,9},{9,1},{17,25},{25,17},{2,10},{10... | collective-permute-start | bytes 1228808 | tf_op jit(solution)/shard_map/ppermute | solution.py:23
  23.1 19.7 %collective-permute-start.14 = (bf16[80,2560]{1,0:T(8,128)(2,1)S(1)}, bf16[80,2560]{1,0:T(8,128)(2,1)S(1)}, u32[]{:S(2)}, u32[]{:S(2)}) collective-permute-start(bf16[80,2560]{1,0:T(8,128)(2,1)S(1)} %copy-done), channel_id=1, source_target_pairs={{0,16},{8,24},{16,0},{24,8},{1,17},{9,25},{17,1},{25,9},{2,18},{10... | collective-permute-start | bytes 1228808 | tf_op jit(solution)/shard_map/ppermute | solution.py:23
  24.8 5.0 %collective-permute-start.10 = (bf16[64,384]{1,0:T(8,128)(2,1)S(1)}, bf16[64,384]{1,0:T(8,128)(2,1)S(1)}, u32[]{:S(2)}, u32[]{:S(2)}) collective-permute-start(bf16[64,384]{1,0:T(8,128)(2,1)S(1)} %pad_maximum_fusion.1.refs_0_), channel_id=1, source_target_pairs={{0,6},{1,7},{2,4},{3,5},{4,2},{5,3},{6,0},{7,1},{8,14},{9,15},{10,... | collective-permute-start | bytes 147464 | tf_op jit(solution)/shard_map/ppermute | solution.py:23
  27.7 4.2 %collective-permute-start.6 = (bf16[64,384]{1,0:T(8,128)(2,1)S(1)}, bf16[64,384]{1,0:T(8,128)(2,1)S(1)}, u32[]{:S(2)}, u32[]{:S(2)}) collective-permute-start(bf16[64,384]{1,0:T(8,128)(2,1)S(1)} %pad_maximum_fusion.1.refs_0_), channel_id=1, source_target_pairs={{0,2},{1,3},{2,0},{3,1},{4,6},{5,7},{6,4},{7,5},{8,10},{9,11},{10,... | collective-permute-start | bytes 147464 | tf_op jit(solution)/shard_map/ppermute | solution.py:23
  28.3 4.1 %collective-permute-start.8 = (bf16[64,384]{1,0:T(8,128)(2,1)S(1)}, bf16[64,384]{1,0:T(8,128)(2,1)S(1)}, u32[]{:S(2)}, u32[]{:S(2)}) collective-permute-start(bf16[64,384]{1,0:T(8,128)(2,1)S(1)} %pad_maximum_fusion.1.refs_0_), channel_id=1, source_target_pairs={{0,4},{1,5},{2,6},{3,7},{4,0},{5,1},{6,2},{7,3},{8,12},{9,13},{10,... | collective-permute-start | bytes 147464 | tf_op jit(solution)/shard_map/ppermute | solution.py:23
  29.9 2.5 %collective-permute-start.5 = (bf16[64,384]{1,0:T(8,128)(2,1)S(1)}, bf16[64,384]{1,0:T(8,128)(2,1)S(1)}, u32[]{:S(2)}, u32[]{:S(2)}) collective-permute-start(bf16[64,384]{1,0:T(8,128)(2,1)S(1)} %pad_maximum_fusion.1.refs_0_), channel_id=1, source_target_pairs={{0,1},{1,0},{2,3},{3,2},{4,5},{5,4},{6,7},{7,6},{8,9},{9,8},{10,11... | collective-permute-start | bytes 147464 | tf_op jit(solution)/shard_map/ppermute | solution.py:23
  38.8 1.5 %collective-permute-start.12 = (bf16[336,256]{1,0:T(8,128)(2,1)S(1)}, bf16[336,256]{1,0:T(8,128)(2,1)S(1)}, u32[]{:S(2)}, u32[]{:S(2)}) collective-permute-start(bf16[336,256]{1,0:T(8,128)(2,1)S(1)} %get-tuple-element.37), channel_id=1, source_target_pairs={{0,1},{1,0},{2,3},{3,2},{4,5},{5,4},{6,7},{7,6},{8,9},{9,8},{10,11... | collective-permute-start | bytes 516104 | tf_op jit(solution)/shard_map/ppermute | solution.py:23
  42.8 10.6 %collective-permute-start.18 = (bf16[80,2560]{1,0:T(8,128)(2,1)S(1)}, bf16[80,2560]{1,0:T(8,128)(2,1)S(1)}, u32[]{:S(2)}, u32[]{:S(2)}) collective-permute-start(bf16[80,2560]{1,0:T(8,128)(2,1)S(1)} %collective-permute-done.14.refs_2_), channel_id=1, source_target_pairs={{0,8},{8,0},{16,24},{24,16},{1,9},{9,1},{17,25},{25,17},{2,10},{10... | collective-permute-start | bytes 1228808 | tf_op jit(solution)/shard_map/ppermute | solution.py:23
  42.8 8.8 %collective-permute-start.15 = (bf16[336,256]{1,0:T(8,128)(2,1)S(1)}, bf16[336,256]{1,0:T(8,128)(2,1)S(1)}, u32[]{:S(2)}, u32[]{:S(2)}) collective-permute-start(bf16[336,256]{1,0:T(8,128)(2,1)S(1)} %merge_pair.1.after.refs_0_), channel_id=1, source_target_pairs={{0,2},{1,3},{2,0},{3,1},{4,6},{5,7},{6,4},{7,5},{8,10},{9,11},{10,... | collective-permute-start | bytes 516104 | tf_op jit(solution)/shard_map/ppermute | solution.py:23
  44.3 9.0 %collective-permute-start.16 = (bf16[336,256]{1,0:T(8,128)(2,1)S(1)}, bf16[336,256]{1,0:T(8,128)(2,1)S(1)}, u32[]{:S(2)}, u32[]{:S(2)}) collective-permute-start(bf16[336,256]{1,0:T(8,128)(2,1)S(1)} %merge_pair.1.after.refs_0_), channel_id=1, source_target_pairs={{0,4},{1,5},{2,6},{3,7},{4,0},{5,1},{6,2},{7,3},{8,12},{9,13},{10,... | collective-permute-start | bytes 516104 | tf_op jit(solution)/shard_map/ppermute | solution.py:23
  45.8 7.5 %collective-permute-start.17 = (bf16[336,256]{1,0:T(8,128)(2,1)S(1)}, bf16[336,256]{1,0:T(8,128)(2,1)S(1)}, u32[]{:S(2)}, u32[]{:S(2)}) collective-permute-start(bf16[336,256]{1,0:T(8,128)(2,1)S(1)} %merge_pair.1.after.refs_0_), channel_id=1, source_target_pairs={{0,6},{1,7},{2,4},{3,5},{4,2},{5,3},{6,0},{7,1},{8,14},{9,15},{10,... | collective-permute-start | bytes 516104 | tf_op jit(solution)/shard_map/ppermute | solution.py:23
  55.9 4.2 %collective-permute-start.21 = (bf16[64,320]{1,0:T(8,128)(2,1)S(1)}, bf16[64,320]{1,0:T(8,128)(2,1)S(1)}, u32[]{:S(2)}, u32[]{:S(2)}) collective-permute-start(bf16[64,320]{1,0:T(8,128)(2,1)S(1)} %project_out.1.refs_0_), channel_id=1, source_target_pairs={{0,2},{1,3},{2,0},{3,1},{4,6},{5,7},{6,4},{7,5},{8,10},{9,11},{10,... | collective-permute-start | bytes 122888 | tf_op jit(solution)/shard_map/ppermute | solution.py:23
  56.6 4.1 %collective-permute-start.23 = (bf16[64,320]{1,0:T(8,128)(2,1)S(1)}, bf16[64,320]{1,0:T(8,128)(2,1)S(1)}, u32[]{:S(2)}, u32[]{:S(2)}) collective-permute-start(bf16[64,320]{1,0:T(8,128)(2,1)S(1)} %project_out.1.refs_0_), channel_id=1, source_target_pairs={{0,4},{1,5},{2,6},{3,7},{4,0},{5,1},{6,2},{7,3},{8,12},{9,13},{10,... | collective-permute-start | bytes 122888 | tf_op jit(solution)/shard_map/ppermute | solution.py:23
  58.0 5.0 %collective-permute-start.25 = (bf16[64,320]{1,0:T(8,128)(2,1)S(1)}, bf16[64,320]{1,0:T(8,128)(2,1)S(1)}, u32[]{:S(2)}, u32[]{:S(2)}) collective-permute-start(bf16[64,320]{1,0:T(8,128)(2,1)S(1)} %project_out.1.refs_0_), channel_id=1, source_target_pairs={{0,6},{1,7},{2,4},{3,5},{4,2},{5,3},{6,0},{7,1},{8,14},{9,15},{10,... | collective-permute-start | bytes 122888 | tf_op jit(solution)/shard_map/ppermute | solution.py:23
  59.4 3.6 %collective-permute-start.20 = (bf16[64,320]{1,0:T(8,128)(2,1)S(1)}, bf16[64,320]{1,0:T(8,128)(2,1)S(1)}, u32[]{:S(2)}, u32[]{:S(2)}) collective-permute-start(bf16[64,320]{1,0:T(8,128)(2,1)S(1)} %project_out.1.refs_0_), channel_id=1, source_target_pairs={{0,1},{1,0},{2,3},{3,2},{4,5},{5,4},{6,7},{7,6},{8,9},{9,8},{10,11... | collective-permute-start | bytes 122888 | tf_op jit(solution)/shard_map/ppermute | solution.py:23
  60.0 3.0 %collective-permute-start.22 = (bf16[64,320]{1,0:T(8,128)(2,1)S(1)}, bf16[64,320]{1,0:T(8,128)(2,1)S(1)}, u32[]{:S(2)}, u32[]{:S(2)}) collective-permute-start(bf16[64,320]{1,0:T(8,128)(2,1)S(1)} %collective-permute-done.21.refs_2_), channel_id=1, source_target_pairs={{0,1},{1,0},{2,3},{3,2},{4,5},{5,4},{6,7},{7,6},{8,9},{9,8},{10,11... | collective-permute-start | bytes 122888 | tf_op jit(solution)/shard_map/ppermute | solution.py:23
  60.7 2.3 %collective-permute-start.24 = (bf16[64,320]{1,0:T(8,128)(2,1)S(1)}, bf16[64,320]{1,0:T(8,128)(2,1)S(1)}, u32[]{:S(2)}, u32[]{:S(2)}) collective-permute-start(bf16[64,320]{1,0:T(8,128)(2,1)S(1)} %collective-permute-done.23.refs_4_), channel_id=1, source_target_pairs={{0,1},{1,0},{2,3},{3,2},{4,5},{5,4},{6,7},{7,6},{8,9},{9,8},{10,11... | collective-permute-start | bytes 122888 | tf_op jit(solution)/shard_map/ppermute | solution.py:23
  69.6 10.4 %collective-permute-start.28 = (bf16[32,2560]{1,0:T(8,128)(2,1)S(1)}, bf16[32,2560]{1,0:T(8,128)(2,1)S(1)}, u32[]{:S(2)}, u32[]{:S(2)}) collective-permute-start(bf16[32,2560]{1,0:T(8,128)(2,1)S(1)} %add_convert_fusion.1), channel_id=1, source_target_pairs={{0,2},{1,3},{2,0},{3,1},{4,6},{5,7},{6,4},{7,5},{8,10},{9,11},{10,... | collective-permute-start | bytes 491528 | tf_op jit(solution)/shard_map/ppermute | solution.py:23
  70.8 9.5 %collective-permute-start.29 = (bf16[32,2560]{1,0:T(8,128)(2,1)S(1)}, bf16[32,2560]{1,0:T(8,128)(2,1)S(1)}, u32[]{:S(2)}, u32[]{:S(2)}) collective-permute-start(bf16[32,2560]{1,0:T(8,128)(2,1)S(1)} %add_convert_fusion.1), channel_id=1, source_target_pairs={{0,4},{1,5},{2,6},{3,7},{4,0},{5,1},{6,2},{7,3},{8,12},{9,13},{10,... | collective-permute-start | bytes 491528 | tf_op jit(solution)/shard_map/ppermute | solution.py:23
  71.7 8.7 %collective-permute-start.30 = (bf16[32,2560]{1,0:T(8,128)(2,1)S(1)}, bf16[32,2560]{1,0:T(8,128)(2,1)S(1)}, u32[]{:S(2)}, u32[]{:S(2)}) collective-permute-start(bf16[32,2560]{1,0:T(8,128)(2,1)S(1)} %add_convert_fusion.1), channel_id=1, source_target_pairs={{0,6},{1,7},{2,4},{3,5},{4,2},{5,3},{6,0},{7,1},{8,14},{9,15},{10,... | collective-permute-start | bytes 491528 | tf_op jit(solution)/shard_map/ppermute | solution.py:23
  (14 other events, 55.9 us)

commit v8 on v7

--- a/solution.py
+++ b/solution.py
@@ -227,6 +227,12 @@
     )(*packs, token)
 
 
+def chunk_bounds(pages, chunk):
+    if pages < 2 * chunk:
+        return [0, pages]
+    return [0, *range(chunk // 2, pages - chunk // 2 + 1, chunk), pages]
+
+
 def attention_kernel(dims, count, slot_source, cosine, sine, *refs):
     requests, new_count, heads, pages, page_len, window, chunk, n_seq = dims
     pieces, refs = refs[:count], refs[count:]
@@ -237,11 +243,13 @@
     rows = new_count * heads
     lines = requests * new_count
 
+    bounds = chunk_bounds(pages, chunk)
+
     def load(c):
-        span = pl.ds(c * chunk, chunk)
+        span = pl.ds(bounds[c], bounds[c + 1] - bounds[c])
         return pltpu.make_async_copy(pool.at[span], buffer.at[span], in_sems.at[c])
 
-    for c in range(pages // chunk):
+    for c in range(len(bounds) - 1):
         load(c).start()
 
     me = lax.axis_index("seq")
@@ -317,15 +325,15 @@
 
     def chunk_scores(c):
         load(c).wait()
-        numbers = range(c * chunk, (c + 1) * chunk)
+        numbers = range(bounds[c], bounds[c + 1])
         return [score(slots[0, page], buffer[page, :, 0:256]) for page in numbers]
 
     ahead = chunk_scores(0)
-    for c in range(pages // chunk):
+    for c in range(len(bounds) - 1):
         scores = ahead
-        if (c + 1) * chunk < pages:
+        if c + 2 < len(bounds):
             ahead = chunk_scores(c + 1)
-        numbers = range(c * chunk, (c + 1) * chunk)
+        numbers = range(bounds[c], bounds[c + 1])
         weighed = []
         for page, values in zip(numbers, scores):
             length = slots[1, page]
@@ -383,7 +391,7 @@
             pltpu.VMEM((requests * rows, 256), f32),
             pltpu.SMEM(slots.shape, jnp.int32),
             pltpu.SemaphoreType.DMA,
-            pltpu.SemaphoreType.DMA((pages // chunk,)),
+            pltpu.SemaphoreType.DMA((len(chunk_bounds(pages, chunk)) - 1,)),
         ],
         compiler_params=pltpu.CompilerParams(vmem_limit_bytes=20 * 1024 * 1024),
         cost_estimate=pl.CostEstimate(flops=0, bytes_accessed=1024, transcendentals=0),

time: 82.9 us -> 82.9 us (level)
  no operation moved by 1% of the time
where the time goes in v8:
time: 82.9 us; the launch traced here: 82.7 us
  starting transfers between devices  27.8 us (34%)
  waiting for transfers between devices  24.9 us (30%)
  Pallas kernels  23.7 us (29%)
  local copies, waits for them, and re-layouts  2.85 us (3%)
  other arithmetic  1.47 us (2%)
  between operations  1.12 us (1%)
    ppermute x32, starting transfers between devices, swap(): return lax.ppermute(values, axis, [(i, i ^ mask) for i in range(size)])  27.8 us
    ppermute x32, waiting for transfers between devices, swap(): return lax.ppermute(values, axis, [(i, i ^ mask) for i in range(size)])  24.9 us
    pallas_call x1, Pallas kernels, write_pool(): pl.pallas_call(functools.partial(write_kernel, dims, parts), out_shape=pl...  6.64 us
    pallas_call x1, Pallas kernels, fetch_weights(): pl.pallas_call(functools.partial(fetch_kernel, parts), out_shape=(jax.Sha...  5.33 us
    pallas_call x1, Pallas kernels, attention(): pl.pallas_call(functools.partial(attention_kernel, dims, len(pieces)), ou...  5.15 us
    pallas_call x1, Pallas kernels, feed_forward(): pl.pallas_call(functools.partial(mlp_kernel, chunk, len(heads_out)), out_...  3.88 us
  transfers between devices with their start and end apart: 32, of which 22 were waited for; matrix products, arithmetic and copies ran while one was open for 4% of the time, Pallas kernels for 22%

profile of v8, /device:TPU:0, one launch (start us, length us, event | category | flops | bytes accessed | tf_op | source)
XLA Modules:
  0.0 82.7 jit_solution(8658163507680422817)
XLA Ops:
  1.6 4.1 %collective-permute-start = (bf16[4,4,2560]{2,1,0:T(4,128)(2,1)S(1)}, bf16[4,4,2560]{2,1,0:T(4,128)(2,1)S(1)}, u32[]{:S(2)}, u32[]{:S(2)}) collective-permute-start(bf16[4,4,2560]{2,1,0:T(4,128)(2,1)S(1)} %constant_dynamic-slice_fusion), channel_id=1, source_target_pairs={{0,16},{8,24},{16,0},{24,8},{1,17},{9,25},{17,1},{25,9},{2,18},{10... | collective-permute-start | bytes 245768 | tf_op jit(solution)/shard_map/ppermute | solution.py:23
  5.7 1.6 %collective-permute-start.3 = (bf16[96,2560]{1,0:T(8,128)(2,1)}, bf16[96,2560]{1,0:T(8,128)(2,1)S(1)}, u32[]{:S(2)}, u32[]{:S(2)}) collective-permute-start(bf16[96,2560]{1,0:T(8,128)(2,1)} %param.12), channel_id=1, source_target_pairs={{0,8},{8,0},{16,24},{24,16},{1,9},{9,1},{17,25},{25,17},{2,10},{10... | collective-permute-start | bytes 1474568 | tf_op jit(solution)/shard_map/ppermute | solution.py:23
  9.5 1.9 %collective-permute-start.1 = (bf16[4,4,2560]{2,1,0:T(4,128)(2,1)S(1)}, bf16[4,4,2560]{2,1,0:T(4,128)(2,1)S(1)}, u32[]{:S(2)}, u32[]{:S(2)}) collective-permute-start(bf16[4,4,2560]{2,1,0:T(4,128)(2,1)S(1)} %collective-permute-done), channel_id=1, source_target_pairs={{0,2},{1,3},{2,0},{3,1},{4,6},{5,7},{6,4},{7,5},{8,10},{9,11},{10,... | collective-permute-start | bytes 245768 | tf_op jit(solution)/shard_map/ppermute | solution.py:23
  12.2 1.7 %collective-permute-done.1 = bf16[4,4,2560]{2,1,0:T(4,128)(2,1)S(1)} collective-permute-done((bf16[4,4,2560]{2,1,0:T(4,128)(2,1)S(1)}, bf16[4,4,2560]{2,1,0:T(4,128)(2,1)S(1)}, u32[]{:S(2)}, u32[]{:S(2)}) %collective-permute-start.1) | collective-permute-done | bytes 81952 | tf_op jit(solution)/shard_map/ppermute | solution.py:23
  14.2 1.3 %collective-permute-done.2 = bf16[8,4,2560]{2,1,0:T(4,128)(2,1)S(1)} collective-permute-done((bf16[8,4,2560]{2,1,0:T(4,128)(2,1)S(1)}, bf16[8,4,2560]{2,1,0:T(4,128)(2,1)S(1)}, u32[]{:S(2)}, u32[]{:S(2)}) %collective-permute-start.2) | collective-permute-done | bytes 163872 | tf_op jit(solution)/shard_map/ppermute | solution.py:23
  16.4 2.8 %collective-permute-done.3 = bf16[96,2560]{1,0:T(8,128)(2,1)S(1)} collective-permute-done((bf16[96,2560]{1,0:T(8,128)(2,1)}, bf16[96,2560]{1,0:T(8,128)(2,1)S(1)}, u32[]{:S(2)}, u32[]{:S(2)}) %collective-permute-start.3) | collective-permute-done | bytes 491552 | tf_op jit(solution)/shard_map/ppermute | solution.py:23
  21.1 2.0 %collective-permute-start.13 = (bf16[80,2560]{1,0:T(8,128)(2,1)S(1)}, bf16[80,2560]{1,0:T(8,128)(2,1)S(1)}, u32[]{:S(2)}, u32[]{:S(2)}) collective-permute-start(bf16[80,2560]{1,0:T(8,128)(2,1)S(1)} %copy-done), channel_id=1, source_target_pairs={{0,8},{8,0},{16,24},{24,16},{1,9},{9,1},{17,25},{25,17},{2,10},{10... | collective-permute-start | bytes 1228808 | tf_op jit(solution)/shard_map/ppermute | solution.py:23
  23.1 1.3 %collective-permute-start.14 = (bf16[80,2560]{1,0:T(8,128)(2,1)S(1)}, bf16[80,2560]{1,0:T(8,128)(2,1)S(1)}, u32[]{:S(2)}, u32[]{:S(2)}) collective-permute-start(bf16[80,2560]{1,0:T(8,128)(2,1)S(1)} %copy-done), channel_id=1, source_target_pairs={{0,16},{8,24},{16,0},{24,8},{1,17},{9,25},{17,1},{25,9},{2,18},{10... | collective-permute-start | bytes 1228808 | tf_op jit(solution)/shard_map/ppermute | solution.py:23
  24.8 2.7 %collective-permute-start.10 = (bf16[64,384]{1,0:T(8,128)(2,1)S(1)}, bf16[64,384]{1,0:T(8,128)(2,1)S(1)}, u32[]{:S(2)}, u32[]{:S(2)}) collective-permute-start(bf16[64,384]{1,0:T(8,128)(2,1)S(1)} %pad_maximum_fusion.1.refs_0_), channel_id=1, source_target_pairs={{0,6},{1,7},{2,4},{3,5},{4,2},{5,3},{6,0},{7,1},{8,14},{9,15},{10,... | collective-permute-start | bytes 147464 | tf_op jit(solution)/shard_map/ppermute | solution.py:23
  28.5 1.3 %collective-permute-done.10.refs_6_ = bf16[64,384]{1,0:T(8,128)(2,1)S(1)} collective-permute-done((bf16[64,384]{1,0:T(8,128)(2,1)S(1)}, bf16[64,384]{1,0:T(8,128)(2,1)S(1)}, u32[]{:S(2)}, u32[]{:S(2)}) %collective-permute-start.10) | collective-permute-done | bytes 49184 | tf_op jit(solution)/shard_map/ppermute | solution.py:23
  30.2 1.6 %collective-permute-done.6.refs_2_ = bf16[64,384]{1,0:T(8,128)(2,1)S(1)} collective-permute-done((bf16[64,384]{1,0:T(8,128)(2,1)S(1)}, bf16[64,384]{1,0:T(8,128)(2,1)S(1)}, u32[]{:S(2)}, u32[]{:S(2)}) %collective-permute-start.6) | collective-permute-done | bytes 49184 | tf_op jit(solution)/shard_map/ppermute | solution.py:23
  33.7 5.1 %page_attention.1 = (bf16[336,256]{1,0:T(8,128)(2,1)S(1)}, bf16[336,256]{1,0:T(8,128)(2,1)S(1)}, bf16[64,512]{1,0:T(8,128)(2,1)S(1)}) custom-call(s32[3,64]{1,0:T(4,128)S(1)} %pad_add_fusion.slot_source, f32[64,128]{1,0:T(8,128)S(1)} %get-tuple-element.79.cosine, f32[64,128]{1,0:T(8,128)S(1)} %get-tuple-element.80.sine, ...), custom_call_target="tpu_custom_call" | custom-call | bytes 1024 | tf_op jit(solution)/shard_map/page_attention/pallas_call | solution.py:375
  40.7 2.1 %collective-permute-done.14.refs_2_ = bf16[80,2560]{1,0:T(8,128)(2,1)S(1)} collective-permute-done((bf16[80,2560]{1,0:T(8,128)(2,1)S(1)}, bf16[80,2560]{1,0:T(8,128)(2,1)S(1)}, u32[]{:S(2)}, u32[]{:S(2)}) %collective-permute-start.14) | collective-permute-done | bytes 409632 | tf_op jit(solution)/shard_map/ppermute | solution.py:23
  42.8 1.5 %collective-permute-start.15 = (bf16[336,256]{1,0:T(8,128)(2,1)S(1)}, bf16[336,256]{1,0:T(8,128)(2,1)S(1)}, u32[]{:S(2)}, u32[]{:S(2)}) collective-permute-start(bf16[336,256]{1,0:T(8,128)(2,1)S(1)} %merge_pair.1.after.refs_0_), channel_id=1, source_target_pairs={{0,2},{1,3},{2,0},{3,1},{4,6},{5,7},{6,4},{7,5},{8,10},{9,11},{10,... | collective-permute-start | bytes 516104 | tf_op jit(solution)/shard_map/ppermute | solution.py:23
  44.3 1.5 %collective-permute-start.16 = (bf16[336,256]{1,0:T(8,128)(2,1)S(1)}, bf16[336,256]{1,0:T(8,128)(2,1)S(1)}, u32[]{:S(2)}, u32[]{:S(2)}) collective-permute-start(bf16[336,256]{1,0:T(8,128)(2,1)S(1)} %merge_pair.1.after.refs_0_), channel_id=1, source_target_pairs={{0,4},{1,5},{2,6},{3,7},{4,0},{5,1},{6,2},{7,3},{8,12},{9,13},{10,... | collective-permute-start | bytes 516104 | tf_op jit(solution)/shard_map/ppermute | solution.py:23
  46.3 5.3 %fetch_weights.1 = (bf16[2,960,2560]{2,1,0:T(8,128)(2,1)S(1)}, bf16[960,2560]{1,0:T(8,128)(2,1)S(1)}, f32[8,128]{1,0:T(8,128)S(1)}) custom-call(bf16[2,960,2560]{2,1,0:T(8,128)(2,1)} %gate_up.1, bf16[960,2560]{1,0:T(8,128)(2,1)} %down.1, bf16[336,256]{1,0:T(8,128)(2,1)S(1)} %merge_pair.1.after.refs_0_), custom_call_target="tpu_custom_call" | custom-call | bytes 14745600 | tf_op jit(solution)/shard_map/fetch_weights/pallas_call | solution.py:465
  51.6 1.8 %collective-permute-done.16.refs_2_ = bf16[336,256]{1,0:T(8,128)(2,1)S(1)} collective-permute-done((bf16[336,256]{1,0:T(8,128)(2,1)S(1)}, bf16[336,256]{1,0:T(8,128)(2,1)S(1)}, u32[]{:S(2)}, u32[]{:S(2)}) %collective-permute-start.16) | collective-permute-done | bytes 172064 | tf_op jit(solution)/shard_map/ppermute | solution.py:23
  53.9 1.4 %collective-permute-done.19.other = bf16[32,2560]{1,0:T(8,128)(2,1)S(1)} collective-permute-done((bf16[32,2560]{1,0:T(8,128)(2,1)S(1)}, bf16[32,2560]{1,0:T(8,128)(2,1)S(1)}, u32[]{:S(2)}, u32[]{:S(2)}) %collective-permute-start.19) | collective-permute-done | bytes 163872 | tf_op jit(solution)/shard_map/ppermute | solution.py:23
  56.6 1.5 %collective-permute-start.23 = (bf16[64,320]{1,0:T(8,128)(2,1)S(1)}, bf16[64,320]{1,0:T(8,128)(2,1)S(1)}, u32[]{:S(2)}, u32[]{:S(2)}) collective-permute-start(bf16[64,320]{1,0:T(8,128)(2,1)S(1)} %project_out.1.refs_0_), channel_id=1, source_target_pairs={{0,4},{1,5},{2,6},{3,7},{4,0},{5,1},{6,2},{7,3},{8,12},{9,13},{10,... | collective-permute-start | bytes 122888 | tf_op jit(solution)/shard_map/ppermute | solution.py:23
  58.1 1.5 %collective-permute-start.25 = (bf16[64,320]{1,0:T(8,128)(2,1)S(1)}, bf16[64,320]{1,0:T(8,128)(2,1)S(1)}, u32[]{:S(2)}, u32[]{:S(2)}) collective-permute-start(bf16[64,320]{1,0:T(8,128)(2,1)S(1)} %project_out.1.refs_0_), channel_id=1, source_target_pairs={{0,6},{1,7},{2,4},{3,5},{4,2},{5,3},{6,0},{7,1},{8,14},{9,15},{10,... | collective-permute-start | bytes 122888 | tf_op jit(solution)/shard_map/ppermute | solution.py:23
  60.7 2.4 %collective-permute-done.25.refs_6_ = bf16[64,320]{1,0:T(8,128)(2,1)S(1)} collective-permute-done((bf16[64,320]{1,0:T(8,128)(2,1)S(1)}, bf16[64,320]{1,0:T(8,128)(2,1)S(1)}, u32[]{:S(2)}, u32[]{:S(2)}) %collective-permute-start.25) | collective-permute-done | bytes 40992 | tf_op jit(solution)/shard_map/ppermute | solution.py:23
  64.3 3.9 %feed_forward.1 = (f32[32,2560]{1,0:T(8,128)S(1)}, bf16[32,2560]{1,0:T(8,128)(2,1)S(1)}, bf16[32,2560]{1,0:T(8,128)(2,1)S(1)}) custom-call(bf16[64,2560]{1,0:T(8,128)(2,1)S(1)} %reshape.318.stream, f32[1,2560]{1,0:T(1,128)S(1)} %reshape.319.gain, bf16[2,960,2560]{2,1,0:T(8,128)(2,1)S(1)} %get-tuple-element.40.gates, ...), custom_call_target="tpu_custom_call" | custom-call | tf_op jit(solution)/shard_map/feed_forward/pallas_call | solution.py:538
  71.8 1.5 %collective-permute-start.30 = (bf16[32,2560]{1,0:T(8,128)(2,1)S(1)}, bf16[32,2560]{1,0:T(8,128)(2,1)S(1)}, u32[]{:S(2)}, u32[]{:S(2)}) collective-permute-start(bf16[32,2560]{1,0:T(8,128)(2,1)S(1)} %add_convert_fusion.1), channel_id=1, source_target_pairs={{0,6},{1,7},{2,4},{3,5},{4,2},{5,3},{6,0},{7,1},{8,14},{9,15},{10,... | collective-permute-start | bytes 491528 | tf_op jit(solution)/shard_map/ppermute | solution.py:23
  73.3 6.6 %write_pool.1 = bf16[64,128,512]{2,1,0:T(8,128)(2,1)} custom-call(s32[4,32]{1,0:T(4,128)S(1)} %pad_add_fusion.1.patch_source, bf16[64,512]{1,0:T(8,128)(2,1)S(1)} %get-tuple-element.54.fresh, bf16[64,128,512]{2,1,0:T(8,128)(2,1)} %source.1), custom_call_target="tpu_custom_call" | custom-call | bytes 16777216 | tf_op jit(solution)/shard_map/write_pool/pallas_call | solution.py:103
  (109 shorter events, 23.0 us)
Async XLA Ops:
  1.6 7.8 %collective-permute-start = (bf16[4,4,2560]{2,1,0:T(4,128)(2,1)S(1)}, bf16[4,4,2560]{2,1,0:T(4,128)(2,1)S(1)}, u32[]{:S(2)}, u32[]{:S(2)}) collective-permute-start(bf16[4,4,2560]{2,1,0:T(4,128)(2,1)S(1)} %constant_dynamic-slice_fusion), channel_id=1, source_target_pairs={{0,16},{8,24},{16,0},{24,8},{1,17},{9,25},{17,1},{25,9},{2,18},{10... | collective-permute-start | bytes 245768 | tf_op jit(solution)/shard_map/ppermute | solution.py:23
  5.7 13.5 %collective-permute-start.3 = (bf16[96,2560]{1,0:T(8,128)(2,1)}, bf16[96,2560]{1,0:T(8,128)(2,1)S(1)}, u32[]{:S(2)}, u32[]{:S(2)}) collective-permute-start(bf16[96,2560]{1,0:T(8,128)(2,1)} %param.12), channel_id=1, source_target_pairs={{0,8},{8,0},{16,24},{24,16},{1,9},{9,1},{17,25},{25,17},{2,10},{10... | collective-permute-start | bytes 1474568 | tf_op jit(solution)/shard_map/ppermute | solution.py:23
  9.5 4.5 %collective-permute-start.1 = (bf16[4,4,2560]{2,1,0:T(4,128)(2,1)S(1)}, bf16[4,4,2560]{2,1,0:T(4,128)(2,1)S(1)}, u32[]{:S(2)}, u32[]{:S(2)}) collective-permute-start(bf16[4,4,2560]{2,1,0:T(4,128)(2,1)S(1)} %collective-permute-done), channel_id=1, source_target_pairs={{0,2},{1,3},{2,0},{3,1},{4,6},{5,7},{6,4},{7,5},{8,10},{9,11},{10,... | collective-permute-start | bytes 245768 | tf_op jit(solution)/shard_map/ppermute | solution.py:23
  19.7 5.0 %collective-permute-start.4 = (bf16[64,192]{1,0:T(8,128)(2,1)S(1)}, bf16[64,192]{1,0:T(8,128)(2,1)S(1)}, u32[]{:S(2)}, u32[]{:S(2)}) collective-permute-start(bf16[64,192]{1,0:T(8,128)(2,1)S(1)} %slice.60), channel_id=1, source_target_pairs={{0,16},{8,24},{16,0},{24,8},{1,17},{9,25},{17,1},{25,9},{2,18},{10... | collective-permute-start | bytes 73736 | tf_op jit(solution)/shard_map/ppermute | solution.py:23
  21.1 19.6 %collective-permute-start.13 = (bf16[80,2560]{1,0:T(8,128)(2,1)S(1)}, bf16[80,2560]{1,0:T(8,128)(2,1)S(1)}, u32[]{:S(2)}, u32[]{:S(2)}) collective-permute-start(bf16[80,2560]{1,0:T(8,128)(2,1)S(1)} %copy-done), channel_id=1, source_target_pairs={{0,8},{8,0},{16,24},{24,16},{1,9},{9,1},{17,25},{25,17},{2,10},{10... | collective-permute-start | bytes 1228808 | tf_op jit(solution)/shard_map/ppermute | solution.py:23
  23.1 19.7 %collective-permute-start.14 = (bf16[80,2560]{1,0:T(8,128)(2,1)S(1)}, bf16[80,2560]{1,0:T(8,128)(2,1)S(1)}, u32[]{:S(2)}, u32[]{:S(2)}) collective-permute-start(bf16[80,2560]{1,0:T(8,128)(2,1)S(1)} %copy-done), channel_id=1, source_target_pairs={{0,16},{8,24},{16,0},{24,8},{1,17},{9,25},{17,1},{25,9},{2,18},{10... | collective-permute-start | bytes 1228808 | tf_op jit(solution)/shard_map/ppermute | solution.py:23
  24.8 5.0 %collective-permute-start.10 = (bf16[64,384]{1,0:T(8,128)(2,1)S(1)}, bf16[64,384]{1,0:T(8,128)(2,1)S(1)}, u32[]{:S(2)}, u32[]{:S(2)}) collective-permute-start(bf16[64,384]{1,0:T(8,128)(2,1)S(1)} %pad_maximum_fusion.1.refs_0_), channel_id=1, source_target_pairs={{0,6},{1,7},{2,4},{3,5},{4,2},{5,3},{6,0},{7,1},{8,14},{9,15},{10,... | collective-permute-start | bytes 147464 | tf_op jit(solution)/shard_map/ppermute | solution.py:23
  27.7 4.2 %collective-permute-start.6 = (bf16[64,384]{1,0:T(8,128)(2,1)S(1)}, bf16[64,384]{1,0:T(8,128)(2,1)S(1)}, u32[]{:S(2)}, u32[]{:S(2)}) collective-permute-start(bf16[64,384]{1,0:T(8,128)(2,1)S(1)} %pad_maximum_fusion.1.refs_0_), channel_id=1, source_target_pairs={{0,2},{1,3},{2,0},{3,1},{4,6},{5,7},{6,4},{7,5},{8,10},{9,11},{10,... | collective-permute-start | bytes 147464 | tf_op jit(solution)/shard_map/ppermute | solution.py:23
  28.3 4.1 %collective-permute-start.8 = (bf16[64,384]{1,0:T(8,128)(2,1)S(1)}, bf16[64,384]{1,0:T(8,128)(2,1)S(1)}, u32[]{:S(2)}, u32[]{:S(2)}) collective-permute-start(bf16[64,384]{1,0:T(8,128)(2,1)S(1)} %pad_maximum_fusion.1.refs_0_), channel_id=1, source_target_pairs={{0,4},{1,5},{2,6},{3,7},{4,0},{5,1},{6,2},{7,3},{8,12},{9,13},{10,... | collective-permute-start | bytes 147464 | tf_op jit(solution)/shard_map/ppermute | solution.py:23
  29.9 2.5 %collective-permute-start.5 = (bf16[64,384]{1,0:T(8,128)(2,1)S(1)}, bf16[64,384]{1,0:T(8,128)(2,1)S(1)}, u32[]{:S(2)}, u32[]{:S(2)}) collective-permute-start(bf16[64,384]{1,0:T(8,128)(2,1)S(1)} %pad_maximum_fusion.1.refs_0_), channel_id=1, source_target_pairs={{0,1},{1,0},{2,3},{3,2},{4,5},{5,4},{6,7},{7,6},{8,9},{9,8},{10,11... | collective-permute-start | bytes 147464 | tf_op jit(solution)/shard_map/ppermute | solution.py:23
  38.9 1.5 %collective-permute-start.12 = (bf16[336,256]{1,0:T(8,128)(2,1)S(1)}, bf16[336,256]{1,0:T(8,128)(2,1)S(1)}, u32[]{:S(2)}, u32[]{:S(2)}) collective-permute-start(bf16[336,256]{1,0:T(8,128)(2,1)S(1)} %get-tuple-element.37), channel_id=1, source_target_pairs={{0,1},{1,0},{2,3},{3,2},{4,5},{5,4},{6,7},{7,6},{8,9},{9,8},{10,11... | collective-permute-start | bytes 516104 | tf_op jit(solution)/shard_map/ppermute | solution.py:23
  42.8 10.7 %collective-permute-start.18 = (bf16[80,2560]{1,0:T(8,128)(2,1)S(1)}, bf16[80,2560]{1,0:T(8,128)(2,1)S(1)}, u32[]{:S(2)}, u32[]{:S(2)}) collective-permute-start(bf16[80,2560]{1,0:T(8,128)(2,1)S(1)} %collective-permute-done.14.refs_2_), channel_id=1, source_target_pairs={{0,8},{8,0},{16,24},{24,16},{1,9},{9,1},{17,25},{25,17},{2,10},{10... | collective-permute-start | bytes 1228808 | tf_op jit(solution)/shard_map/ppermute | solution.py:23
  42.8 8.8 %collective-permute-start.15 = (bf16[336,256]{1,0:T(8,128)(2,1)S(1)}, bf16[336,256]{1,0:T(8,128)(2,1)S(1)}, u32[]{:S(2)}, u32[]{:S(2)}) collective-permute-start(bf16[336,256]{1,0:T(8,128)(2,1)S(1)} %merge_pair.1.after.refs_0_), channel_id=1, source_target_pairs={{0,2},{1,3},{2,0},{3,1},{4,6},{5,7},{6,4},{7,5},{8,10},{9,11},{10,... | collective-permute-start | bytes 516104 | tf_op jit(solution)/shard_map/ppermute | solution.py:23
  44.3 9.2 %collective-permute-start.16 = (bf16[336,256]{1,0:T(8,128)(2,1)S(1)}, bf16[336,256]{1,0:T(8,128)(2,1)S(1)}, u32[]{:S(2)}, u32[]{:S(2)}) collective-permute-start(bf16[336,256]{1,0:T(8,128)(2,1)S(1)} %merge_pair.1.after.refs_0_), channel_id=1, source_target_pairs={{0,4},{1,5},{2,6},{3,7},{4,0},{5,1},{6,2},{7,3},{8,12},{9,13},{10,... | collective-permute-start | bytes 516104 | tf_op jit(solution)/shard_map/ppermute | solution.py:23
  45.8 7.6 %collective-permute-start.17 = (bf16[336,256]{1,0:T(8,128)(2,1)S(1)}, bf16[336,256]{1,0:T(8,128)(2,1)S(1)}, u32[]{:S(2)}, u32[]{:S(2)}) collective-permute-start(bf16[336,256]{1,0:T(8,128)(2,1)S(1)} %merge_pair.1.after.refs_0_), channel_id=1, source_target_pairs={{0,6},{1,7},{2,4},{3,5},{4,2},{5,3},{6,0},{7,1},{8,14},{9,15},{10,... | collective-permute-start | bytes 516104 | tf_op jit(solution)/shard_map/ppermute | solution.py:23
  56.0 4.2 %collective-permute-start.21 = (bf16[64,320]{1,0:T(8,128)(2,1)S(1)}, bf16[64,320]{1,0:T(8,128)(2,1)S(1)}, u32[]{:S(2)}, u32[]{:S(2)}) collective-permute-start(bf16[64,320]{1,0:T(8,128)(2,1)S(1)} %project_out.1.refs_0_), channel_id=1, source_target_pairs={{0,2},{1,3},{2,0},{3,1},{4,6},{5,7},{6,4},{7,5},{8,10},{9,11},{10,... | collective-permute-start | bytes 122888 | tf_op jit(solution)/shard_map/ppermute | solution.py:23
  56.6 4.1 %collective-permute-start.23 = (bf16[64,320]{1,0:T(8,128)(2,1)S(1)}, bf16[64,320]{1,0:T(8,128)(2,1)S(1)}, u32[]{:S(2)}, u32[]{:S(2)}) collective-permute-start(bf16[64,320]{1,0:T(8,128)(2,1)S(1)} %project_out.1.refs_0_), channel_id=1, source_target_pairs={{0,4},{1,5},{2,6},{3,7},{4,0},{5,1},{6,2},{7,3},{8,12},{9,13},{10,... | collective-permute-start | bytes 122888 | tf_op jit(solution)/shard_map/ppermute | solution.py:23
  58.1 5.0 %collective-permute-start.25 = (bf16[64,320]{1,0:T(8,128)(2,1)S(1)}, bf16[64,320]{1,0:T(8,128)(2,1)S(1)}, u32[]{:S(2)}, u32[]{:S(2)}) collective-permute-start(bf16[64,320]{1,0:T(8,128)(2,1)S(1)} %project_out.1.refs_0_), channel_id=1, source_target_pairs={{0,6},{1,7},{2,4},{3,5},{4,2},{5,3},{6,0},{7,1},{8,14},{9,15},{10,... | collective-permute-start | bytes 122888 | tf_op jit(solution)/shard_map/ppermute | solution.py:23
  59.6 3.5 %collective-permute-start.20 = (bf16[64,320]{1,0:T(8,128)(2,1)S(1)}, bf16[64,320]{1,0:T(8,128)(2,1)S(1)}, u32[]{:S(2)}, u32[]{:S(2)}) collective-permute-start(bf16[64,320]{1,0:T(8,128)(2,1)S(1)} %project_out.1.refs_0_), channel_id=1, source_target_pairs={{0,1},{1,0},{2,3},{3,2},{4,5},{5,4},{6,7},{7,6},{8,9},{9,8},{10,11... | collective-permute-start | bytes 122888 | tf_op jit(solution)/shard_map/ppermute | solution.py:23
  60.2 3.0 %collective-permute-start.22 = (bf16[64,320]{1,0:T(8,128)(2,1)S(1)}, bf16[64,320]{1,0:T(8,128)(2,1)S(1)}, u32[]{:S(2)}, u32[]{:S(2)}) collective-permute-start(bf16[64,320]{1,0:T(8,128)(2,1)S(1)} %collective-permute-done.21.refs_2_), channel_id=1, source_target_pairs={{0,1},{1,0},{2,3},{3,2},{4,5},{5,4},{6,7},{7,6},{8,9},{9,8},{10,11... | collective-permute-start | bytes 122888 | tf_op jit(solution)/shard_map/ppermute | solution.py:23
  60.7 2.4 %collective-permute-start.24 = (bf16[64,320]{1,0:T(8,128)(2,1)S(1)}, bf16[64,320]{1,0:T(8,128)(2,1)S(1)}, u32[]{:S(2)}, u32[]{:S(2)}) collective-permute-start(bf16[64,320]{1,0:T(8,128)(2,1)S(1)} %collective-permute-done.23.refs_4_), channel_id=1, source_target_pairs={{0,1},{1,0},{2,3},{3,2},{4,5},{5,4},{6,7},{7,6},{8,9},{9,8},{10,11... | collective-permute-start | bytes 122888 | tf_op jit(solution)/shard_map/ppermute | solution.py:23
  69.7 10.2 %collective-permute-start.28 = (bf16[32,2560]{1,0:T(8,128)(2,1)S(1)}, bf16[32,2560]{1,0:T(8,128)(2,1)S(1)}, u32[]{:S(2)}, u32[]{:S(2)}) collective-permute-start(bf16[32,2560]{1,0:T(8,128)(2,1)S(1)} %add_convert_fusion.1), channel_id=1, source_target_pairs={{0,2},{1,3},{2,0},{3,1},{4,6},{5,7},{6,4},{7,5},{8,10},{9,11},{10,... | collective-permute-start | bytes 491528 | tf_op jit(solution)/shard_map/ppermute | solution.py:23
  70.9 9.5 %collective-permute-start.29 = (bf16[32,2560]{1,0:T(8,128)(2,1)S(1)}, bf16[32,2560]{1,0:T(8,128)(2,1)S(1)}, u32[]{:S(2)}, u32[]{:S(2)}) collective-permute-start(bf16[32,2560]{1,0:T(8,128)(2,1)S(1)} %add_convert_fusion.1), channel_id=1, source_target_pairs={{0,4},{1,5},{2,6},{3,7},{4,0},{5,1},{6,2},{7,3},{8,12},{9,13},{10,... | collective-permute-start | bytes 491528 | tf_op jit(solution)/shard_map/ppermute | solution.py:23
  71.8 8.6 %collective-permute-start.30 = (bf16[32,2560]{1,0:T(8,128)(2,1)S(1)}, bf16[32,2560]{1,0:T(8,128)(2,1)S(1)}, u32[]{:S(2)}, u32[]{:S(2)}) collective-permute-start(bf16[32,2560]{1,0:T(8,128)(2,1)S(1)} %add_convert_fusion.1), channel_id=1, source_target_pairs={{0,6},{1,7},{2,4},{3,5},{4,2},{5,3},{6,0},{7,1},{8,14},{9,15},{10,... | collective-permute-start | bytes 491528 | tf_op jit(solution)/shard_map/ppermute | solution.py:23
  (14 other events, 55.9 us)

commit v9 on v8

--- a/solution.py
+++ b/solution.py
@@ -228,9 +228,12 @@
 
 
 def chunk_bounds(pages, chunk):
-    if pages < 2 * chunk:
-        return [0, pages]
-    return [0, *range(chunk // 2, pages - chunk // 2 + 1, chunk), pages]
+    if pages < 4 * chunk:
+        return [*range(0, pages, chunk), pages]
+    cut = chunk // 4
+    first, last = chunk - cut, pages - chunk + cut
+    count = pages // chunk - 2
+    return [0, *[first + (last - first) * i // count for i in range(count + 1)], pages]
 
 
 def attention_kernel(dims, count, slot_source, cosine, sine, *refs):

time: 82.9 us -> 83 us (level)
  no operation moved by 1% of the time
where the time goes in v9:
time: 83 us; the launch traced here: 82.8 us
  starting transfers between devices  27.7 us (33%)
  waiting for transfers between devices  24.7 us (30%)
  Pallas kernels  24.2 us (29%)
  local copies, waits for them, and re-layouts  2.85 us (3%)
  other arithmetic  1.47 us (2%)
  between operations  1.12 us (1%)
    ppermute x32, starting transfers between devices, swap(): return lax.ppermute(values, axis, [(i, i ^ mask) for i in range(size)])  27.7 us
    ppermute x32, waiting for transfers between devices, swap(): return lax.ppermute(values, axis, [(i, i ^ mask) for i in range(size)])  24.7 us
    pallas_call x1, Pallas kernels, write_pool(): pl.pallas_call(functools.partial(write_kernel, dims, parts), out_shape=pl...  6.95 us
    pallas_call x1, Pallas kernels, fetch_weights(): pl.pallas_call(functools.partial(fetch_kernel, parts), out_shape=(jax.Sha...  5.33 us
    pallas_call x1, Pallas kernels, attention(): pl.pallas_call(functools.partial(attention_kernel, dims, len(pieces)), ou...  5.29 us
    pallas_call x1, Pallas kernels, feed_forward(): pl.pallas_call(functools.partial(mlp_kernel, chunk, len(heads_out)), out_...  3.88 us
  transfers between devices with their start and end apart: 32, of which 22 were waited for; matrix products, arithmetic and copies ran while one was open for 4% of the time, Pallas kernels for 22%

profile of v9, /device:TPU:0, one launch (start us, length us, event | category | flops | bytes accessed | tf_op | source)
XLA Modules:
  0.0 82.8 jit_solution(18307242686418356454)
XLA Ops:
  1.6 4.1 %collective-permute-start = (bf16[4,4,2560]{2,1,0:T(4,128)(2,1)S(1)}, bf16[4,4,2560]{2,1,0:T(4,128)(2,1)S(1)}, u32[]{:S(2)}, u32[]{:S(2)}) collective-permute-start(bf16[4,4,2560]{2,1,0:T(4,128)(2,1)S(1)} %constant_dynamic-slice_fusion), channel_id=1, source_target_pairs={{0,16},{8,24},{16,0},{24,8},{1,17},{9,25},{17,1},{25,9},{2,18},{10... | collective-permute-start | bytes 245768 | tf_op jit(solution)/shard_map/ppermute | solution.py:23
  5.7 1.6 %collective-permute-start.3 = (bf16[96,2560]{1,0:T(8,128)(2,1)}, bf16[96,2560]{1,0:T(8,128)(2,1)S(1)}, u32[]{:S(2)}, u32[]{:S(2)}) collective-permute-start(bf16[96,2560]{1,0:T(8,128)(2,1)} %param.12), channel_id=1, source_target_pairs={{0,8},{8,0},{16,24},{24,16},{1,9},{9,1},{17,25},{25,17},{2,10},{10... | collective-permute-start | bytes 1474568 | tf_op jit(solution)/shard_map/ppermute | solution.py:23
  9.5 1.9 %collective-permute-start.1 = (bf16[4,4,2560]{2,1,0:T(4,128)(2,1)S(1)}, bf16[4,4,2560]{2,1,0:T(4,128)(2,1)S(1)}, u32[]{:S(2)}, u32[]{:S(2)}) collective-permute-start(bf16[4,4,2560]{2,1,0:T(4,128)(2,1)S(1)} %collective-permute-done), channel_id=1, source_target_pairs={{0,2},{1,3},{2,0},{3,1},{4,6},{5,7},{6,4},{7,5},{8,10},{9,11},{10,... | collective-permute-start | bytes 245768 | tf_op jit(solution)/shard_map/ppermute | solution.py:23
  12.2 1.7 %collective-permute-done.1 = bf16[4,4,2560]{2,1,0:T(4,128)(2,1)S(1)} collective-permute-done((bf16[4,4,2560]{2,1,0:T(4,128)(2,1)S(1)}, bf16[4,4,2560]{2,1,0:T(4,128)(2,1)S(1)}, u32[]{:S(2)}, u32[]{:S(2)}) %collective-permute-start.1) | collective-permute-done | bytes 81952 | tf_op jit(solution)/shard_map/ppermute | solution.py:23
  14.2 1.3 %collective-permute-done.2 = bf16[8,4,2560]{2,1,0:T(4,128)(2,1)S(1)} collective-permute-done((bf16[8,4,2560]{2,1,0:T(4,128)(2,1)S(1)}, bf16[8,4,2560]{2,1,0:T(4,128)(2,1)S(1)}, u32[]{:S(2)}, u32[]{:S(2)}) %collective-permute-start.2) | collective-permute-done | bytes 163872 | tf_op jit(solution)/shard_map/ppermute | solution.py:23
  16.4 2.8 %collective-permute-done.3 = bf16[96,2560]{1,0:T(8,128)(2,1)S(1)} collective-permute-done((bf16[96,2560]{1,0:T(8,128)(2,1)}, bf16[96,2560]{1,0:T(8,128)(2,1)S(1)}, u32[]{:S(2)}, u32[]{:S(2)}) %collective-permute-start.3) | collective-permute-done | bytes 491552 | tf_op jit(solution)/shard_map/ppermute | solution.py:23
  21.1 2.0 %collective-permute-start.13 = (bf16[80,2560]{1,0:T(8,128)(2,1)S(1)}, bf16[80,2560]{1,0:T(8,128)(2,1)S(1)}, u32[]{:S(2)}, u32[]{:S(2)}) collective-permute-start(bf16[80,2560]{1,0:T(8,128)(2,1)S(1)} %copy-done), channel_id=1, source_target_pairs={{0,8},{8,0},{16,24},{24,16},{1,9},{9,1},{17,25},{25,17},{2,10},{10... | collective-permute-start | bytes 1228808 | tf_op jit(solution)/shard_map/ppermute | solution.py:23
  23.1 1.3 %collective-permute-start.14 = (bf16[80,2560]{1,0:T(8,128)(2,1)S(1)}, bf16[80,2560]{1,0:T(8,128)(2,1)S(1)}, u32[]{:S(2)}, u32[]{:S(2)}) collective-permute-start(bf16[80,2560]{1,0:T(8,128)(2,1)S(1)} %copy-done), channel_id=1, source_target_pairs={{0,16},{8,24},{16,0},{24,8},{1,17},{9,25},{17,1},{25,9},{2,18},{10... | collective-permute-start | bytes 1228808 | tf_op jit(solution)/shard_map/ppermute | solution.py:23
  24.8 2.7 %collective-permute-start.10 = (bf16[64,384]{1,0:T(8,128)(2,1)S(1)}, bf16[64,384]{1,0:T(8,128)(2,1)S(1)}, u32[]{:S(2)}, u32[]{:S(2)}) collective-permute-start(bf16[64,384]{1,0:T(8,128)(2,1)S(1)} %pad_maximum_fusion.1.refs_0_), channel_id=1, source_target_pairs={{0,6},{1,7},{2,4},{3,5},{4,2},{5,3},{6,0},{7,1},{8,14},{9,15},{10,... | collective-permute-start | bytes 147464 | tf_op jit(solution)/shard_map/ppermute | solution.py:23
  28.5 1.3 %collective-permute-done.10.refs_6_ = bf16[64,384]{1,0:T(8,128)(2,1)S(1)} collective-permute-done((bf16[64,384]{1,0:T(8,128)(2,1)S(1)}, bf16[64,384]{1,0:T(8,128)(2,1)S(1)}, u32[]{:S(2)}, u32[]{:S(2)}) %collective-permute-start.10) | collective-permute-done | bytes 49184 | tf_op jit(solution)/shard_map/ppermute | solution.py:23
  30.2 1.6 %collective-permute-done.6.refs_2_ = bf16[64,384]{1,0:T(8,128)(2,1)S(1)} collective-permute-done((bf16[64,384]{1,0:T(8,128)(2,1)S(1)}, bf16[64,384]{1,0:T(8,128)(2,1)S(1)}, u32[]{:S(2)}, u32[]{:S(2)}) %collective-permute-start.6) | collective-permute-done | bytes 49184 | tf_op jit(solution)/shard_map/ppermute | solution.py:23
  33.7 5.3 %page_attention.1 = (bf16[336,256]{1,0:T(8,128)(2,1)S(1)}, bf16[336,256]{1,0:T(8,128)(2,1)S(1)}, bf16[64,512]{1,0:T(8,128)(2,1)S(1)}) custom-call(s32[3,64]{1,0:T(4,128)S(1)} %pad_add_fusion.slot_source, f32[64,128]{1,0:T(8,128)S(1)} %get-tuple-element.79.cosine, f32[64,128]{1,0:T(8,128)S(1)} %get-tuple-element.80.sine, ...), custom_call_target="tpu_custom_call" | custom-call | bytes 1024 | tf_op jit(solution)/shard_map/page_attention/pallas_call | solution.py:378
  40.8 2.0 %collective-permute-done.14.refs_2_ = bf16[80,2560]{1,0:T(8,128)(2,1)S(1)} collective-permute-done((bf16[80,2560]{1,0:T(8,128)(2,1)S(1)}, bf16[80,2560]{1,0:T(8,128)(2,1)S(1)}, u32[]{:S(2)}, u32[]{:S(2)}) %collective-permute-start.14) | collective-permute-done | bytes 409632 | tf_op jit(solution)/shard_map/ppermute | solution.py:23
  42.8 1.5 %collective-permute-start.15 = (bf16[336,256]{1,0:T(8,128)(2,1)S(1)}, bf16[336,256]{1,0:T(8,128)(2,1)S(1)}, u32[]{:S(2)}, u32[]{:S(2)}) collective-permute-start(bf16[336,256]{1,0:T(8,128)(2,1)S(1)} %merge_pair.1.after.refs_0_), channel_id=1, source_target_pairs={{0,2},{1,3},{2,0},{3,1},{4,6},{5,7},{6,4},{7,5},{8,10},{9,11},{10,... | collective-permute-start | bytes 516104 | tf_op jit(solution)/shard_map/ppermute | solution.py:23
  44.3 1.5 %collective-permute-start.16 = (bf16[336,256]{1,0:T(8,128)(2,1)S(1)}, bf16[336,256]{1,0:T(8,128)(2,1)S(1)}, u32[]{:S(2)}, u32[]{:S(2)}) collective-permute-start(bf16[336,256]{1,0:T(8,128)(2,1)S(1)} %merge_pair.1.after.refs_0_), channel_id=1, source_target_pairs={{0,4},{1,5},{2,6},{3,7},{4,0},{5,1},{6,2},{7,3},{8,12},{9,13},{10,... | collective-permute-start | bytes 516104 | tf_op jit(solution)/shard_map/ppermute | solution.py:23
  46.3 5.3 %fetch_weights.1 = (bf16[2,960,2560]{2,1,0:T(8,128)(2,1)S(1)}, bf16[960,2560]{1,0:T(8,128)(2,1)S(1)}, f32[8,128]{1,0:T(8,128)S(1)}) custom-call(bf16[2,960,2560]{2,1,0:T(8,128)(2,1)} %gate_up.1, bf16[960,2560]{1,0:T(8,128)(2,1)} %down.1, bf16[336,256]{1,0:T(8,128)(2,1)S(1)} %merge_pair.1.after.refs_0_), custom_call_target="tpu_custom_call" | custom-call | bytes 14745600 | tf_op jit(solution)/shard_map/fetch_weights/pallas_call | solution.py:468
  51.6 1.9 %collective-permute-done.16.refs_2_ = bf16[336,256]{1,0:T(8,128)(2,1)S(1)} collective-permute-done((bf16[336,256]{1,0:T(8,128)(2,1)S(1)}, bf16[336,256]{1,0:T(8,128)(2,1)S(1)}, u32[]{:S(2)}, u32[]{:S(2)}) %collective-permute-start.16) | collective-permute-done | bytes 172064 | tf_op jit(solution)/shard_map/ppermute | solution.py:23
  54.0 1.4 %collective-permute-done.19.other = bf16[32,2560]{1,0:T(8,128)(2,1)S(1)} collective-permute-done((bf16[32,2560]{1,0:T(8,128)(2,1)S(1)}, bf16[32,2560]{1,0:T(8,128)(2,1)S(1)}, u32[]{:S(2)}, u32[]{:S(2)}) %collective-permute-start.19) | collective-permute-done | bytes 163872 | tf_op jit(solution)/shard_map/ppermute | solution.py:23
  56.8 1.3 %collective-permute-start.23 = (bf16[64,320]{1,0:T(8,128)(2,1)S(1)}, bf16[64,320]{1,0:T(8,128)(2,1)S(1)}, u32[]{:S(2)}, u32[]{:S(2)}) collective-permute-start(bf16[64,320]{1,0:T(8,128)(2,1)S(1)} %project_out.1.refs_0_), channel_id=1, source_target_pairs={{0,4},{1,5},{2,6},{3,7},{4,0},{5,1},{6,2},{7,3},{8,12},{9,13},{10,... | collective-permute-start | bytes 122888 | tf_op jit(solution)/shard_map/ppermute | solution.py:23
  58.1 1.6 %collective-permute-start.25 = (bf16[64,320]{1,0:T(8,128)(2,1)S(1)}, bf16[64,320]{1,0:T(8,128)(2,1)S(1)}, u32[]{:S(2)}, u32[]{:S(2)}) collective-permute-start(bf16[64,320]{1,0:T(8,128)(2,1)S(1)} %project_out.1.refs_0_), channel_id=1, source_target_pairs={{0,6},{1,7},{2,4},{3,5},{4,2},{5,3},{6,0},{7,1},{8,14},{9,15},{10,... | collective-permute-start | bytes 122888 | tf_op jit(solution)/shard_map/ppermute | solution.py:23
  60.9 2.2 %collective-permute-done.25.refs_6_ = bf16[64,320]{1,0:T(8,128)(2,1)S(1)} collective-permute-done((bf16[64,320]{1,0:T(8,128)(2,1)S(1)}, bf16[64,320]{1,0:T(8,128)(2,1)S(1)}, u32[]{:S(2)}, u32[]{:S(2)}) %collective-permute-start.25) | collective-permute-done | bytes 40992 | tf_op jit(solution)/shard_map/ppermute | solution.py:23
  64.3 3.9 %feed_forward.1 = (f32[32,2560]{1,0:T(8,128)S(1)}, bf16[32,2560]{1,0:T(8,128)(2,1)S(1)}, bf16[32,2560]{1,0:T(8,128)(2,1)S(1)}) custom-call(bf16[64,2560]{1,0:T(8,128)(2,1)S(1)} %reshape.318.stream, f32[1,2560]{1,0:T(1,128)S(1)} %reshape.319.gain, bf16[2,960,2560]{2,1,0:T(8,128)(2,1)S(1)} %get-tuple-element.40.gates, ...), custom_call_target="tpu_custom_call" | custom-call | tf_op jit(solution)/shard_map/feed_forward/pallas_call | solution.py:541
  71.9 1.3 %collective-permute-start.30 = (bf16[32,2560]{1,0:T(8,128)(2,1)S(1)}, bf16[32,2560]{1,0:T(8,128)(2,1)S(1)}, u32[]{:S(2)}, u32[]{:S(2)}) collective-permute-start(bf16[32,2560]{1,0:T(8,128)(2,1)S(1)} %add_convert_fusion.1), channel_id=1, source_target_pairs={{0,6},{1,7},{2,4},{3,5},{4,2},{5,3},{6,0},{7,1},{8,14},{9,15},{10,... | collective-permute-start | bytes 491528 | tf_op jit(solution)/shard_map/ppermute | solution.py:23
  73.3 7.0 %write_pool.1 = bf16[64,128,512]{2,1,0:T(8,128)(2,1)} custom-call(s32[4,32]{1,0:T(4,128)S(1)} %pad_add_fusion.1.patch_source, bf16[64,512]{1,0:T(8,128)(2,1)S(1)} %get-tuple-element.54.fresh, bf16[64,128,512]{2,1,0:T(8,128)(2,1)} %source.1), custom_call_target="tpu_custom_call" | custom-call | bytes 16777216 | tf_op jit(solution)/shard_map/write_pool/pallas_call | solution.py:103
  (109 shorter events, 22.9 us)
Async XLA Ops:
  1.6 7.8 %collective-permute-start = (bf16[4,4,2560]{2,1,0:T(4,128)(2,1)S(1)}, bf16[4,4,2560]{2,1,0:T(4,128)(2,1)S(1)}, u32[]{:S(2)}, u32[]{:S(2)}) collective-permute-start(bf16[4,4,2560]{2,1,0:T(4,128)(2,1)S(1)} %constant_dynamic-slice_fusion), channel_id=1, source_target_pairs={{0,16},{8,24},{16,0},{24,8},{1,17},{9,25},{17,1},{25,9},{2,18},{10... | collective-permute-start | bytes 245768 | tf_op jit(solution)/shard_map/ppermute | solution.py:23
  5.7 13.5 %collective-permute-start.3 = (bf16[96,2560]{1,0:T(8,128)(2,1)}, bf16[96,2560]{1,0:T(8,128)(2,1)S(1)}, u32[]{:S(2)}, u32[]{:S(2)}) collective-permute-start(bf16[96,2560]{1,0:T(8,128)(2,1)} %param.12), channel_id=1, source_target_pairs={{0,8},{8,0},{16,24},{24,16},{1,9},{9,1},{17,25},{25,17},{2,10},{10... | collective-permute-start | bytes 1474568 | tf_op jit(solution)/shard_map/ppermute | solution.py:23
  9.5 4.5 %collective-permute-start.1 = (bf16[4,4,2560]{2,1,0:T(4,128)(2,1)S(1)}, bf16[4,4,2560]{2,1,0:T(4,128)(2,1)S(1)}, u32[]{:S(2)}, u32[]{:S(2)}) collective-permute-start(bf16[4,4,2560]{2,1,0:T(4,128)(2,1)S(1)} %collective-permute-done), channel_id=1, source_target_pairs={{0,2},{1,3},{2,0},{3,1},{4,6},{5,7},{6,4},{7,5},{8,10},{9,11},{10,... | collective-permute-start | bytes 245768 | tf_op jit(solution)/shard_map/ppermute | solution.py:23
  19.7 5.0 %collective-permute-start.4 = (bf16[64,192]{1,0:T(8,128)(2,1)S(1)}, bf16[64,192]{1,0:T(8,128)(2,1)S(1)}, u32[]{:S(2)}, u32[]{:S(2)}) collective-permute-start(bf16[64,192]{1,0:T(8,128)(2,1)S(1)} %slice.60), channel_id=1, source_target_pairs={{0,16},{8,24},{16,0},{24,8},{1,17},{9,25},{17,1},{25,9},{2,18},{10... | collective-permute-start | bytes 73736 | tf_op jit(solution)/shard_map/ppermute | solution.py:23
  21.1 19.7 %collective-permute-start.13 = (bf16[80,2560]{1,0:T(8,128)(2,1)S(1)}, bf16[80,2560]{1,0:T(8,128)(2,1)S(1)}, u32[]{:S(2)}, u32[]{:S(2)}) collective-permute-start(bf16[80,2560]{1,0:T(8,128)(2,1)S(1)} %copy-done), channel_id=1, source_target_pairs={{0,8},{8,0},{16,24},{24,16},{1,9},{9,1},{17,25},{25,17},{2,10},{10... | collective-permute-start | bytes 1228808 | tf_op jit(solution)/shard_map/ppermute | solution.py:23
  23.1 19.7 %collective-permute-start.14 = (bf16[80,2560]{1,0:T(8,128)(2,1)S(1)}, bf16[80,2560]{1,0:T(8,128)(2,1)S(1)}, u32[]{:S(2)}, u32[]{:S(2)}) collective-permute-start(bf16[80,2560]{1,0:T(8,128)(2,1)S(1)} %copy-done), channel_id=1, source_target_pairs={{0,16},{8,24},{16,0},{24,8},{1,17},{9,25},{17,1},{25,9},{2,18},{10... | collective-permute-start | bytes 1228808 | tf_op jit(solution)/shard_map/ppermute | solution.py:23
  24.8 5.0 %collective-permute-start.10 = (bf16[64,384]{1,0:T(8,128)(2,1)S(1)}, bf16[64,384]{1,0:T(8,128)(2,1)S(1)}, u32[]{:S(2)}, u32[]{:S(2)}) collective-permute-start(bf16[64,384]{1,0:T(8,128)(2,1)S(1)} %pad_maximum_fusion.1.refs_0_), channel_id=1, source_target_pairs={{0,6},{1,7},{2,4},{3,5},{4,2},{5,3},{6,0},{7,1},{8,14},{9,15},{10,... | collective-permute-start | bytes 147464 | tf_op jit(solution)/shard_map/ppermute | solution.py:23
  27.7 4.2 %collective-permute-start.6 = (bf16[64,384]{1,0:T(8,128)(2,1)S(1)}, bf16[64,384]{1,0:T(8,128)(2,1)S(1)}, u32[]{:S(2)}, u32[]{:S(2)}) collective-permute-start(bf16[64,384]{1,0:T(8,128)(2,1)S(1)} %pad_maximum_fusion.1.refs_0_), channel_id=1, source_target_pairs={{0,2},{1,3},{2,0},{3,1},{4,6},{5,7},{6,4},{7,5},{8,10},{9,11},{10,... | collective-permute-start | bytes 147464 | tf_op jit(solution)/shard_map/ppermute | solution.py:23
  28.3 4.1 %collective-permute-start.8 = (bf16[64,384]{1,0:T(8,128)(2,1)S(1)}, bf16[64,384]{1,0:T(8,128)(2,1)S(1)}, u32[]{:S(2)}, u32[]{:S(2)}) collective-permute-start(bf16[64,384]{1,0:T(8,128)(2,1)S(1)} %pad_maximum_fusion.1.refs_0_), channel_id=1, source_target_pairs={{0,4},{1,5},{2,6},{3,7},{4,0},{5,1},{6,2},{7,3},{8,12},{9,13},{10,... | collective-permute-start | bytes 147464 | tf_op jit(solution)/shard_map/ppermute | solution.py:23
  29.9 2.5 %collective-permute-start.5 = (bf16[64,384]{1,0:T(8,128)(2,1)S(1)}, bf16[64,384]{1,0:T(8,128)(2,1)S(1)}, u32[]{:S(2)}, u32[]{:S(2)}) collective-permute-start(bf16[64,384]{1,0:T(8,128)(2,1)S(1)} %pad_maximum_fusion.1.refs_0_), channel_id=1, source_target_pairs={{0,1},{1,0},{2,3},{3,2},{4,5},{5,4},{6,7},{7,6},{8,9},{9,8},{10,11... | collective-permute-start | bytes 147464 | tf_op jit(solution)/shard_map/ppermute | solution.py:23
  39.0 1.5 %collective-permute-start.12 = (bf16[336,256]{1,0:T(8,128)(2,1)S(1)}, bf16[336,256]{1,0:T(8,128)(2,1)S(1)}, u32[]{:S(2)}, u32[]{:S(2)}) collective-permute-start(bf16[336,256]{1,0:T(8,128)(2,1)S(1)} %get-tuple-element.37), channel_id=1, source_target_pairs={{0,1},{1,0},{2,3},{3,2},{4,5},{5,4},{6,7},{7,6},{8,9},{9,8},{10,11... | collective-permute-start | bytes 516104 | tf_op jit(solution)/shard_map/ppermute | solution.py:23
  42.8 10.8 %collective-permute-start.18 = (bf16[80,2560]{1,0:T(8,128)(2,1)S(1)}, bf16[80,2560]{1,0:T(8,128)(2,1)S(1)}, u32[]{:S(2)}, u32[]{:S(2)}) collective-permute-start(bf16[80,2560]{1,0:T(8,128)(2,1)S(1)} %collective-permute-done.14.refs_2_), channel_id=1, source_target_pairs={{0,8},{8,0},{16,24},{24,16},{1,9},{9,1},{17,25},{25,17},{2,10},{10... | collective-permute-start | bytes 1228808 | tf_op jit(solution)/shard_map/ppermute | solution.py:23
  42.8 8.8 %collective-permute-start.15 = (bf16[336,256]{1,0:T(8,128)(2,1)S(1)}, bf16[336,256]{1,0:T(8,128)(2,1)S(1)}, u32[]{:S(2)}, u32[]{:S(2)}) collective-permute-start(bf16[336,256]{1,0:T(8,128)(2,1)S(1)} %merge_pair.1.after.refs_0_), channel_id=1, source_target_pairs={{0,2},{1,3},{2,0},{3,1},{4,6},{5,7},{6,4},{7,5},{8,10},{9,11},{10,... | collective-permute-start | bytes 516104 | tf_op jit(solution)/shard_map/ppermute | solution.py:23
  44.3 9.3 %collective-permute-start.16 = (bf16[336,256]{1,0:T(8,128)(2,1)S(1)}, bf16[336,256]{1,0:T(8,128)(2,1)S(1)}, u32[]{:S(2)}, u32[]{:S(2)}) collective-permute-start(bf16[336,256]{1,0:T(8,128)(2,1)S(1)} %merge_pair.1.after.refs_0_), channel_id=1, source_target_pairs={{0,4},{1,5},{2,6},{3,7},{4,0},{5,1},{6,2},{7,3},{8,12},{9,13},{10,... | collective-permute-start | bytes 516104 | tf_op jit(solution)/shard_map/ppermute | solution.py:23
  45.8 7.7 %collective-permute-start.17 = (bf16[336,256]{1,0:T(8,128)(2,1)S(1)}, bf16[336,256]{1,0:T(8,128)(2,1)S(1)}, u32[]{:S(2)}, u32[]{:S(2)}) collective-permute-start(bf16[336,256]{1,0:T(8,128)(2,1)S(1)} %merge_pair.1.after.refs_0_), channel_id=1, source_target_pairs={{0,6},{1,7},{2,4},{3,5},{4,2},{5,3},{6,0},{7,1},{8,14},{9,15},{10,... | collective-permute-start | bytes 516104 | tf_op jit(solution)/shard_map/ppermute | solution.py:23
  56.1 4.2 %collective-permute-start.21 = (bf16[64,320]{1,0:T(8,128)(2,1)S(1)}, bf16[64,320]{1,0:T(8,128)(2,1)S(1)}, u32[]{:S(2)}, u32[]{:S(2)}) collective-permute-start(bf16[64,320]{1,0:T(8,128)(2,1)S(1)} %project_out.1.refs_0_), channel_id=1, source_target_pairs={{0,2},{1,3},{2,0},{3,1},{4,6},{5,7},{6,4},{7,5},{8,10},{9,11},{10,... | collective-permute-start | bytes 122888 | tf_op jit(solution)/shard_map/ppermute | solution.py:23
  56.8 4.1 %collective-permute-start.23 = (bf16[64,320]{1,0:T(8,128)(2,1)S(1)}, bf16[64,320]{1,0:T(8,128)(2,1)S(1)}, u32[]{:S(2)}, u32[]{:S(2)}) collective-permute-start(bf16[64,320]{1,0:T(8,128)(2,1)S(1)} %project_out.1.refs_0_), channel_id=1, source_target_pairs={{0,4},{1,5},{2,6},{3,7},{4,0},{5,1},{6,2},{7,3},{8,12},{9,13},{10,... | collective-permute-start | bytes 122888 | tf_op jit(solution)/shard_map/ppermute | solution.py:23
  58.1 5.0 %collective-permute-start.25 = (bf16[64,320]{1,0:T(8,128)(2,1)S(1)}, bf16[64,320]{1,0:T(8,128)(2,1)S(1)}, u32[]{:S(2)}, u32[]{:S(2)}) collective-permute-start(bf16[64,320]{1,0:T(8,128)(2,1)S(1)} %project_out.1.refs_0_), channel_id=1, source_target_pairs={{0,6},{1,7},{2,4},{3,5},{4,2},{5,3},{6,0},{7,1},{8,14},{9,15},{10,... | collective-permute-start | bytes 122888 | tf_op jit(solution)/shard_map/ppermute | solution.py:23
  59.7 3.4 %collective-permute-start.20 = (bf16[64,320]{1,0:T(8,128)(2,1)S(1)}, bf16[64,320]{1,0:T(8,128)(2,1)S(1)}, u32[]{:S(2)}, u32[]{:S(2)}) collective-permute-start(bf16[64,320]{1,0:T(8,128)(2,1)S(1)} %project_out.1.refs_0_), channel_id=1, source_target_pairs={{0,1},{1,0},{2,3},{3,2},{4,5},{5,4},{6,7},{7,6},{8,9},{9,8},{10,11... | collective-permute-start | bytes 122888 | tf_op jit(solution)/shard_map/ppermute | solution.py:23
  60.3 2.8 %collective-permute-start.22 = (bf16[64,320]{1,0:T(8,128)(2,1)S(1)}, bf16[64,320]{1,0:T(8,128)(2,1)S(1)}, u32[]{:S(2)}, u32[]{:S(2)}) collective-permute-start(bf16[64,320]{1,0:T(8,128)(2,1)S(1)} %collective-permute-done.21.refs_2_), channel_id=1, source_target_pairs={{0,1},{1,0},{2,3},{3,2},{4,5},{5,4},{6,7},{7,6},{8,9},{9,8},{10,11... | collective-permute-start | bytes 122888 | tf_op jit(solution)/shard_map/ppermute | solution.py:23
  60.9 2.3 %collective-permute-start.24 = (bf16[64,320]{1,0:T(8,128)(2,1)S(1)}, bf16[64,320]{1,0:T(8,128)(2,1)S(1)}, u32[]{:S(2)}, u32[]{:S(2)}) collective-permute-start(bf16[64,320]{1,0:T(8,128)(2,1)S(1)} %collective-permute-done.23.refs_4_), channel_id=1, source_target_pairs={{0,1},{1,0},{2,3},{3,2},{4,5},{5,4},{6,7},{7,6},{8,9},{9,8},{10,11... | collective-permute-start | bytes 122888 | tf_op jit(solution)/shard_map/ppermute | solution.py:23
  69.7 10.5 %collective-permute-start.28 = (bf16[32,2560]{1,0:T(8,128)(2,1)S(1)}, bf16[32,2560]{1,0:T(8,128)(2,1)S(1)}, u32[]{:S(2)}, u32[]{:S(2)}) collective-permute-start(bf16[32,2560]{1,0:T(8,128)(2,1)S(1)} %add_convert_fusion.1), channel_id=1, source_target_pairs={{0,2},{1,3},{2,0},{3,1},{4,6},{5,7},{6,4},{7,5},{8,10},{9,11},{10,... | collective-permute-start | bytes 491528 | tf_op jit(solution)/shard_map/ppermute | solution.py:23
  71.0 9.5 %collective-permute-start.29 = (bf16[32,2560]{1,0:T(8,128)(2,1)S(1)}, bf16[32,2560]{1,0:T(8,128)(2,1)S(1)}, u32[]{:S(2)}, u32[]{:S(2)}) collective-permute-start(bf16[32,2560]{1,0:T(8,128)(2,1)S(1)} %add_convert_fusion.1), channel_id=1, source_target_pairs={{0,4},{1,5},{2,6},{3,7},{4,0},{5,1},{6,2},{7,3},{8,12},{9,13},{10,... | collective-permute-start | bytes 491528 | tf_op jit(solution)/shard_map/ppermute | solution.py:23
  71.9 8.6 %collective-permute-start.30 = (bf16[32,2560]{1,0:T(8,128)(2,1)S(1)}, bf16[32,2560]{1,0:T(8,128)(2,1)S(1)}, u32[]{:S(2)}, u32[]{:S(2)}) collective-permute-start(bf16[32,2560]{1,0:T(8,128)(2,1)S(1)} %add_convert_fusion.1), channel_id=1, source_target_pairs={{0,6},{1,7},{2,4},{3,5},{4,2},{5,3},{6,0},{7,1},{8,14},{9,15},{10,... | collective-permute-start | bytes 491528 | tf_op jit(solution)/shard_map/ppermute | solution.py:23
  (14 other events, 55.8 us)
